TPU v7x, 32 devices: a whole 2x2x4 slice. The times are simulated.
32 devices in a mesh: dp: 8 (over z, x), seq: 4 (over y, core).
Axes of the slice: x: 2, y: 2, z: 4, core: 2. Of those that a mesh axis runs over, the one named last changes fastest.
Arguments:
- tokens: bfloat16 [8, 4096, 768], P('dp', 'seq'), may hold values from -6 to 6
- cotangent: bfloat16 [8, 4096, 768], P('dp', 'seq'), may hold values from -6 to 6
- in_weight: float32 [768, 3352], P('dp'), may hold values from -0.21875 to 0.21875
- in_moment: float32 [768, 3352], P('dp'), may hold values from -32 to 32
- in_second: float32 [768, 3352], P('dp'), may hold values from 2.94912 to 11.79648
- out_weight: float32 [1536, 768], P('dp'), may hold values from -0.15625 to 0.15625
- out_moment: float32 [1536, 768], P('dp'), may hold values from -128 to 128
- out_second: float32 [1536, 768], P('dp'), may hold values from 32.768 to 131.072
- channels: float32 [11336], replicated, as said below
- channel_moment: float32 [11336], replicated, as said below
- channel_second: float32 [11336], replicated, as said below
Outputs:
- block_out: float32 [8, 4096, 768], P('dp', 'seq')
- token_grad: float32 [8, 4096, 768], P('dp', 'seq')
- in_weight_new: float32 [768, 3352], P('dp')
- in_moment_new: float32 [768, 3352], P('dp')
- in_second_new: float32 [768, 3352], P('dp')
- out_weight_new: float32 [1536, 768], P('dp')
- out_moment_new: float32 [1536, 768], P('dp')
- out_second_new: float32 [1536, 768], P('dp')
- channels_new: float32 [11336], replicated
- channel_moment_new: float32 [11336], replicated
- channel_second_new: float32 [11336], replicated
Inputs may be any that keep to these rules, and one draw needn't show every extreme that they name: channels holds in order pre_gain (768), norm_gain (1536), conv_weight (1792 x 4, row by row), conv_bias (1792), step_bias, rate_log, skip_gain (24 each). `channel_moment`: laid out like channels. `channel_second`: laid out like channels, every entry positive.
All inputs are finite; a program needn't handle non-finite values.
Results may differ from a plain program's by a relative error of at most 0.012.
The roundings to bfloat16 on the way count: a program that leaves them out, or rounds other values in their place, can miss the bound.
Values may be sent and summed in bfloat16 or wider, within the bound.
No kernel may reach another device: no remote copies, remote signals or barrier semaphores. Data moves between devices by JAX's collectives and lax.ppermute only.
A program may use at most 192 MiB of HBM per device.

v0:
```python
import jax
import jax.numpy as jnp
from jax import lax
from jax.sharding import PartitionSpec as P

D = 768
HEADS = 24
HEADDIM = 64
STATE = 128
CONV = 4
STRETCH = 256
STEP = 10
INNER = 1536
XBC = 1792


highest = lax.Precision.HIGHEST
norm_eps = 1e-05
beta_one = 0.9
beta_two = 0.999
adam_eps = 1e-08
rate_matrix = 0.1
rate_channel = 0.5
decay_matrix = 0.1


def unpack_channels(channels):
    pieces = []
    offset = 0
    for piece_len in (D, INNER, XBC * CONV, XBC, HEADS, HEADS, HEADS):
        pieces.append(channels[offset : offset + piece_len])
        offset = offset + piece_len
    pre_gain, norm_gain, conv_flat, conv_bias, step_bias, rate_log, skip_gain = pieces
    return (
        pre_gain,
        norm_gain,
        conv_flat.reshape(XBC, CONV),
        conv_bias,
        step_bias,
        rate_log,
        skip_gain,
    )


def pre_norm(tok_vals, pre_gain):
    return (
        tok_vals * lax.rsqrt(jnp.mean(tok_vals * tok_vals, -1, keepdims=True) + norm_eps) * pre_gain
    )


def conv_apply(padded, length, weights, bias_row):
    summed = jnp.zeros((length, padded.shape[1]), jnp.float32) + bias_row[None, :]
    for offset in range(CONV):
        summed = summed + padded[offset : offset + length] * weights[:, offset][None, :]
    return jax.nn.silu(summed)


def causal_conv(values, weights, bias_row):
    padded = jnp.concatenate([jnp.zeros((CONV - 1, values.shape[1]), jnp.float32), values], axis=0)
    return conv_apply(padded, values.shape[0], weights, bias_row)


def state_space(inputs, steps, rates, write_keys, read_keys):
    seq_len = inputs.shape[0]
    head_count = inputs.shape[1]
    block_len = min(STRETCH, seq_len)
    blocks = seq_len // block_len
    lower_mask = jnp.arange(block_len)[:, None] >= jnp.arange(block_len)[None, :]

    def block_step(carry_state, block_data):
        block_inputs, block_steps, block_write, block_read = block_data
        log_decay = -block_steps * rates[None, :]
        cumul = jnp.cumsum(log_decay, axis=0)
        cumul_heads = cumul.T
        gaps_log = cumul_heads[:, :, None] - cumul_heads[:, None, :]
        decays = jnp.exp(jnp.where(lower_mask[None, :, :], gaps_log, -1e30))
        scores = jnp.dot(block_read, block_write.T, precision=highest)
        scaled = block_inputs * block_steps[:, :, None]
        within = jnp.einsum("hij,jhp->ihp", decays * scores[None, :, :], scaled, precision=highest)
        carried = (
            jnp.einsum("in,hpn->ihp", block_read, carry_state, precision=highest)
            * jnp.exp(cumul)[:, :, None]
        )
        tail_decay = jnp.exp(cumul[-1][None, :] - cumul)
        state_next = carry_state * jnp.exp(cumul[-1])[:, None, None] + jnp.einsum(
            "jhp,jn->hpn", scaled * tail_decay[:, :, None], block_write, precision=highest
        )
        return (state_next, within + carried)

    state_zero = jnp.zeros((head_count, HEADDIM, STATE), jnp.float32)
    packed = (
        inputs.reshape(blocks, block_len, head_count, HEADDIM),
        steps.reshape(blocks, block_len, head_count),
        write_keys.reshape(blocks, block_len, STATE),
        read_keys.reshape(blocks, block_len, STATE),
    )
    last_state, outputs = lax.scan(jax.checkpoint(block_step), state_zero, packed)
    return (outputs.reshape(seq_len, head_count, HEADDIM), last_state)


def mixer_heads(conv_vals, step_raw, step_bias, rate_log, skip_gain):
    head_count = step_raw.shape[1]
    head_width = head_count * HEADDIM
    inputs = conv_vals[:, :head_width].reshape(-1, head_count, HEADDIM)
    write_keys = conv_vals[:, head_width : head_width + STATE]
    read_keys = conv_vals[:, head_width + STATE :]
    steps = jax.nn.softplus(step_raw + step_bias[None, :])
    outputs, last_state = state_space(inputs, steps, jnp.exp(rate_log), write_keys, read_keys)
    mixed = outputs + skip_gain[None, :, None] * inputs
    return mixed.reshape(-1, head_width)


def gate_norm(mixed, gate_vals, norm_gain):
    gated = mixed * jax.nn.silu(gate_vals)
    return gated * lax.rsqrt(jnp.mean(gated * gated, -1, keepdims=True) + norm_eps) * norm_gain


def adamw_step(weight, moment, second, gradient, step_rate, decay_rate):
    moment_next = beta_one * moment + (1.0 - beta_one) * gradient
    second_next = beta_two * second + (1.0 - beta_two) * gradient * gradient
    first_fix = 1.0 - beta_one**STEP
    second_fix = 1.0 - beta_two**STEP
    update = moment_next / first_fix / (jnp.sqrt(second_next / second_fix) + adam_eps)
    return (weight - step_rate * (update + decay_rate * weight), moment_next, second_next)


def local(
    tokens,
    cotangent,
    in_weight,
    in_moment,
    in_second,
    out_weight,
    out_moment,
    out_second,
    channels,
    channel_moment,
    channel_second,
):
    groups = lax.axis_size("seq")
    seq_rank = lax.axis_index("seq")
    local_heads = HEADS // groups
    local_width = local_heads * HEADDIM
    pre_gain, norm_gain, conv_weight, conv_bias, step_bias, rate_log, skip_gain = unpack_channels(
        channels
    )
    tok_vals = tokens[0].astype(jnp.float32)
    tok_count = tok_vals.shape[0]
    seq_len = tok_count * groups
    contract = (((1,), (1,)), ((), ()))
    grad_pair = (((0,), (0,)), ((), ()))
    normed, norm_pull = jax.vjp(pre_norm, tok_vals, pre_gain)
    normed_low = normed.astype(jnp.bfloat16)
    in_low = in_weight.astype(jnp.bfloat16)
    out_low = out_weight.astype(jnp.bfloat16)
    full_in, full_out = (
        lax.all_gather(in_low, "dp", axis=0, tiled=True),
        lax.all_gather(out_low, "dp", axis=0, tiled=True),
    )
    projected = jnp.dot(normed_low, full_in, preferred_element_type=jnp.float32)
    proj_low = projected.astype(jnp.bfloat16)
    gate_vals = proj_low[:, :INNER].astype(jnp.float32)
    conv_src = proj_low[:, INNER : INNER + XBC]
    step_low = proj_low[:, INNER + XBC :]
    head_send = conv_src[:, :INNER].reshape(tok_count, groups, local_width)
    shared_send = jnp.broadcast_to(conv_src[:, None, INNER:], (tok_count, groups, 2 * STATE))
    step_send = step_low.reshape(tok_count, groups, local_heads)
    head_got, shared_got, step_got = (
        lax.all_to_all(head_send, "seq", split_axis=1, concat_axis=0, tiled=True),
        lax.all_to_all(shared_send, "seq", split_axis=1, concat_axis=0, tiled=True),
        lax.all_to_all(step_send, "seq", split_axis=1, concat_axis=0, tiled=True),
    )
    conv_in = jnp.concatenate([head_got[:, 0], shared_got[:, 0]], axis=1).astype(jnp.float32)
    step_raw = step_got[:, 0].astype(jnp.float32)
    head_first = seq_rank * local_width
    head_start = seq_rank * local_heads
    conv_local = jnp.concatenate(
        [lax.dynamic_slice_in_dim(conv_weight, head_first, local_width, 0), conv_weight[INNER:]],
        axis=0,
    )
    bias_local = jnp.concatenate(
        [lax.dynamic_slice_in_dim(conv_bias, head_first, local_width, 0), conv_bias[INNER:]], axis=0
    )
    step_local = lax.dynamic_slice_in_dim(step_bias, head_start, local_heads, 0)
    rate_local = lax.dynamic_slice_in_dim(rate_log, head_start, local_heads, 0)
    skip_local = lax.dynamic_slice_in_dim(skip_gain, head_start, local_heads, 0)
    conv_out, conv_pull = jax.vjp(causal_conv, conv_in, conv_local, bias_local)
    conv_vals = lax.optimization_barrier(conv_out.astype(jnp.bfloat16)).astype(jnp.float32)
    mixed, mixer_pull = jax.vjp(
        mixer_heads, conv_vals, step_raw, step_local, rate_local, skip_local
    )
    mixed_low = mixed.astype(jnp.bfloat16).reshape(seq_len, 1, local_width)
    mixed_tok = lax.all_to_all(mixed_low, "seq", split_axis=0, concat_axis=1, tiled=True).reshape(
        tok_count, INNER
    )
    mixed_tok = mixed_tok.astype(jnp.float32)
    hidden, gate_pull = jax.vjp(gate_norm, mixed_tok, gate_vals, norm_gain)
    hidden_low = hidden.astype(jnp.bfloat16)
    branch = jnp.dot(hidden_low, full_out, preferred_element_type=jnp.float32)
    block_out = (tok_vals + branch)[None]
    cot_low = cotangent[0]
    hidden_grad = lax.dot_general(cot_low, full_out, contract, preferred_element_type=jnp.float32)
    mixed_grad, gate_grad, norm_gain_grad = gate_pull(hidden_grad)
    head_grad = lax.all_to_all(
        mixed_grad.reshape(tok_count, groups, local_width),
        "seq",
        split_axis=1,
        concat_axis=0,
        tiled=True,
    )
    conv_grad, step_grad, step_local_grad, rate_local_grad, skip_local_grad = mixer_pull(
        head_grad[:, 0]
    )
    source_grad, conv_local_grad, bias_local_grad = conv_pull(conv_grad)
    back_head, back_shared, back_step = (
        lax.all_to_all(
            source_grad[:, :local_width].reshape(seq_len, 1, local_width),
            "seq",
            split_axis=0,
            concat_axis=1,
            tiled=True,
        ),
        lax.all_to_all(
            source_grad[:, local_width:].reshape(seq_len, 1, 2 * STATE),
            "seq",
            split_axis=0,
            concat_axis=1,
            tiled=True,
        ),
        lax.all_to_all(
            step_grad.reshape(seq_len, 1, local_heads),
            "seq",
            split_axis=0,
            concat_axis=1,
            tiled=True,
        ),
    )
    source_all = jnp.concatenate(
        [back_head.reshape(tok_count, INNER), jnp.sum(back_shared, axis=1)], axis=1
    )
    step_all = back_step.reshape(tok_count, HEADS)
    conv_w_grad = jnp.concatenate(
        [
            lax.dynamic_update_slice_in_dim(
                jnp.zeros((INNER, CONV), jnp.float32), conv_local_grad[:local_width], head_first, 0
            ),
            conv_local_grad[local_width:],
        ],
        axis=0,
    )
    conv_b_grad = jnp.concatenate(
        [
            lax.dynamic_update_slice_in_dim(
                jnp.zeros((INNER,), jnp.float32), bias_local_grad[:local_width], head_first, 0
            ),
            bias_local_grad[local_width:],
        ],
        axis=0,
    )

    def spread_heads(values):
        return lax.dynamic_update_slice_in_dim(
            jnp.zeros((HEADS,), jnp.float32), values, head_start, 0
        )

    step_bias_grad = spread_heads(step_local_grad)
    rate_log_grad = spread_heads(rate_local_grad)
    skip_gain_grad = spread_heads(skip_local_grad)
    proj_grad = jnp.concatenate([gate_grad, source_all, step_all], axis=1).astype(jnp.bfloat16)
    columns = normed_low
    in_grad = lax.psum_scatter(
        lax.dot_general(columns, proj_grad, grad_pair, preferred_element_type=jnp.float32),
        "dp",
        scatter_dimension=0,
        tiled=True,
    )
    columns = hidden_low
    out_grad = lax.psum_scatter(
        lax.dot_general(columns, cot_low, grad_pair, preferred_element_type=jnp.float32),
        "dp",
        scatter_dimension=0,
        tiled=True,
    )
    in_grad, out_grad = lax.psum((in_grad, out_grad), "seq")
    normed_grad = lax.dot_general(proj_grad, full_in, contract, preferred_element_type=jnp.float32)
    tok_norm_grad, pre_gain_grad = norm_pull(normed_grad)
    token_grad = (cot_low.astype(jnp.float32) + tok_norm_grad)[None]
    chan_grad = jnp.concatenate(
        [
            pre_gain_grad,
            norm_gain_grad,
            conv_w_grad.reshape(-1),
            conv_b_grad,
            step_bias_grad,
            rate_log_grad,
            skip_gain_grad,
        ]
    )
    chan_grad = lax.psum(chan_grad, ("dp", "seq"))
    in_new, in_mom, in_sec = adamw_step(
        in_weight, in_moment, in_second, in_grad, rate_matrix, decay_matrix
    )
    out_new, out_mom, out_sec = adamw_step(
        out_weight, out_moment, out_second, out_grad, rate_matrix, decay_matrix
    )
    chan_new, chan_mom, chan_sec = adamw_step(
        channels, channel_moment, channel_second, chan_grad, rate_channel, 0.0
    )
    return (
        block_out,
        token_grad,
        in_new,
        in_mom,
        in_sec,
        out_new,
        out_mom,
        out_sec,
        chan_new,
        chan_mom,
        chan_sec,
    )


def solution(mesh):
    in_specs = (
        P("dp", "seq", None),
        P("dp", "seq", None),
        P("dp", None),
        P("dp", None),
        P("dp", None),
        P("dp", None),
        P("dp", None),
        P("dp", None),
        P(),
        P(),
        P(),
    )
    out_specs = (
        P("dp", "seq", None),
        P("dp", "seq", None),
        P("dp", None),
        P("dp", None),
        P("dp", None),
        P("dp", None),
        P("dp", None),
        P("dp", None),
        P(),
        P(),
        P(),
    )
    return jax.shard_map(local, mesh=mesh, in_specs=in_specs, out_specs=out_specs, check_vma=False)
```

profile of v0, /device:TPU:0, one launch (start us, length us, event | category | flops | bytes accessed | tf_op | source)
XLA Modules:
  0.0 2168.9 jit_solution(13405714208237086959)
XLA Ops:
  12.6 88.0 %all-gather.3.cloned.1.call-done = bf16[768,3352]{1,0:T(8,128)(2,1)} async-done(((bf16[96,3352]{1,0:T(8,128)(2,1)}), bf16[768,3352]{1,0:T(8,128)(2,1)}) %all-gather.3.cloned.1.call-update) | async-done | bytes 5148688 | tf_op jit(solution)/shard_map/all_gather | solution.py:157
  100.6 9.0 convolution_convert_fusion
  134.1 17.2 all-to-all-done.2
  158.8 34.1 %all-to-all-done.1 = bf16[1024,4,384]{2,0,1:T(8,128)(2,1)} async-done(((bf16[1024,4,384]{2,0,1:T(8,128)(2,1)}), bf16[1024,4,384]{2,0,1:T(8,128)(2,1)}, u32[]{:S(2)}, u32[]{:S(2)}) %all-to-all-start.1) | async-done | bytes 3145760 | tf_op jit(solution)/shard_map/all_to_all | solution.py:169
  196.2 8.7 multiply_convert_fusion
  236.9 333.2 %while.41 = (s32[]{:T(128)}, f32[6,64,128]{2,1,0:T(8,128)S(1)}, f32[16,256,6,64]{1,0,3,2:T(8,128)}, f32[16,6,64,128]{3,2,1,0:T(8,128)}, f32[16,256,6]{1,2,0:T(8,...) while((s32[]{:T(128)}, f32[6,64,128]{2,1,0:T(8,128)S(1)}, ...), condition=%wide.region_4.5_spmd.clone, body=%wide.region_1.4_spmd.clone.sunk | while | flops 706761216 | bytes 5769577 | solution.py:97
  245.5 9.9 dynamic_update_slice.89
  266.3 9.9 dynamic_update_slice.89
  287.1 9.9 dynamic_update_slice.89
  307.9 9.9 dynamic_update_slice.89
  328.8 9.9 dynamic_update_slice.89
  349.6 9.9 dynamic_update_slice.89
  370.4 9.9 dynamic_update_slice.89
  391.2 9.9 dynamic_update_slice.89
  412.0 9.9 dynamic_update_slice.89
  432.8 9.9 dynamic_update_slice.89
  453.6 9.9 dynamic_update_slice.89
  474.4 9.9 dynamic_update_slice.89
  495.2 9.9 dynamic_update_slice.89
  515.9 9.9 dynamic_update_slice.89
  536.7 9.9 dynamic_update_slice.89
  557.5 9.9 dynamic_update_slice.89
  570.1 11.4 copy.309
  608.7 35.0 %all-to-all-done.3 = bf16[4,2,196608]{2,1,0:T(2,128)(2,1)S(1)} async-done(((bf16[4,2,196608]{2,1,0:T(2,128)(2,1)}), bf16[4,2,196608]{2,1,0:T(2,128)(2,1)S(1)}, u32[]{:S(2)}, u32[]{:S(2)}) %all-to-all-start.3) | async-done | bytes 3145760 | tf_op jit(solution)/shard_map/all_to_all | solution.py:193
  667.8 8.3 multiply_reduce_fusion.10
  676.1 8.6 fusion.107
  697.5 7.6 fusion.120
  705.1 62.3 %all-to-all-done.4 = f32[1024,4,384]{2,0,1:T(8,128)} async-done(((f32[1024,4,384]{2,0,1:T(8,128)}), f32[1024,4,384]{2,0,1:T(8,128)}, u32[]{:S(2)}, u32[]{:S(2)}) %all-to-all-start.4) | async-done | bytes 6291488 | tf_op jit(solution)/shard_map/all_to_all | solution.py:204
  767.4 8.2 copy.254
  775.7 8.3 reshape_squeeze.6
  789.9 934.4 %while.42 = (s32[]{:T(128)}, f32[6]{0:T(128)}, f32[6,64,128]{2,1,0:T(8,128)}, f32[16,256,6,64]{1,0,3,2:T(8,128)}, f32[16,256,6]{1,2,0:T(8,128)}, /*index=5*/f32[...) while((s32[]{:T(128)}, f32[6]{0:T(128)}, ...), condition=%wide.region_21.22_spmd.clone, body=%wide.region_7.21_spmd.clone.sunk | while | flops 1667868160 | bytes 14989784 | solution.py:97
  822.5 9.9 dynamic_update_slice.93
  834.5 7.6 reduce-window.74
  880.4 9.9 dynamic_update_slice.93
  892.4 7.6 reduce-window.74
  938.9 9.9 dynamic_update_slice.93
  997.3 9.9 dynamic_update_slice.93
  1009.3 7.6 reduce-window.74
  1055.8 9.9 dynamic_update_slice.93
  1114.3 9.9 dynamic_update_slice.93
  1126.3 7.6 reduce-window.74
  1172.8 9.9 dynamic_update_slice.93
  1231.2 9.9 dynamic_update_slice.93
  1243.2 7.6 reduce-window.74
  1289.7 9.9 dynamic_update_slice.93
  1348.2 9.9 dynamic_update_slice.93
  1406.7 9.9 dynamic_update_slice.93
  1465.1 9.9 dynamic_update_slice.93
  1523.6 9.9 dynamic_update_slice.93
  1582.1 9.9 dynamic_update_slice.93
  1640.5 9.9 dynamic_update_slice.93
  1699.0 9.9 dynamic_update_slice.93
  1724.3 11.3 copy.310
  1747.7 20.3 multiply_reduce_fusion.7
  1768.0 14.4 broadcast_multiply_fusion
  1789.5 14.4 pad_add_fusion
  1823.8 19.2 copy.262
  1843.0 10.5 all-to-all-done.5
  1877.1 29.4 %all-to-all-done.6 = f32[4096,1,256]{2,1,0:T(1,128)} async-done(((f32[4096,1,256]{2,1,0:T(1,128)}), f32[4096,1,256]{2,1,0:T(1,128)}, u32[]{:S(2)}, u32[]{:S(2)}) %all-to-all-start.6) | async-done | bytes 4194336 | tf_op jit(solution)/shard_map/all_to_all | solution.py:223
  1913.9 13.0 fusion.125
  1927.6 8.1 fusion.117
  1943.5 11.2 fusion.112
  1954.8 149.6 %reduce-scatter.3.cloned.1.call-done = f32[96,3352]{1,0:T(8,128)} async-done(((f32[768,3352]{1,0:T(8,128)}), f32[96,3352]{1,0:T(8,128)}) %reduce-scatter.3.cloned.1.call-update) | async-done | bytes 1287184 | tf_op jit(solution)/shard_map/reduce_scatter | solution.py:271
  2104.5 40.4 %psum.23 = f32[11336]{0:T(1024)S(1)} all-reduce(f32[11336]{0:T(1024)S(1)} %concatenate.28), channel_id=1, replica_groups=mesh['dp'=8,'seq'=4] {'dp','seq'}, use_global_device_ids=true, to_apply=%region_38.39 | all-reduce | flops 11336 | bytes 90688 | tf_op jit(solution)/shard_map/psum | solution.py:299
  (1404 shorter events, 1147.2 us)
Async XLA Ops:
  7.2 93.4 %all-gather.3.cloned.1.call-start = ((), (), s32[]{:S(2)}) async-start(), calls=%async_computation.10 | async-start | bytes 5971968 | tf_op jit(solution)/shard_map/all_gather | solution.py:157
  10.2 90.4 %copy-start.39 = (f32[768]{0:T(1024)}, f32[768]{0:T(1024)S(1)}, u32[]{:S(2)}) copy-start(f32[768]{0:T(1024)S(1)} %slice.180) | copy-start | bytes 9220
  12.6 88.0 %copy-start.41 = (f32[1024]{0:T(1024)}, f32[1024]{0:T(1024)S(1)}, u32[]{:S(2)}) copy-start(f32[1024]{0:T(1024)S(1)} %fusion.138) | copy-start | bytes 12292
  113.1 7.4 all-to-all-start
  122.0 29.3 %all-to-all-start.2 = ((bf16[1024,4,256]{2,0,1:T(8,128)(2,1)}), bf16[1024,4,256]{2,0,1:T(8,128)(2,1)S(1)}, u32[]{:S(2)}, u32[]{:S(2)}) async-start(bf16[1024,4,256]{2,0,1:T(8,128)(2,1)} %broadcast_in_dim.178), calls=%async_computation.2 | async-start | bytes 4194304 | tf_op jit(solution)/shard_map/all_to_all | solution.py:170
  129.5 26.5 %copy-start.19 = (f32[11336]{0:T(1024)S(1)}, f32[11336]{0:T(1024)}, u32[]{:S(2)}) copy-start(f32[11336]{0:T(1024)} %param.23) | copy-start | bytes 136036
  151.3 4.7 copy-start.2
  151.3 41.7 %all-to-all-start.1 = ((bf16[1024,4,384]{2,0,1:T(8,128)(2,1)}), bf16[1024,4,384]{2,0,1:T(8,128)(2,1)}, u32[]{:S(2)}, u32[]{:S(2)}) async-start(bf16[1024,4,384]{2,0,1:T(8,128)(2,1)} %copy.241), calls=%async_computation.1 | async-start | bytes 6291456 | tf_op jit(solution)/shard_map/all_to_all | solution.py:169
  157.5 539.3 %copy-start.50 = (f32[24]{0:T(128)}, f32[24]{0:T(128)S(1)}, u32[]{:S(2)}) copy-start(f32[24]{0:T(128)S(1)} %get-tuple-element.756) | copy-start | bytes 292
  157.6 38.6 %copy-start.47 = (f32[6]{0:T(128)}, f32[6]{0:T(128)S(1)}, u32[]{:S(2)}) copy-start(f32[6]{0:T(128)S(1)} %dynamic_slice.93) | copy-start | bytes 76
  157.8 430.3 %copy-start.36 = (f32[384]{0:T(512)}, f32[384]{0:T(512)S(1)}, u32[]{:S(2)}) copy-start(f32[384]{0:T(512)S(1)} %mul.746) | copy-start | bytes 4612
  157.8 38.3 %copy-start.24 = (f32[640]{0:T(1024)}, f32[640]{0:T(1024)S(1)}, u32[]{:S(2)}) copy-start(f32[640]{0:T(1024)S(1)} %get-tuple-element.662) | copy-start | bytes 7684
  157.9 38.3 %copy-start.26 = (f32[640]{0:T(1024)}, f32[640]{0:T(1024)S(1)}, u32[]{:S(2)}) copy-start(f32[640]{0:T(1024)S(1)} %get-tuple-element.663) | copy-start | bytes 7684
  157.9 38.3 %copy-start.28 = (f32[640]{0:T(1024)}, f32[640]{0:T(1024)S(1)}, u32[]{:S(2)}) copy-start(f32[640]{0:T(1024)S(1)} %get-tuple-element.664) | copy-start | bytes 7684
  157.9 38.3 %copy-start.30 = (f32[640]{0:T(1024)}, f32[640]{0:T(1024)S(1)}, u32[]{:S(2)}) copy-start(f32[640]{0:T(1024)S(1)} %get-tuple-element.665) | copy-start | bytes 7684
  196.1 8.8 copy-start
  570.1 11.4 copy-start.18
  603.1 40.6 %all-to-all-start.3 = ((bf16[4,2,196608]{2,1,0:T(2,128)(2,1)}), bf16[4,2,196608]{2,1,0:T(2,128)(2,1)S(1)}, u32[]{:S(2)}, u32[]{:S(2)}) async-start(bf16[4,2,196608]{2,1,0:T(2,128)(2,1)} %reshape.575), calls=%async_computation.3 | async-start | bytes 6291456 | tf_op jit(solution)/shard_map/all_to_all | solution.py:193
  606.8 61.0 %all-gather.5.cloned.1.call-start = ((), (), s32[]{:S(2)}) async-start(), calls=%async_computation.11 | async-start | bytes 2654208 | tf_op jit(solution)/shard_map/all_gather | solution.py:158
  608.7 88.8 %copy-start.34 = (f32[1536]{0:T(1024)}, f32[1536]{0:T(1024)S(1)}, u32[]{:S(2)}) copy-start(f32[1536]{0:T(1024)S(1)} %slice.203) | copy-start | bytes 18436
  661.1 15.0 slice-start
  667.7 29.7 %copy-start.43 = (f32[1024]{0:T(1024)}, f32[1024]{0:T(1024)S(1)}, u32[]{:S(2)}) copy-start(f32[1024]{0:T(1024)S(1)} %fusion.139) | copy-start | bytes 12292
  667.8 8.3 slice-start.1
  667.8 8.3 copy-start.1
  691.3 6.1 copy-start.11
  691.3 76.1 %all-to-all-start.4 = ((f32[1024,4,384]{2,0,1:T(8,128)}), f32[1024,4,384]{2,0,1:T(8,128)}, u32[]{:S(2)}, u32[]{:S(2)}) async-start(f32[1024,4,384]{2,0,1:T(8,128)} %copy.253), calls=%async_computation.4 | async-start | bytes 12582912 | tf_op jit(solution)/shard_map/all_to_all | solution.py:204
  696.7 1258.1 %reduce-scatter.5.cloned.1.call-start = ((), (), s32[]{:S(2)}) async-start(), calls=%async_computation.13 | async-start | bytes 5308416 | tf_op jit(solution)/shard_map/reduce_scatter | solution.py:278
  984.6 4.7 copy-start.21
  1335.5 4.7 copy-start.21
  1394.0 4.7 copy-start.21
  1452.4 4.7 copy-start.21
  1510.9 4.7 copy-start.21
  1627.8 4.7 copy-start.21
  1735.7 6.6 copy-start.37
  1742.2 5.4 copy-start.3
  1747.6 20.3 copy-start.25
  1747.6 20.3 copy-start.27
  1747.6 20.3 copy-start.29
  1747.7 20.3 copy-start.31
  1768.0 14.5 copy-start.9
  1768.0 14.5 copy-start.13
  1768.0 14.5 copy-start.48
  1786.2 26.7 %all-to-all-start.7 = ((bf16[4,2,3072]{2,1,0:T(2,128)(2,1)}), bf16[4,2,3072]{2,1,0:T(2,128)(2,1)S(1)}, u32[]{:S(2)}, u32[]{:S(2)}) async-start(bf16[4,2,3072]{2,1,0:T(2,128)(2,1)} %reshape.577), calls=%async_computation.7 | async-start | bytes 98304 | tf_op jit(solution)/shard_map/all_to_all | solution.py:230
  1812.9 40.6 %all-to-all-start.5 = ((bf16[4,2,196608]{2,1,0:T(2,128)(2,1)}), bf16[4,2,196608]{2,1,0:T(2,128)(2,1)S(1)}, u32[]{:S(2)}, u32[]{:S(2)}) async-start(bf16[4,2,196608]{2,1,0:T(2,128)(2,1)} %reshape.579), calls=%async_computation.5 | async-start | bytes 6291456 | tf_op jit(solution)/shard_map/all_to_all | solution.py:216
  1853.5 53.1 %all-to-all-start.6 = ((f32[4096,1,256]{2,1,0:T(1,128)}), f32[4096,1,256]{2,1,0:T(1,128)}, u32[]{:S(2)}, u32[]{:S(2)}) async-start(f32[4096,1,256]{2,1,0:T(1,128)} %copy.262), calls=%async_computation.6 | async-start | bytes 8388608 | tf_op jit(solution)/shard_map/all_to_all | solution.py:223
  1858.3 246.1 %reduce-scatter.3.cloned.1.call-start = ((), (), s32[]{:S(2)}) async-start(), calls=%async_computation.12 | async-start | bytes 11943936 | tf_op jit(solution)/shard_map/reduce_scatter | solution.py:271
  1877.1 36.7 %copy-start.5 = (bf16[1,1024,768]{2,1,0:T(8,128)(2,1)S(1)}, bf16[1,1024,768]{2,1,0:T(8,128)(2,1)}, u32[]{:S(2)}) copy-start(bf16[1,1024,768]{2,1,0:T(8,128)(2,1)} %param.15) | copy-start | bytes 4718596
  1877.1 36.7 %copy-start.40 = (f32[768]{0:T(1024)S(1)}, f32[768]{0:T(1024)}, u32[]{:S(2)}) copy-start(f32[768]{0:T(1024)} %copy-done.39) | copy-start | bytes 9220
  1877.1 36.7 %copy-start.42 = (f32[1024]{0:T(1024)S(1)}, f32[1024]{0:T(1024)}, u32[]{:S(2)}) copy-start(f32[1024]{0:T(1024)} %copy-done.41) | copy-start | bytes 12292
  1926.9 228.8 %all-reduce.17.cloned.1.call-start = ((), (), s32[]{:S(2)}) async-start(), calls=%async_computation.14 | async-start | bytes 3833856 | tf_op jit(solution)/shard_map/psum | solution.py:284
  1927.6 8.1 copy-start.45
  1936.6 6.1 copy-start.49
  1936.6 6.6 copy-start.38
  1936.7 6.6 copy-start.51
  1943.5 11.3 copy-start.33
  1943.5 161.0 %copy-start.46 = (f32[1536]{0:T(1024)S(1)}, f32[1536]{0:T(1024)}, u32[]{:S(2)}) copy-start(f32[1536]{0:T(1024)} %get-tuple-element.656) | copy-start | bytes 18436
  1943.5 201.5 %copy-start.20 = (f32[11336]{0:T(1024)S(1)}, f32[11336]{0:T(1024)}, u32[]{:S(2)}) copy-start(f32[11336]{0:T(1024)} %param.23) | copy-start | bytes 136036
  1943.5 201.5 %copy-start.22 = (f32[11336]{0:T(1024)S(1)}, f32[11336]{0:T(1024)}, u32[]{:S(2)}) copy-start(f32[11336]{0:T(1024)} %param.24) | copy-start | bytes 136036
  1943.5 201.5 %copy-start.23 = (f32[11336]{0:T(1024)S(1)}, f32[11336]{0:T(1024)}, u32[]{:S(2)}) copy-start(f32[11336]{0:T(1024)} %param.25) | copy-start | bytes 136036
  2104.4 51.2 %copy-start.6 = (f32[96,3352]{1,0:T(8,128)S(1)}, f32[96,3352]{1,0:T(8,128)}, u32[]{:S(2)}) copy-start(f32[96,3352]{1,0:T(8,128)} %param.17) | copy-start | bytes 3861508
  2150.6 9.8 copy-start.7
  2150.6 9.8 copy-start.15
  2150.6 9.8 copy-start.16
  2155.7 4.8 copy-start.17
  (63 other events, 145.0 us)
Sparse Core Ops, SparseCore 0:
  10.8 89.7 all-gather.2
  610.4 50.8 all-gather.4
  705.3 93.9 reduce-scatter.4
  1927.0 177.3 reduce-scatter.2
  2106.8 48.7 all-reduce.16
where the time goes:
time: 2200 us; the launch traced here: 2170 us
  local copies, waits for them, and re-layouts  741 us (34%)
  other arithmetic  520 us (24%)
  waiting for transfers between devices  434 us (20%)
  matrix products  382 us (17%)
  blocking collectives  40.4 us (2%)
  starting transfers between devices  32.9 us (1%)
    dynamic_update_slice x64, local copies, waits for them, and re-layouts, state_space(): lax.scan(jax.checkpoint(block_step), state_zero, packed)  330 us
    another operation x145, other arithmetic  257 us
    dot_general x48, matrix products, block_step(): jnp.einsum('hij,jhp->ihp', decays * scores[None, :, :], scaled, precision...  152 us
    reduce_scatter x1, waiting for transfers between devices, local(): lax.psum_scatter(lax.dot_general(columns, proj_grad, grad_pair, preferred...  150 us
    another operation x231, local copies, waits for them, and re-layouts  98.2 us
    all_gather x1, waiting for transfers between devices, local(): lax.all_gather(in_low, 'dp', axis=0, tiled=True)  88 us
    dot_general x64, matrix products, block_step(): jnp.einsum('in,hpn->ihp', block_read, carry_state, precision=highest)  73 us
    unnamed x112, local copies, waits for them, and re-layouts  66.1 us
  transfers between devices with their start and end apart: 13, of which 10 were waited for; matrix products, arithmetic and copies ran while one was open for 54% of the time, Pallas kernels for 0%

commit v1 on v0

v1 whole, which is shorter than its diff:
```python
import math

import jax
import jax.numpy as jnp
from jax import lax
from jax.experimental import pallas as pl
from jax.experimental.pallas import tpu as pltpu
from jax.sharding import PartitionSpec as P

D = 768
HEADS = 24
HEADDIM = 64
STATE = 128
CONV = 4
STEP = 10
INNER = 1536
XBC = 1792
PROJ = 3352
SIDE = 1920
LANES = 128
CHUNK = 128
PAIRS = HEADS // 2
TILES = XBC // LANES
EXTRA = 16

norm_eps = 1e-05
beta_one = 0.9
beta_two = 0.999
adam_eps = 1e-08
rate_matrix = 0.1
rate_channel = 0.5
decay_matrix = 0.1
LOG2E = 1.0 / math.log(2.0)
VMEM = 56 * 1024 * 1024

f32 = jnp.float32
bf16 = jnp.bfloat16
NT = (((1,), (1,)), ((), ()))
TN = (((0,), (0,)), ((), ()))


def dot(a, b):
    return jnp.dot(a, b, preferred_element_type=f32)


def dot_nt(a, b):
    return lax.dot_general(a, b, NT, preferred_element_type=f32)


def dot_tn(a, b):
    return lax.dot_general(a, b, TN, preferred_element_type=f32)


def dot_full(a, b):
    return jnp.dot(a, b, preferred_element_type=f32, precision=lax.Precision.HIGHEST)


def sigmoid(v):
    return 0.5 * jnp.tanh(0.5 * v) + 0.5


def halves(v):
    high = v.astype(bf16)
    return high, (v - high.astype(f32)).astype(bf16)


def expand(v, spread):
    high, rest = halves(v)
    return dot(jnp.concatenate([high, rest], axis=1), spread)


def fold(v):
    return jnp.sum(v.reshape(v.shape[0] // 8, 8, v.shape[1]), axis=0)


def lane(i):
    return slice(i * LANES, (i + 1) * LANES)


def iota(shape, dim):
    return lax.broadcasted_iota(jnp.int32, shape, dim)


def tri(lower):
    rows, cols = iota((CHUNK, CHUNK), 0), iota((CHUNK, CHUNK), 1)
    return (rows >= cols) if lower else (rows <= cols)


def conv_pre(ext, convp, tile):
    cols = lane(tile)
    taps = [ext[5 + k : 5 + k + CHUNK, cols] for k in range(CONV)]
    pre = taps[0] * convp[0:1, cols] + convp[4:5, cols]
    for k in range(1, CONV):
        pre = pre + taps[k] * convp[k : k + 1, cols]
    return pre, taps


def pair_stack(v):
    side = iota(v.shape, 1) < HEADDIM
    zero = jnp.zeros_like(v)
    return jnp.concatenate([jnp.where(side, v, zero), jnp.where(side, zero, v)], axis=0)


def conv_state_kernel(
    proj, halo, convp, headp, spread, x_out, bc_out, u_out, cum_out, cumt_out, dt_out, hst_out,
    pfx_out, send_out, ext, state, scaled, total,
):
    step = pl.program_id(0)

    @pl.when(step == 0)
    def _():
        ext[0:8, :] = halo[8:16, :].astype(f32)
        state[...] = jnp.zeros_like(state)
        total[...] = jnp.zeros_like(total)

    @pl.when(step > 0)
    def _():
        ext[0:8, :] = ext[CHUNK : CHUNK + 8, :]

    ext[8:, :] = proj[:, :XBC].astype(f32)
    raw = proj[:, XBC:].astype(f32) + headp[0:1, :]
    steps = jnp.maximum(raw, 0.0) + jnp.log1p(jnp.exp(-jnp.abs(raw)))
    log_decay = steps * (headp[1:2, :] * (-LOG2E))
    cum = dot_full(jnp.where(tri(True), 1.0, 0.0), log_decay)
    cum_out[...] = cum
    cumt_out[...] = jnp.transpose(cum)[0:32, :]
    dt_out[...] = steps
    last = cum[CHUNK - 1 : CHUNK, :]
    steps_wide = expand(steps, spread[...])
    tail_wide = expand(jnp.exp2(last - cum), spread[...])
    for tile in range(TILES):
        pre, _ = conv_pre(ext, convp, tile)
        value = (pre * sigmoid(pre)).astype(bf16)
        if tile < PAIRS:
            x_out[:, lane(tile)] = value
            u = (value.astype(f32) * steps_wide[:, lane(tile)]).astype(bf16)
            u_out[:, lane(tile)] = u
            scaled[:, lane(tile)] = (u.astype(f32) * tail_wide[:, lane(tile)]).astype(bf16)
        else:
            bc_out[:, lane(tile - PAIRS)] = value
    decay = expand(jnp.broadcast_to(jnp.exp2(last), (8, LANES)), spread[...])[0:1, :]
    new_state = state[...] * decay + dot_tn(bc_out[:, :STATE], scaled[...])
    state[...] = new_state
    hst_out[0] = new_state
    new_total = total[...] + jnp.broadcast_to(last, (8, LANES))
    total[...] = new_total
    pfx_out[0] = new_total

    @pl.when(step == pl.num_programs(0) - 1)
    def _():
        send_out[:STATE, :] = new_state.astype(bf16)
        row = iota((EXTRA, LANES), 0)
        wide = jnp.broadcast_to(new_total[0:1, :], (EXTRA, LANES))
        high, rest = halves(wide)
        left = (wide - high.astype(f32) - rest.astype(f32)).astype(bf16)
        parts = jnp.where(
            row == 0,
            high.astype(f32),
            jnp.where(row == 1, rest.astype(f32), jnp.where(row == 2, left.astype(f32), 0.0)),
        )
        send_out[STATE:, :] = dot(parts.astype(bf16), spread[:LANES, :]).astype(bf16)


def within_kernel(u, bc, cum, cumt, y_out):
    scores = jnp.where(tri(True), dot_nt(bc[:, STATE:], bc[:, :STATE]), 0.0)
    for pair in range(PAIRS):
        weights = []
        for head in (2 * pair, 2 * pair + 1):
            gap = cum[:, head : head + 1] - cumt[head : head + 1, :]
            weights.append((jnp.exp2(jnp.minimum(gap, 0.0)) * scores).astype(bf16))
        y_out[:, lane(pair)] = dot(jnp.concatenate(weights, axis=1), pair_stack(u[:, lane(pair)]))


def arrived(gathered, logs, rank, groups, later):
    sums = [
        jnp.sum(logs[g].astype(f32), axis=0, keepdims=True) for g in range(groups)
    ]
    entered = jnp.zeros((STATE, INNER), f32)
    for g in range(groups):
        between = jnp.zeros((1, INNER), f32)
        for s in range(groups):
            if (s < g) if later else (s > g):
                inside = (s > rank) if later else (s < rank)
                between = between + jnp.where(inside, sums[s], 0.0)
        counts = (g > rank) if later else (g < rank)
        weight = jnp.where(counts, jnp.exp2(between), 0.0)
        entered = entered + gathered[g].astype(f32) * weight
    return entered


def gate_kernel(
    groups, rank, y_in, x, bc, cum, hst, gathered, logs, gate, tok, cot, wout, spread, rows,
    block_out, hidden_out, y_out, dy_out, dgate_out, dcc_out, ust_out, glocal_out, ng_out, h0_out,
    prefix, h0, hg_all, gated_all, dy_scaled,
):
    step = pl.program_id(0)

    @pl.when(step == 0)
    def _():
        value = arrived(gathered, logs, rank[0], groups, False)
        h0[...] = value
        h0_out[...] = value
        prefix[...] = jnp.zeros_like(prefix)
        glocal_out[...] = jnp.zeros_like(glocal_out)
        ng_out[...] = jnp.zeros_like(ng_out)

    start = expand(jnp.exp2(prefix[...]), spread[...])[0:1, :]
    state = h0[...] * start + jnp.where(step > 0, hst[0], 0.0)
    state_low = state.astype(bf16)
    grown = expand(jnp.exp2(cum[...]), spread[...])
    carried = dot(bc[:, STATE:], state_low)
    hg_all[...] = dot_nt(cot[...], wout[...])
    squares = jnp.zeros((CHUNK, LANES), f32)
    cross = jnp.zeros((CHUNK, LANES), f32)
    for tile in range(PAIRS):
        cols = lane(tile)
        y = y_in[:, cols] + carried[:, cols] * grown[:, cols]
        y_out[:, cols] = y
        mixed = (y + rows[1:2, cols] * x[:, cols].astype(f32)).astype(bf16).astype(f32)
        gate_val = gate[:, cols].astype(f32)
        gated = mixed * (gate_val * sigmoid(gate_val))
        gated_all[:, cols] = gated
        squares = squares + gated * gated
        cross = cross + gated * (hg_all[:, cols] * rows[0:1, cols])
    mean = jnp.sum(squares, axis=1, keepdims=True) * (1.0 / INNER)
    scale = lax.rsqrt(mean + norm_eps)
    cross_mean = jnp.sum(cross, axis=1, keepdims=True) * (1.0 / INNER) * scale * scale * scale
    for tile in range(PAIRS):
        cols = lane(tile)
        gated = gated_all[:, cols]
        normal = gated * scale
        hidden_out[:, cols] = (normal * rows[0:1, cols]).astype(bf16)
        grad = hg_all[:, cols]
        ng_out[:, cols] += fold(grad * normal)
        dgated = grad * rows[0:1, cols] * scale - gated * cross_mean
        gate_val = gate[:, cols].astype(f32)
        sig = sigmoid(gate_val)
        silu = gate_val * sig
        mixed = (y_out[:, cols] + rows[1:2, cols] * x[:, cols].astype(f32)).astype(bf16).astype(f32)
        dgate_out[:, cols] = (dgated * mixed * (sig + silu * (1.0 - sig))).astype(bf16)
        dy = (dgated * silu).astype(bf16)
        dy_out[:, cols] = dy
        dy_scaled[:, cols] = (dy.astype(f32) * grown[:, cols]).astype(bf16)
    block_out[...] = tok[...].astype(f32) + dot(hidden_out[...], wout[...])
    update = dot_tn(bc[:, STATE:], dy_scaled[...])
    ust_out[0] = update
    glocal_out[...] += update * start
    dcc_out[...] = dot_nt(dy_scaled[...], state_low)
    prefix[...] += jnp.broadcast_to(cum[CHUNK - 1 : CHUNK, :], (8, LANES))


def within_back_kernel(u, dy, bc, cum, cumt, dxs_out, dbc_out):
    upper = tri(False)
    scores = jnp.where(upper, dot_nt(bc[:, :STATE], bc[:, STATE:]), 0.0)
    total = jnp.zeros((CHUNK, CHUNK), f32)
    for pair in range(PAIRS):
        stacked = pair_stack(dy[:, lane(pair)])
        products = dot_nt(u[:, lane(pair)], stacked)
        weights = []
        for half in range(2):
            head = 2 * pair + half
            gap = cumt[head : head + 1, :] - cum[:, head : head + 1]
            decay = jnp.exp2(jnp.minimum(gap, 0.0))
            weights.append((decay * scores).astype(bf16))
            total = total + decay * products[:, lane(half)]
        dxs_out[:, lane(pair)] = dot(jnp.concatenate(weights, axis=1), stacked)
    low = jnp.where(upper, total, 0.0).astype(bf16)
    dbc_out[:, :STATE] = dot(low, bc[:, STATE:])
    dbc_out[:, STATE:] = dot_tn(low, bc[:, :STATE])


def back_kernel(
    groups, rank, dxs, dy, x, u, y, bc, dbc, dcc, cum, dt, hst, pfx, h0, gathered, logs, ust, proj,
    before, halo, convp, headp, spread, collect, rows,
    pg_out, first_out, tail_out, wg_out, hg_out, skip_out,
    gstate, ext, dext, scaled, prod_q, prod_p,
):
    step = pl.program_id(0)
    chunk = pl.num_programs(0) - 1 - step

    @pl.when(step == 0)
    def _():
        gstate[...] = arrived(gathered, logs, rank[0], groups, True)
        dext[CHUNK:, :] = jnp.zeros((8, XBC), f32)
        wg_out[...] = jnp.zeros_like(wg_out)
        hg_out[...] = jnp.zeros_like(hg_out)
        skip_out[...] = jnp.zeros_like(skip_out)

    @pl.when(step > 0)
    def _():
        dext[CHUNK:, :] = dext[0:8, :]

    @pl.when(chunk == 0)
    def _():
        ext[0:8, :] = halo[8:16, :].astype(f32)

    @pl.when(chunk > 0)
    def _():
        ext[0:8, :] = before[8:16, :XBC].astype(f32)

    ext[8:, :] = proj[:, :XBC].astype(f32)
    grad_state = gstate[...]
    grad_low = grad_state.astype(bf16)
    last = cum[CHUNK - 1 : CHUNK, :]
    tail_wide = expand(jnp.exp2(last - cum[...]), spread[...])
    steps_wide = expand(dt[...], spread[...])
    reach = dot(bc[:, :STATE], grad_low)

    def conv_back(tile, grad):
        cols = lane(tile)
        pre, taps = conv_pre(ext, convp, tile)
        sig = sigmoid(pre)
        dpre = grad * (sig + pre * sig * (1.0 - sig))
        dext[0:CHUNK, cols] = dpre
        for k in range(CONV):
            wg_out[8 * k : 8 * k + 8, cols] += fold(dpre * taps[k])
        wg_out[32:40, cols] += fold(dpre)
        source = dpre * convp[3:4, cols]
        for k in range(CONV - 1):
            source = source + dext[3 - k : 3 - k + CHUNK, cols] * convp[k : k + 1, cols]
        pg_out[:, cols] = source.astype(bf16)

        @pl.when(step == 0)
        def _():
            tail_out[:, cols] = source[CHUNK - 8 :, :]

    for tile in range(PAIRS):
        cols = lane(tile)
        dxs_full = dxs[:, cols] + tail_wide[:, cols] * reach[:, cols]
        uf = u[:, cols].astype(f32)
        dyf = dy[:, cols].astype(f32)
        scaled[:, cols] = (uf * tail_wide[:, cols]).astype(bf16)
        q = uf * dxs_full
        high, rest = halves(q)
        prod_q[:, cols] = high
        prod_q[:, INNER + tile * LANES : INNER + (tile + 1) * LANES] = rest
        high, rest = halves(dyf * y[:, cols] - q)
        prod_p[:, cols] = high
        prod_p[:, INNER + tile * LANES : INNER + (tile + 1) * LANES] = rest
        skip_out[:, cols] += fold(dyf * x[:, cols].astype(f32))
        conv_back(tile, rows[1:2, cols] * dyf + steps_wide[:, cols] * dxs_full)
    conv_back(PAIRS, dbc[:, :STATE] + dot_nt(scaled[...], grad_low))
    conv_back(PAIRS + 1, dbc[:, STATE:] + dcc[...])
    first_out[...] = dext[0:8, :]

    q_heads = dot(prod_q[...], collect[...])
    gap_heads = dot(prod_p[...], collect[...])
    end = expand(jnp.exp2(pfx[0]), spread[...])[0:1, :]
    meet = fold(grad_state * (hst[0] + h0[...] * end))
    meet_high, meet_rest = halves(meet)
    meet_heads = jnp.sum(
        dot(jnp.concatenate([meet_high, meet_rest], axis=1), collect[...]), axis=0, keepdims=True
    )
    dlog = dot_full(jnp.where(tri(False), 1.0, 0.0), gap_heads) + meet_heads
    sig = sigmoid(proj[:, XBC:].astype(f32) + headp[0:1, :])
    steps = dt[...]
    ratio = jnp.where(steps > 1e-30, sig / jnp.maximum(steps, 1e-30), 1.0)
    raw_grad = q_heads * ratio - dlog * headp[1:2, :] * sig
    pg_out[:, XBC:] = raw_grad.astype(bf16)
    hg_out[0:8, :] += fold(raw_grad)
    hg_out[8:16, :] += fold(dlog * steps * headp[1:2, :]) * (-1.0)
    decay = expand(jnp.broadcast_to(jnp.exp2(last), (8, LANES)), spread[...])[0:1, :]
    gstate[...] = grad_state * decay + ust[0]


def full(shape):
    return pl.BlockSpec(shape, lambda c: (0,) * len(shape))


def by_chunk(width, rows=CHUNK):
    return pl.BlockSpec((rows, width), lambda c: (c, 0))


def shape(dims, dtype):
    return jax.ShapeDtypeStruct(dims, dtype)


def params():
    return pltpu.CompilerParams(dimension_semantics=("arbitrary",), vmem_limit_bytes=VMEM)


def cost(flops, moved):
    return pl.CostEstimate(flops=flops, bytes_accessed=moved, transcendentals=0)


def spread_map():
    heads = jnp.arange(LANES)[:, None]
    cols = jnp.arange(INNER)[None, :] // HEADDIM
    once = (heads == cols).astype(bf16)
    return jnp.concatenate([once, once], axis=0)


def unpack_channels(channels):
    pieces = []
    offset = 0
    for piece_len in (D, INNER, XBC * CONV, XBC, HEADS, HEADS, HEADS):
        pieces.append(channels[offset : offset + piece_len])
        offset = offset + piece_len
    pre_gain, norm_gain, conv_flat, conv_bias, step_bias, rate_log, skip_gain = pieces
    return (
        pre_gain,
        norm_gain,
        conv_flat.reshape(XBC, CONV),
        conv_bias,
        step_bias,
        rate_log,
        skip_gain,
    )


def pre_norm(tok_vals, pre_gain):
    return (
        tok_vals * lax.rsqrt(jnp.mean(tok_vals * tok_vals, -1, keepdims=True) + norm_eps) * pre_gain
    )


def adamw_step(weight, moment, second, gradient, step_rate, decay_rate):
    moment_next = beta_one * moment + (1.0 - beta_one) * gradient
    second_next = beta_two * second + (1.0 - beta_two) * gradient * gradient
    first_fix = 1.0 - beta_one**STEP
    second_fix = 1.0 - beta_two**STEP
    update = moment_next / first_fix / (jnp.sqrt(second_next / second_fix) + adam_eps)
    return (weight - step_rate * (update + decay_rate * weight), moment_next, second_next)


def local(
    tokens,
    cotangent,
    in_weight,
    in_moment,
    in_second,
    out_weight,
    out_moment,
    out_second,
    channels,
    channel_moment,
    channel_second,
):
    groups = lax.axis_size("seq")
    everyone = ("dp", "seq")
    seq_rank = lax.axis_index("seq")
    rank = seq_rank.astype(jnp.int32).reshape(1)
    pre_gain, norm_gain, conv_weight, conv_bias, step_bias, rate_log, skip_gain = unpack_channels(
        channels
    )
    tok_low = tokens[0]
    cot_low = cotangent[0]
    count = tok_low.shape[0]
    chunks = count // CHUNK

    def quarter(weight):
        size = weight.shape[0] // groups
        return lax.dynamic_slice_in_dim(weight, seq_rank * size, size, 0).astype(bf16)

    in_part = quarter(in_weight)
    side_part = jnp.pad(in_part[:, INNER:], ((0, 0), (0, SIDE + INNER - PROJ)))
    full_side = lax.all_gather(side_part, everyone, axis=0, tiled=True)
    full_gate = lax.all_gather(in_part[:, :INNER], everyone, axis=0, tiled=True)
    full_out = lax.all_gather(quarter(out_weight), everyone, axis=0, tiled=True)

    forward = [(s, s + 1) for s in range(groups - 1)]
    backward = [(s + 1, s) for s in range(groups - 1)]
    tok_halo = lax.ppermute(tok_low[count - 16 :], "seq", forward)
    halo_norm = pre_norm(tok_halo.astype(f32), pre_gain).astype(bf16)
    tok_vals = tok_low.astype(f32)
    normed_low = pre_norm(tok_vals, pre_gain).astype(bf16)

    convp = jnp.concatenate(
        [conv_weight.T, conv_bias[None, :], jnp.zeros((3, XBC), f32)], axis=0
    )
    pad_heads = lambda v: jnp.pad(v, (0, LANES - HEADS))[None, :]
    headp = jnp.concatenate(
        [pad_heads(step_bias), pad_heads(jnp.exp(rate_log)), jnp.zeros((6, LANES), f32)], axis=0
    )
    rows = jnp.concatenate(
        [norm_gain[None, :], jnp.repeat(skip_gain, HEADDIM)[None, :], jnp.zeros((6, INNER), f32)],
        axis=0,
    )
    spread = spread_map()
    collect = jnp.concatenate([spread[:LANES].T, spread[:LANES].T], axis=0)

    proj = dot(normed_low, full_side).astype(bf16)
    halo = dot(halo_norm, full_side[:, :XBC]).astype(bf16)

    x, bc, u, cum, cumt, dt, hst, pfx, send = pl.pallas_call(
        conv_state_kernel,
        grid=(chunks,),
        in_specs=[
            by_chunk(SIDE), full((16, XBC)), full((8, XBC)), full((8, LANES)),
            full((2 * LANES, INNER)),
        ],
        out_specs=[
            by_chunk(INNER), by_chunk(2 * STATE), by_chunk(INNER), by_chunk(LANES),
            pl.BlockSpec((32, CHUNK), lambda c: (0, c)), by_chunk(LANES),
            pl.BlockSpec((1, STATE, INNER), lambda c: (c, 0, 0)),
            pl.BlockSpec((1, 8, LANES), lambda c: (c, 0, 0)),
            full((STATE + EXTRA, INNER)),
        ],
        out_shape=[
            shape((count, INNER), bf16), shape((count, 2 * STATE), bf16),
            shape((count, INNER), bf16), shape((count, LANES), f32), shape((32, count), f32),
            shape((count, LANES), f32), shape((chunks, STATE, INNER), f32),
            shape((chunks, 8, LANES), f32), shape((STATE + EXTRA, INNER), bf16),
        ],
        scratch_shapes=[
            pltpu.VMEM((CHUNK + 8, XBC), f32), pltpu.VMEM((STATE, INNER), f32),
            pltpu.VMEM((CHUNK, INNER), bf16), pltpu.VMEM((8, LANES), f32),
        ],
        compiler_params=params(),
        cost_estimate=cost(10**9, 24 * 2**20),
        name="conv_state",
    )(proj, halo, convp, headp, spread)

    states = lax.all_gather(send, "seq", axis=0, tiled=False)

    y_within = pl.pallas_call(
        within_kernel,
        grid=(chunks,),
        in_specs=[
            by_chunk(INNER), by_chunk(2 * STATE), by_chunk(LANES),
            pl.BlockSpec((32, CHUNK), lambda c: (0, c)),
        ],
        out_specs=by_chunk(INNER),
        out_shape=shape((count, INNER), f32),
        compiler_params=params(),
        cost_estimate=cost(4 * 10**9, 16 * 2**20),
        name="within",
    )(u, bc, cum, cumt)
    gate = dot(normed_low, full_gate).astype(bf16)

    gathered_spec = full((groups, STATE, INNER))
    logs_spec = pl.BlockSpec((groups, EXTRA, INNER), lambda c: (0, STATE // EXTRA, 0))
    smem = pl.BlockSpec(memory_space=pltpu.SMEM)

    def gate_call(*refs):
        gate_kernel(groups, *refs)

    block, hidden, y, dy, dgate, dcc, ust, glocal, ng, h0 = pl.pallas_call(
        gate_call,
        grid=(chunks,),
        in_specs=[
            smem, by_chunk(INNER), by_chunk(INNER), by_chunk(2 * STATE), by_chunk(LANES),
            pl.BlockSpec((1, STATE, INNER), lambda c: (jnp.maximum(c - 1, 0), 0, 0)),
            gathered_spec, logs_spec, by_chunk(INNER), by_chunk(D), by_chunk(D),
            full((INNER, D)), full((2 * LANES, INNER)), full((8, INNER)),
        ],
        out_specs=[
            by_chunk(D), by_chunk(INNER), by_chunk(INNER), by_chunk(INNER), by_chunk(INNER),
            by_chunk(LANES), pl.BlockSpec((1, STATE, INNER), lambda c: (c, 0, 0)),
            full((STATE, INNER)), full((8, INNER)), full((STATE, INNER)),
        ],
        out_shape=[
            shape((count, D), f32), shape((count, INNER), bf16), shape((count, INNER), f32),
            shape((count, INNER), bf16), shape((count, INNER), bf16), shape((count, LANES), f32),
            shape((chunks, STATE, INNER), f32), shape((STATE, INNER), f32), shape((8, INNER), f32),
            shape((STATE, INNER), f32),
        ],
        scratch_shapes=[
            pltpu.VMEM((8, LANES), f32), pltpu.VMEM((STATE, INNER), f32),
            pltpu.VMEM((CHUNK, INNER), f32), pltpu.VMEM((CHUNK, INNER), f32),
            pltpu.VMEM((CHUNK, INNER), bf16),
        ],
        compiler_params=params(),
        cost_estimate=cost(8 * 10**9, 48 * 2**20),
        name="gate_norm",
    )(
        rank, y_within, x, bc, cum, hst, states, states, gate, tok_low, cot_low, full_out, spread,
        rows,
    )

    grads = lax.all_gather(glocal.astype(bf16), "seq", axis=0, tiled=False)

    dxs, dbc = pl.pallas_call(
        within_back_kernel,
        grid=(chunks,),
        in_specs=[
            by_chunk(INNER), by_chunk(INNER), by_chunk(2 * STATE), by_chunk(LANES),
            pl.BlockSpec((32, CHUNK), lambda c: (0, c)),
        ],
        out_specs=[by_chunk(INNER), by_chunk(2 * STATE)],
        out_shape=[shape((count, INNER), f32), shape((count, 2 * STATE), f32)],
        compiler_params=params(),
        cost_estimate=cost(8 * 10**9, 16 * 2**20),
        name="within_back",
    )(u, dy, bc, cum, cumt)

    def summed(left, right):
        product = lax.dot_general(left, right, TN, preferred_element_type=f32).astype(bf16)
        return lax.psum_scatter(product, everyone, scatter_dimension=0, tiled=True)

    out_scattered = summed(hidden, cot_low)
    gate_scattered = summed(normed_low, dgate)

    def back(width, height=CHUNK):
        return pl.BlockSpec((height, width), lambda c: (chunks - 1 - c, 0))

    def back_three(height):
        return pl.BlockSpec((1, height, INNER), lambda c: (chunks - 1 - c, 0, 0))

    def back_call(*refs):
        back_kernel(groups, *refs)

    per = CHUNK // 16
    pg, first, tail, wg, hgr, skip = pl.pallas_call(
        back_call,
        grid=(chunks,),
        in_specs=[
            smem, back(INNER), back(INNER), back(INNER), back(INNER), back(INNER), back(2 * STATE),
            back(2 * STATE), back(LANES), back(LANES), back(LANES), back_three(STATE),
            pl.BlockSpec((1, 8, LANES), lambda c: (chunks - 1 - c, 0, 0)),
            full((STATE, INNER)), gathered_spec, logs_spec, back_three(STATE), back(SIDE),
            pl.BlockSpec(
                (16, SIDE), lambda c: (jnp.maximum((chunks - 1 - c) * per - 1, 0), 0)
            ),
            full((16, XBC)), full((8, XBC)), full((8, LANES)), full((2 * LANES, INNER)),
            full((2 * INNER, LANES)), full((8, INNER)),
        ],
        out_specs=[
            back(SIDE), full((8, XBC)), full((8, XBC)), full((40, XBC)), full((16, LANES)),
            full((8, INNER)),
        ],
        out_shape=[
            shape((count, SIDE), bf16), shape((8, XBC), f32), shape((8, XBC), f32),
            shape((40, XBC), f32), shape((16, LANES), f32), shape((8, INNER), f32),
        ],
        scratch_shapes=[
            pltpu.VMEM((STATE, INNER), f32), pltpu.VMEM((CHUNK + 8, XBC), f32),
            pltpu.VMEM((CHUNK + 8, XBC), f32), pltpu.VMEM((CHUNK, INNER), bf16),
            pltpu.VMEM((CHUNK, 2 * INNER), bf16), pltpu.VMEM((CHUNK, 2 * INNER), bf16),
        ],
        compiler_params=params(),
        cost_estimate=cost(4 * 10**9, 48 * 2**20),
        name="mixer_back",
    )(
        rank, dxs, dy, x, u, y, bc, dbc, dcc, cum, dt, hst, pfx, h0, grads, states, ust, proj, proj,
        halo, convp, headp, spread, collect, rows,
    )

    after = lax.ppermute(first, "seq", backward)
    fixes = [jnp.zeros((5, XBC), f32)]
    for m in range(CONV - 1):
        fix = convp[0] * after[m]
        for k in range(1, m + 1):
            fix = fix + convp[k] * after[m - k]
        fixes.append(fix[None, :])
    tail_low = (tail + jnp.concatenate(fixes, axis=0)).astype(bf16)
    pg = lax.dynamic_update_slice(pg, tail_low, (count - 8, 0))

    side_scattered = summed(normed_low, pg)

    normed_grad = lax.dot_general(dgate, full_gate, NT, preferred_element_type=f32)
    normed_grad = normed_grad + lax.dot_general(pg, full_side, NT, preferred_element_type=f32)
    _, norm_pull = jax.vjp(pre_norm, tok_vals, pre_gain)
    tok_norm_grad, pre_gain_grad = norm_pull(normed_grad)
    token_grad = (cot_low.astype(f32) + tok_norm_grad)[None]

    wg_sum = jnp.sum(wg.reshape(5, 8, XBC), axis=1)
    chan_grad = jnp.concatenate(
        [
            pre_gain_grad,
            jnp.sum(ng, axis=0),
            wg_sum[:CONV].T.reshape(-1),
            wg_sum[CONV],
            jnp.sum(hgr[:8, :HEADS], axis=0),
            jnp.sum(hgr[8:, :HEADS], axis=0),
            jnp.sum(skip.reshape(8, HEADS, HEADDIM), axis=(0, 2)),
        ]
    )
    chan_grad = lax.psum(chan_grad, everyone)

    def owned(part):
        return lax.all_gather(part, "seq", axis=0, tiled=True).astype(f32)

    out_grad = owned(out_scattered)
    in_grad = jnp.concatenate(
        [owned(gate_scattered), owned(side_scattered)[:, : PROJ - INNER]], axis=1
    )
    in_new, in_mom, in_sec = adamw_step(
        in_weight, in_moment, in_second, in_grad, rate_matrix, decay_matrix
    )
    out_new, out_mom, out_sec = adamw_step(
        out_weight, out_moment, out_second, out_grad, rate_matrix, decay_matrix
    )
    chan_new, chan_mom, chan_sec = adamw_step(
        channels, channel_moment, channel_second, chan_grad, rate_channel, 0.0
    )
    return (
        block[None],
        token_grad,
        in_new,
        in_mom,
        in_sec,
        out_new,
        out_mom,
        out_sec,
        chan_new,
        chan_mom,
        chan_sec,
    )


def solution(mesh):
    acts = P("dp", "seq", None)
    rows = P("dp", None)
    specs = (acts, acts) + (rows,) * 6 + (P(),) * 3
    return jax.shard_map(local, mesh=mesh, in_specs=specs, out_specs=specs, check_vma=False)
```

time: 2200 us -> 588 us (0.27); the launches traced: 2170 us -> 586 us
  local copies, waits for them, and re-layouts: 741 us -> 11 us
  other arithmetic: 520 us -> 22.3 us
  matrix products: 382 us -> 46.5 us
  waiting for transfers between devices: 434 us -> 318 us
  Pallas kernels: 0 us -> 108 us
  starting transfers between devices: 32.9 us -> 4.37 us
    dot_general x230 -> x8, matrix products: 382 us -> 46.5 us  [the longest x3 19.4 us: summed(): lax.dot_general(left, right, TN, preferred_element_type=f32).astype(bf16)]
    dynamic_update_slice x68 -> x0, local copies, waits for them, and re-layouts: 331 us -> none  [the longest x64 330 us: state_space(): lax.scan(jax.checkpoint(block_step), state_zero, packed)]
    another operation x161 -> x0, other arithmetic: 271 us -> none
    all_to_all x8 -> x0, waiting for transfers between devices: 191 us -> none  [the longest x1 62.3 us: local(): lax.all_to_all(mixed_grad.reshape(tok_count, groups, local_width), 'seq',...]
    pallas_call x0 -> x5, Pallas kernels: none -> 108 us  [the longest x1 40.5 us: local(): pl.pallas_call(back_call, grid=(chunks,), in_specs=[smem, back(INNER), ba...]
    another operation x233 -> x1, local copies, waits for them, and re-layouts: 107 us -> 0.08 us  [local(): jnp.repeat(skip_gain, HEADDIM)[None, :]]
    unnamed x5 -> x9, waiting for transfers between devices: 0.08 us -> 89.6 us
    reduce_scatter x2, waiting for transfers between devices: 150 us -> 82 us  [summed(): return lax.psum_scatter(product, everyone, scatter_dimension=0, tiled=True)]
  transfers between devices with their start and end apart: 13 -> 10, of which waited for: 10 -> 6; matrix products, arithmetic and copies ran while one was open for 54% -> 12% of each run, Pallas kernels for 0% -> 14%
where the time goes in v1:
time: 588 us; the launch traced here: 586 us
  waiting for transfers between devices  318 us (54%)
  Pallas kernels  108 us (18%)
  blocking collectives  61.7 us (10%)
  matrix products  46.5 us (8%)
  other arithmetic  22.3 us (4%)
  between operations  14.5 us (2%)
  local copies, waits for them, and re-layouts  11 us (2%)
    unnamed x9, waiting for transfers between devices  89.6 us
    reduce_scatter x2, waiting for transfers between devices, summed(): return lax.psum_scatter(product, everyone, scatter_dimension=0, tiled=True)  82 us
    all_gather x1, waiting for transfers between devices, local(): full_side = lax.all_gather(side_part, everyone, axis=0, tiled=True)  52.5 us
    all_gather x1, waiting for transfers between devices, local(): full_out = lax.all_gather(quarter(out_weight), everyone, axis=0, tiled=True)  44.1 us
    psum x1, blocking collectives, local(): chan_grad = lax.psum(chan_grad, everyone)  42.1 us
    pallas_call x1, Pallas kernels, local(): pl.pallas_call(back_call, grid=(chunks,), in_specs=[smem, back(INNER), ba...  40.5 us
    all_gather x1, waiting for transfers between devices, local(): full_gate = lax.all_gather(in_part[:, :INNER], everyone, axis=0, tiled=True)  27.8 us
    pallas_call x1, Pallas kernels, local(): pl.pallas_call(gate_call, grid=(chunks,), in_specs=[smem, by_chunk(INNER)...  26.2 us
  transfers between devices with their start and end apart: 10, of which 6 were waited for; matrix products, arithmetic and copies ran while one was open for 12% of the time, Pallas kernels for 14%

profile of v1, /device:TPU:0, one launch (start us, length us, event | category | flops | bytes accessed | tf_op | source)
XLA Modules:
  0.0 585.9 jit_solution(9671818515709721872)
XLA Ops:
  7.3 1.1 dynamic-slice_convert_fusion
  8.4 0.7 pad.11
  9.1 0.6 slice.109
  9.7 0.1 all-gather.10.cloned.1.call-update
  9.8 0.0 all-gather.12.cloned.1.call-start
  9.9 1.6 dynamic-slice_convert_fusion.1
  11.5 0.7 slice_bitcast_fusion.1
  12.2 2.3 collective-permute-start
  14.6 0.7 slice.90
  15.3 0.8 slice.89
  16.1 0.1 pad.29.clone
  16.1 0.1 pad.32.clone
  16.2 0.9 reshape.111
  17.2 0.3 copy.27
  17.5 0.1 fusion.42
  17.6 0.4 fusion.6
  18.0 0.1 iota_compare_fusion.1
  18.1 0.9 add_convert_fusion.spread.refs_12_.refs_22_
  19.0 0.7 maximum_maximum_fusion.convp.refs_20_
  19.7 0.7 maximum_maximum_fusion.2.headp.refs_21_
  20.4 0.1 fusion.18
  20.5 52.5 %all-gather.8.cloned.1.call-done = bf16[768,1920]{1,0:T(8,128)(2,1)} async-done(((bf16[24,1920]{1,0:T(8,128)(2,1)}), bf16[768,1920]{1,0:T(8,128)(2,1)}) %all-gather.8.cloned.1.call-update) | async-done | bytes 2949136 | tf_op jit(solution)/shard_map/all_gather | solution.py:457
  73.0 2.9 fusion.10.halo.refs_19_
  75.9 6.9 %convolution_convert_fusion.1.proj.refs_17_.refs_18_ = bf16[1024,1920]{1,0:T(8,128)(2,1)} fusion(bf16[768,1920]{1,0:T(8,128)(2,1)} %all-gather.8.cloned.1.call-done, f32[768]{0:T(1024)S(1)} %slice.84, f32[1024]{0:T(1024)S(1)} %fusion.31, bf16[1,1024,768]{2,1,0:T(8,128)(2,1)S(1)} %copy-done), kind=kOutput, calls=%fused_computation.6 | convolution fusion | flops 3025010688 | bytes 8461312 | tf_op jit(solution)/shard_map/dot_general | solution.py:43
  82.8 21.0 %conv_state.1 = (bf16[1024,1536]{1,0:T(8,128)(2,1)}, bf16[1024,256]{1,0:T(8,128)(2,1)}, bf16[1024,1536]{1,0:T(8,128)(2,1)}, f32[1024,128]{1,0:T(8,128)}, f32[32,...) custom-call(bf16[1024,1920]{1,0:T(8,128)(2,1)} %convolution_convert_, ...), custom_call_target="tpu_custom_call" | custom-call | flops 1000000000 | bytes 25165824 | tf_op jit(solution)/shard_map/conv_state/pallas_call | solution.py:485
  103.9 0.1 broadcast_in_dim.53
  104.0 0.1 broadcast_in_dim_reshape.3
  104.1 0.7 maximum_maximum_fusion.1.refs_13_.refs_24_
  104.8 27.8 %all-gather.10.cloned.1.call-done = bf16[768,1536]{1,0:T(8,128)(2,1)} async-done(((bf16[24,1536]{1,0:T(8,128)(2,1)}), bf16[768,1536]{1,0:T(8,128)(2,1)}) %all-gather.10.cloned.1.call-update) | async-done | bytes 2359312 | tf_op jit(solution)/shard_map/all_gather | solution.py:458
  132.6 5.8 convolution_convert_fusion.refs_8_
  138.4 9.7 %within.1.refs_1_ = f32[1024,1536]{1,0:T(8,128)} custom-call(bf16[1024,1536]{1,0:T(8,128)(2,1)} %get-tuple-element.38.u.refs_4_, bf16[1024,256]{1,0:T(8,128)(2,1)} %get-tuple-element.39.bc.refs_3_.refs_6_, f32[1024,128]{1,0:T(8,128)} %get-tuple-element.40.cum.refs_4_.refs_9_, f32[32,1024]{1,0:T(8,128)} %get-tuple-element.41.cumt), custom_call_target="tpu_custom_call" | custom-call | flops 4000000000 | bytes 16777216 | tf_op jit(solution)/shard_map/within/pallas_call | solution.py:516
  148.1 44.1 %all-gather.12.cloned.1.call-done.refs_11_ = bf16[1536,768]{1,0:T(8,128)(2,1)} async-done(((bf16[48,768]{1,0:T(8,128)(2,1)}), bf16[1536,768]{1,0:T(8,128)(2,1)}) %all-gather.12.cloned.1.call-update) | async-done | bytes 2359312 | tf_op jit(solution)/shard_map/all_gather | solution.py:459
  192.3 21.7 %all-gather.14.cloned.1.call-done = bf16[576,1536]{1,0:T(8,128)(2,1)} async-done(((bf16[144,1536]{1,0:T(8,128)(2,1)}), bf16[576,1536]{1,0:T(8,128)(2,1)}) %all-gather.14.cloned.1.call-update) | async-done | bytes 1769488 | tf_op jit(solution)/shard_map/all_gather | solution.py:514
  213.9 26.2 %gate_norm.1 = (f32[1024,768]{1,0:T(8,128)}, bf16[1024,1536]{1,0:T(8,128)(2,1)}, f32[1024,1536]{1,0:T(8,128)}, bf16[1024,1536]{1,0:T(8,128)(2,1)}, bf16[1024,153...) custom-call(s32[1]{0:T(128)} %bitcast.refs_0_, ...), custom_call_target="tpu_custom_call" | custom-call | flops 8000000000 | bytes 50331648 | tf_op jit(solution)/shard_map/gate_norm/pallas_call | solution.py:538
  240.1 1.9 convert_element_type.67
  242.1 0.2 reduce-scatter.8.cloned.1.call-start
  242.3 6.1 %convolution_convert_fusion.2 = bf16[1536,768]{1,0:T(8,128)(2,1)} fusion(bf16[1024,1536]{1,0:T(8,128)(2,1)} %get-tuple-element.60, bf16[1,1024,768]{2,1,0:T(8,128)(2,1)S(1)} %copy-done.2), kind=kOutput, calls=%fused_computation.9 | convolution fusion | flops 2417098752 | bytes 7077888 | tf_op jit(solution)/shard_map/dot_general | solution.py:588
  248.5 0.3 iota_compare_fusion
  248.8 6.2 %convolution_convert_fusion.3 = bf16[768,1536]{1,0:T(8,128)(2,1)} fusion(bf16[1024,1536]{1,0:T(8,128)(2,1)} %get-tuple-element.46, f32[768]{0:T(1024)S(1)} %slice.84, f32[1024]{0:T(1024)S(1)} %fusion.31, bf16[1,1024,768]{2,1,0:T(8,128)(2,1)S(1)} %copy-done.1), kind=kOutput, calls=%fused_computation.10 | convolution fusion | flops 2420244480 | bytes 7085056 | tf_op jit(solution)/shard_map/dot_general | solution.py:588
  255.1 1.0 add_convert_fusion.1.refs_23_
  256.2 10.5 %within_back.1 = (f32[1024,1536]{1,0:T(8,128)}, f32[1024,256]{1,0:T(8,128)}) custom-call(bf16[1024,1536]{1,0:T(8,128)(2,1)} %get-tuple-element.38.u.refs_4_, bf16[1024,1536]{1,0:T(8,128)(2,1)} %get-tuple-element.47.dy.refs_2_, bf16[1024,256]{1,0:T(8,128)(2,1)} %get-tuple-element.39.bc.refs_3_.refs_6_, f32[1024,128]{1,0:T(8,128)} %get-tuple-element.40.cum.refs_4_.refs_9_, ...), custom_call_target="tpu_custom_call" | custom-call | flops 8000000000 | bytes 16777216 | tf_op jit(solution)/shard_map/within_back/pallas_call | solution.py:573
  266.6 40.5 %mixer_back.1 = (bf16[1024,1920]{1,0:T(8,128)(2,1)}, f32[8,1792]{1,0:T(8,128)}, f32[8,1792]{1,0:T(8,128)}, f32[40,1792]{1,0:T(8,128)}, f32[16,128]{1,0:T(8,128)}, /*index=5*/f32[8,1536]{1,0:T(8,128)}) custom-call(s32[1]{0:T(128)} %bitcast.refs_0_, f32[1024,1536]{1,0:T(8,128)} %get-tuple-element.48.refs_1_, bf16[1024,1536]{1,0:T(8,128)(2,1)} %get-tuple-element.47.dy.refs_2_, ...), custom_call_target="tpu_custom_call" | custom-call | flops 4000000000 | bytes 50331648 | tf_op jit(solution)/shard_map/mixer_back/pallas_call | solution.py:604
  307.1 1.5 collective-permute-start.1
  308.7 1.0 bitcast_reduce_fusion
  309.7 0.8 reduce_sum.108
  310.5 0.1 reduce_sum.109
  310.6 0.1 reduce_sum.110
  310.8 1.5 fusion.22
  312.3 7.1 %convolution_convert_fusion.4 = bf16[768,1920]{1,0:T(8,128)(2,1)} fusion(bf16[1024,1920]{1,0:T(8,128)(2,1)} %fusion.22, f32[768]{0:T(1024)S(1)} %slice.84, f32[1024]{0:T(1024)S(1)} %fusion.31, bf16[1,1024,768]{2,1,0:T(8,128)(2,1)S(1)} %copy-done.1), kind=kOutput, calls=%fused_computation.11 | convolution fusion | flops 3024519168 | bytes 8461312 | tf_op jit(solution)/shard_map/dot_general | solution.py:588
  319.4 1.3 copy.28
  320.6 1.7 reshape.113
  322.4 6.7 %fusion.43 = f32[1024,768]{1,0:T(8,128)S(1)} fusion(bf16[1024,1920]{1,0:T(8,128)(2,1)} %fusion.22, bf16[768,1920]{1,0:T(8,128)(2,1)} %all-gather.8.cloned.1.call-done), kind=kOutput, calls=%fused_computation.84 | convolution fusion | flops 3019898880 | bytes 10027008 | tf_op jit(solution)/shard_map/dot_general | solution.py:652
  329.1 4.8 fusion.3
  333.9 0.1 concatenate.41
  334.0 42.1 %psum.7 = f32[11336]{0:T(1024)S(1)} all-reduce(f32[11336]{0:T(1024)S(1)} %concatenate.41), channel_id=1, replica_groups=mesh['dp'=8,'seq'=4] {'dp','seq'}, use_global_device_ids=true, to_apply=%region_13.14 | all-reduce | flops 11336 | bytes 90688 | tf_op jit(solution)/shard_map/psum | solution.py:669
  376.1 0.7 multiply_subtract_fusion.2
  376.7 4.5 fusion.5
  381.2 7.1 %all_gather.39 = bf16[192,768]{1,0:T(8,128)(2,1)S(1)} all-gather(bf16[48,768]{1,0:T(8,128)(2,1)} %reduce-scatter.8.cloned.1.call-done), channel_id=1, replica_groups=mesh['dp'=8,'seq'=4] {'seq'}, dimensions={0}, use_global_device_ids=true | all-gather | bytes 368640 | tf_op jit(solution)/shard_map/all_gather | solution.py:672
  388.3 82.0 %reduce-scatter.6.cloned.1.call-done = bf16[24,1536]{1,0:T(8,128)(2,1)} async-done(((bf16[768,1536]{1,0:T(8,128)(2,1)}), bf16[24,1536]{1,0:T(8,128)(2,1)}) %reduce-scatter.6.cloned.1.call-update) | async-done | bytes 73744 | tf_op jit(solution)/shard_map/reduce_scatter | solution.py:589
  470.3 6.1 %all_gather.37 = bf16[96,1536]{1,0:T(8,128)(2,1)S(1)} all-gather(bf16[24,1536]{1,0:T(8,128)(2,1)} %reduce-scatter.6.cloned.1.call-done), channel_id=1, replica_groups=mesh['dp'=8,'seq'=4] {'seq'}, dimensions={0}, use_global_device_ids=true | all-gather | bytes 368640 | tf_op jit(solution)/shard_map/all_gather | solution.py:672
  476.4 2.9 multiply_subtract_fusion.1
  479.3 89.5 %reduce-scatter.10.cloned.1.call-done = bf16[24,1920]{1,0:T(8,128)(2,1)} async-done(((bf16[768,1920]{1,0:T(8,128)(2,1)}), bf16[24,1920]{1,0:T(8,128)(2,1)}) %reduce-scatter.10.cloned.1.call-update) | async-done | bytes 92176
  568.7 6.5 %all_gather.38 = bf16[96,1920]{1,0:T(8,128)(2,1)S(1)} all-gather(bf16[24,1920]{1,0:T(8,128)(2,1)} %reduce-scatter.10.cloned.1.call-done), channel_id=1, replica_groups=mesh['dp'=8,'seq'=4] {'seq'}, dimensions={0}, use_global_device_ids=true | all-gather | bytes 460800 | tf_op jit(solution)/shard_map/all_gather | solution.py:672
  575.2 3.9 multiply_subtract_fusion
  (60 shorter events, 0.6 us)
Async XLA Ops:
  7.2 10.4 %copy-start = (bf16[1,1024,768]{2,1,0:T(8,128)(2,1)S(1)}, bf16[1,1024,768]{2,1,0:T(8,128)(2,1)}, u32[]{:S(2)}) copy-start(bf16[1,1024,768]{2,1,0:T(8,128)(2,1)} %param.11) | copy-start | bytes 4718596
  7.2 10.3 %copy-start.5 = (f32[11336]{0:T(1024)S(1)}, f32[11336]{0:T(1024)}, u32[]{:S(2)}) copy-start(f32[11336]{0:T(1024)} %param.19) | copy-start | bytes 136036
  7.2 65.8 %all-gather.8.cloned.1.call-start = ((), (), s32[]{:S(2)}) async-start(), calls=%async_computation.3 | async-start | bytes 3041280 | tf_op jit(solution)/shard_map/all_gather | solution.py:457
  9.0 123.5 %all-gather.10.cloned.1.call-start = ((), (), s32[]{:S(2)}) async-start(), calls=%async_computation.4 | async-start | bytes 2433024 | tf_op jit(solution)/shard_map/all_gather | solution.py:458
  9.8 182.5 %all-gather.12.cloned.1.call-start = ((), (), s32[]{:S(2)}) async-start(), calls=%async_computation.5 | async-start | bytes 2433024 | tf_op jit(solution)/shard_map/all_gather | solution.py:459
  11.4 202.5 %all-gather.14.cloned.1.call-start = ((), (), s32[]{:S(2)}) async-start(), calls=%async_computation.8 | async-start | bytes 2211840 | tf_op jit(solution)/shard_map/all_gather | solution.py:514
  12.2 8.2 %collective-permute-start = (bf16[16,768]{1,0:T(8,128)(2,1)S(1)}, bf16[16,768]{1,0:T(8,128)(2,1)S(1)}, u32[]{:S(2)}, u32[]{:S(2)}) collective-permute-start(bf16[16,768]{1,0:T(8,128)(2,1)S(1)} %slice_bitcast_fusion.1), channel_id=1, source_target_pairs={{0,1},{1,2},{2,3},{4,5},{5,6},{6,7},{8,9},{9,10},{10,11},{12,13},{... | collective-permute-start | bytes 73736 | tf_op jit(solution)/shard_map/ppermute | solution.py:463
  103.9 162.8 %all-gather.16.cloned.1.call-start = ((), (), s32[]{:S(2)}) async-start(), calls=%async_computation.9 | async-start | bytes 1966080 | tf_op jit(solution)/shard_map/all_gather | solution.py:571
  213.9 28.4 %copy-start.2 = (bf16[1,1024,768]{2,1,0:T(8,128)(2,1)S(1)}, bf16[1,1024,768]{2,1,0:T(8,128)(2,1)}, u32[]{:S(2)}) copy-start(bf16[1,1024,768]{2,1,0:T(8,128)(2,1)} %param.12) | copy-start | bytes 4718596
  242.1 139.1 %reduce-scatter.8.cloned.1.call-start = ((), (), s32[]{:S(2)}) async-start(), calls=%async_computation.7 | async-start | bytes 2433024 | tf_op jit(solution)/shard_map/reduce_scatter | solution.py:589
  242.3 6.5 %copy-start.1 = (bf16[1,1024,768]{2,1,0:T(8,128)(2,1)S(1)}, bf16[1,1024,768]{2,1,0:T(8,128)(2,1)}, u32[]{:S(2)}) copy-start(bf16[1,1024,768]{2,1,0:T(8,128)(2,1)} %param.11) | copy-start | bytes 4718596
  248.5 221.8 %reduce-scatter.6.cloned.1.call-start = ((), (), s32[]{:S(2)}) async-start(), calls=%async_computation.6 | async-start | bytes 2433024 | tf_op jit(solution)/shard_map/reduce_scatter | solution.py:589
  255.0 1.1 copy-start.6
  255.1 313.7 %reduce-scatter.10.cloned.1.call-start = ((), (), s32[]{:S(2)}) async-start(), calls=%async_computation.10 | async-start | bytes 3041280
  307.1 3.6 collective-permute-start.1
  319.3 3.0 copy-start.9
  322.4 6.7 %copy-start.10 = (bf16[1024,1536]{1,0:T(8,128)(2,1)S(1)}, bf16[1024,1536]{1,0:T(8,128)(2,1)}, u32[]{:S(2)}) copy-start(bf16[1024,1536]{1,0:T(8,128)(2,1)} %get-tuple-element.46) | copy-start | bytes 9437188
  322.4 6.7 %copy-start.11 = (bf16[768,1536]{1,0:T(8,128)(2,1)S(1)}, bf16[768,1536]{1,0:T(8,128)(2,1)}, u32[]{:S(2)}) copy-start(bf16[768,1536]{1,0:T(8,128)(2,1)} %all-gather.10.cloned.1.call-done) | copy-start | bytes 7077892
  329.1 46.9 %copy-start.7 = (f32[11336]{0:T(1024)S(1)}, f32[11336]{0:T(1024)}, u32[]{:S(2)}) copy-start(f32[11336]{0:T(1024)} %param.20) | copy-start | bytes 136036
  329.1 46.9 %copy-start.8 = (f32[11336]{0:T(1024)S(1)}, f32[11336]{0:T(1024)}, u32[]{:S(2)}) copy-start(f32[11336]{0:T(1024)} %param.21) | copy-start | bytes 136036
  381.2 194.0 %copy-start.3 = (f32[96,3352]{1,0:T(8,128)S(1)}, f32[96,3352]{1,0:T(8,128)}, u32[]{:S(2)}) copy-start(f32[96,3352]{1,0:T(8,128)} %param.13) | copy-start | bytes 3861508
  381.2 194.0 %copy-start.4 = (f32[96,3352]{1,0:T(8,128)S(1)}, f32[96,3352]{1,0:T(8,128)}, u32[]{:S(2)}) copy-start(f32[96,3352]{1,0:T(8,128)} %param.14) | copy-start | bytes 3861508
Sparse Core Ops, SparseCore 0:
  11.4 61.5 all-gather.7
  76.5 56.0 all-gather.9
  136.0 56.1 all-gather.11
  194.2 19.6 all-gather.13
  242.2 19.6 all-gather.15
  267.1 99.0 reduce-scatter.7
  372.3 97.9 reduce-scatter.5
  475.7 92.9 reduce-scatter.9

commit v2 on v1

--- a/solution.py
+++ b/solution.py
@@ -363,6 +363,50 @@
     gstate[...] = grad_state * decay + ust[0]
 
 
+def swap(v, axis, bit):
+    size = lax.axis_size(axis)
+    return lax.ppermute(v, axis, [(i, i ^ (1 << bit)) for i in range(size)])
+
+
+def mesh_bits():
+    found = []
+    for axis in ("dp", "seq"):
+        for bit in reversed(range(lax.axis_size(axis).bit_length() - 1)):
+            found.append((axis, bit))
+    return found
+
+
+def mine(axis, bit):
+    return (lax.axis_index(axis) >> bit) & 1
+
+
+def gather_pairs(v, bits):
+    dims = v.shape
+    for place, (axis, bit) in enumerate(bits):
+        other = swap(v, axis, bit)
+        second = mine(axis, bit) == 1
+        v = jnp.stack([jnp.where(second, other, v), jnp.where(second, v, other)], axis=place)
+    return v.reshape((dims[0] << len(bits),) + dims[1:])
+
+
+def scatter_pairs(v, bits):
+    width = v.shape[1]
+    v = v.reshape((2,) * len(bits) + (v.shape[0] >> len(bits), width))
+    for place in reversed(range(len(bits))):
+        axis, bit = bits[place]
+        own = mine(axis, bit)
+        keep = lax.dynamic_index_in_dim(v, own, place, keepdims=False)
+        give = lax.dynamic_index_in_dim(v, 1 - own, place, keepdims=False)
+        v = (keep.astype(f32) + swap(give, axis, bit).astype(f32)).astype(v.dtype)
+    return v
+
+
+def sum_pairs(v, bits):
+    for axis, bit in bits:
+        v = v + swap(v, axis, bit)
+    return v
+
+
 def full(shape):
     return pl.BlockSpec(shape, lambda c: (0,) * len(shape))
 
@@ -437,7 +481,8 @@
     channel_second,
 ):
     groups = lax.axis_size("seq")
-    everyone = ("dp", "seq")
+    bits = mesh_bits()
+    seq_bits = [(axis, bit) for axis, bit in bits if axis == "seq"]
     seq_rank = lax.axis_index("seq")
     rank = seq_rank.astype(jnp.int32).reshape(1)
     pre_gain, norm_gain, conv_weight, conv_bias, step_bias, rate_log, skip_gain = unpack_channels(
@@ -454,9 +499,9 @@
 
     in_part = quarter(in_weight)
     side_part = jnp.pad(in_part[:, INNER:], ((0, 0), (0, SIDE + INNER - PROJ)))
-    full_side = lax.all_gather(side_part, everyone, axis=0, tiled=True)
-    full_gate = lax.all_gather(in_part[:, :INNER], everyone, axis=0, tiled=True)
-    full_out = lax.all_gather(quarter(out_weight), everyone, axis=0, tiled=True)
+    full_side = gather_pairs(side_part, bits)
+    full_gate = gather_pairs(in_part[:, :INNER], bits)
+    full_out = gather_pairs(quarter(out_weight), bits)
 
     forward = [(s, s + 1) for s in range(groups - 1)]
     backward = [(s + 1, s) for s in range(groups - 1)]
@@ -586,7 +631,7 @@
 
     def summed(left, right):
         product = lax.dot_general(left, right, TN, preferred_element_type=f32).astype(bf16)
-        return lax.psum_scatter(product, everyone, scatter_dimension=0, tiled=True)
+        return scatter_pairs(product, bits)
 
     out_scattered = summed(hidden, cot_low)
     gate_scattered = summed(normed_low, dgate)
@@ -666,10 +711,10 @@
             jnp.sum(skip.reshape(8, HEADS, HEADDIM), axis=(0, 2)),
         ]
     )
-    chan_grad = lax.psum(chan_grad, everyone)
+    chan_grad = sum_pairs(chan_grad, bits)
 
     def owned(part):
-        return lax.all_gather(part, "seq", axis=0, tiled=True).astype(f32)
+        return gather_pairs(part, seq_bits).astype(f32)
 
     out_grad = owned(out_scattered)
     in_grad = jnp.concatenate(

time: 588 us -> 380 us (0.65)
  waiting for transfers between devices: 318 us -> 95.7 us
  blocking collectives: 61.7 us -> 0 us
  starting transfers between devices: 4.37 us -> 46 us
  other arithmetic: 22.3 us -> 43.2 us
  Pallas kernels: 108 us -> 119 us
  matrix products: 46.5 us -> 37.7 us
  local copies, waits for them, and re-layouts: 11 us -> 19 us
    all_gather x3 -> x0, waiting for transfers between devices: 124 us -> none  [the longest x1 52.5 us: local(): full_side = lax.all_gather(side_part, everyone, axis=0, tiled=True)]
    ppermute x0 -> x41, waiting for transfers between devices: none -> 94.5 us  [swap(): return lax.ppermute(v, axis, [(i, i ^ 1 << bit) for i in range(size)])]
    unnamed x9 -> x2, waiting for transfers between devices: 89.6 us -> 0.03 us
    reduce_scatter x2 -> x0, waiting for transfers between devices: 82 us -> none  [summed(): return lax.psum_scatter(product, everyone, scatter_dimension=0, tiled=True)]
    ppermute x0 -> x41, starting transfers between devices: none -> 42.3 us  [swap(): return lax.ppermute(v, axis, [(i, i ^ 1 << bit) for i in range(size)])]
    psum x1 -> x0, blocking collectives: 42.1 us -> none  [local(): chan_grad = lax.psum(chan_grad, everyone)]
    all_gather x1, waiting for transfers between devices: 21.7 us -> 0.01 us  [local(): states = lax.all_gather(send, 'seq', axis=0, tiled=False)]
    all_gather x3 -> x0, blocking collectives: 19.6 us -> none  [owned(): return lax.all_gather(part, 'seq', axis=0, tiled=True).astype(f32)]
  transfers between devices with their start and end apart: 10 -> 45, of which waited for: 6 -> 20; matrix products, arithmetic and copies ran while one was open for 12% -> 24% of each run, Pallas kernels for 14% -> 25%
where the time goes in v2:
time: 380 us; the launch traced here: 376 us
  Pallas kernels  119 us (31%)
  waiting for transfers between devices  95.7 us (25%)
  starting transfers between devices  46 us (12%)
  other arithmetic  43.2 us (11%)
  matrix products  37.7 us (10%)
  local copies, waits for them, and re-layouts  19 us (5%)
  between operations  15.2 us (4%)
    ppermute x41, waiting for transfers between devices, swap(): return lax.ppermute(v, axis, [(i, i ^ 1 << bit) for i in range(size)])  94.5 us
    pallas_call x1, Pallas kernels, local(): pl.pallas_call(back_call, grid=(chunks,), in_specs=[smem, back(INNER), ba...  51.4 us
    ppermute x41, starting transfers between devices, swap(): return lax.ppermute(v, axis, [(i, i ^ 1 << bit) for i in range(size)])  42.3 us
    pallas_call x1, Pallas kernels, local(): pl.pallas_call(gate_call, grid=(chunks,), in_specs=[smem, by_chunk(INNER)...  26.1 us
    pallas_call x1, Pallas kernels, local(): pl.pallas_call(conv_state_kernel, grid=(chunks,), in_specs=[by_chunk(SIDE...  21 us
    dot_general x3, matrix products, summed(): lax.dot_general(left, right, TN, preferred_element_type=f32).astype(bf16)  14 us
    another operation x41, other arithmetic, gather_pairs(): jnp.stack([jnp.where(second, other, v), jnp.where(second, v, other)], axi...  12.7 us
    dot_general x3, matrix products, dot(): return jnp.dot(a, b, preferred_element_type=f32)  10.9 us
  transfers between devices with their start and end apart: 45, of which 20 were waited for; matrix products, arithmetic and copies ran while one was open for 24% of the time, Pallas kernels for 25%

profile of v2, /device:TPU:0, one launch (start us, length us, event | category | flops | bytes accessed | tf_op | source)
XLA Modules:
  0.0 375.6 jit_solution(2507747964982487632)
XLA Ops:
  8.0 2.3 collective-permute-start.5
  11.3 3.5 collective-permute-start.11
  15.9 3.0 collective-permute-start
  18.8 1.8 fusion.6
  26.9 1.6 collective-permute-start.12
  29.1 1.6 collective-permute-start.1
  30.8 2.9 collective-permute-done.12
  33.7 1.6 collective-permute-start.13
  35.3 5.5 %collective-permute-done.1 = bf16[2,24,1920]{2,1,0:T(8,128)(2,1)S(1)} collective-permute-done((bf16[2,24,1920]{2,1,0:T(8,128)(2,1)S(1)}, bf16[2,24,1920]{2,1,0:T(8,128)(2,1)S(1)}, u32[]{:S(2)}, u32[]{:S(2)}) %collective-permute-start.1) | collective-permute-done | bytes 184352 | tf_op jit(solution)/shard_map/ppermute | solution.py:368
  40.9 1.6 collective-permute-start.2
  43.1 9.3 %collective-permute-done.2 = bf16[2,2,24,1920]{3,2,1,0:T(8,128)(2,1)S(1)} collective-permute-done((bf16[2,2,24,1920]{3,2,1,0:T(8,128)(2,1)S(1)}, bf16[2,2,24,1920]{3,2,1,0:T(8,128)(2,1)S(1)}, u32[]{:S(2)}, u32[]{:S(2)}) %collective-permute-start.2) | collective-permute-done | bytes 368672 | tf_op jit(solution)/shard_map/ppermute | solution.py:368
  52.8 2.1 collective-permute-start.14
  54.8 3.0 collective-permute-done.8
  57.9 14.1 %collective-permute-done.3 = bf16[2,2,2,24,1920]{4,3,2,1,0:T(8,128)(2,1)S(1)} collective-permute-done((bf16[2,2,2,24,1920]{4,3,2,1,0:T(8,128)(2,1)S(1)}, bf16[2,2,2,24,1920]{4,3,2,1,0:T(8,128)(2,1)S(1)}, u32[]{:S(2)}, u32[]{:S(2)}) %collective-permute-start.3) | collective-permute-done | bytes 737312 | tf_op jit(solution)/shard_map/ppermute | solution.py:368
  72.6 12.1 %collective-permute-done.14 = bf16[2,2,2,48,768]{4,3,0,1,2:T(8,128)(2,1)S(1)} collective-permute-done((bf16[2,2,2,48,768]{4,3,0,1,2:T(8,128)(2,1)S(1)}, bf16[2,2,2,48,768]{4,3,0,1,2:T(8,128)(2,1)S(1)}, u32[]{:S(2)}, u32[]{:S(2)}) %collective-permute-start.14) | collective-permute-done | bytes 589856 | tf_op jit(solution)/shard_map/ppermute | solution.py:368
  85.9 8.8 %collective-permute-done.9 = bf16[2,2,2,24,1536]{4,3,0,1,2:T(8,128)(2,1)S(1)} collective-permute-done((bf16[2,2,2,24,1536]{4,3,0,1,2:T(8,128)(2,1)S(1)}, bf16[2,2,2,24,1536]{4,3,0,1,2:T(8,128)(2,1)S(1)}, u32[]{:S(2)}, u32[]{:S(2)}) %collective-permute-start.9) | collective-permute-done | bytes 589856 | tf_op jit(solution)/shard_map/ppermute | solution.py:368
  96.7 1.4 copy-done
  98.1 5.2 %convolution_convert_fusion.1.proj.refs_17_.refs_18_ = bf16[1024,1920]{1,0:T(8,128)(2,1)} fusion(bf16[768,1920]{1,0:T(8,128)(2,1)S(1)} %bitcast.234, bf16[1,1024,768]{2,1,0:T(8,128)(2,1)S(1)} %copy-done, f32[768]{0:T(1024)S(1)} %slice.84, f32[1024]{0:T(1024)S(1)} %fusion.51), kind=kOutput, calls=%fused_computation.6 | convolution fusion | flops 3025010688 | bytes 8461312 | tf_op jit(solution)/shard_map/dot_general | solution.py:43
  104.5 21.0 %conv_state.1 = (bf16[1024,1536]{1,0:T(8,128)(2,1)}, bf16[1024,256]{1,0:T(8,128)(2,1)}, bf16[1024,1536]{1,0:T(8,128)(2,1)}, f32[1024,128]{1,0:T(8,128)}, f32[32,...) custom-call(bf16[1024,1920]{1,0:T(8,128)(2,1)} %convolution_convert_, ...), custom_call_target="tpu_custom_call" | custom-call | flops 1000000000 | bytes 25165824 | tf_op jit(solution)/shard_map/conv_state/pallas_call | solution.py:530
  126.6 1.4 select_bitcast_fusion.3
  128.3 1.7 copy.53
  130.0 1.5 select_bitcast_fusion.5
  132.0 4.5 %convolution_convert_fusion.refs_8_ = bf16[1024,1536]{1,0:T(8,128)(2,1)} fusion(bf16[768,1536]{1,0:T(8,128)(2,1)S(1)} %bitcast.241, bf16[1,1024,768]{2,1,0:T(8,128)(2,1)S(1)} %copy-done, f32[768]{0:T(1024)S(1)} %slice.84, f32[1024]{0:T(1024)S(1)} %fusion.51), kind=kOutput, calls=%fused_computation.5 | convolution fusion | flops 2420637696 | bytes 7085056 | tf_op jit(solution)/shard_map/dot_general | solution.py:43
  136.5 9.8 %within.1.refs_1_ = f32[1024,1536]{1,0:T(8,128)} custom-call(bf16[1024,1536]{1,0:T(8,128)(2,1)} %get-tuple-element.38.u.refs_4_, bf16[1024,256]{1,0:T(8,128)(2,1)} %get-tuple-element.39.bc.refs_3_.refs_6_, f32[1024,128]{1,0:T(8,128)} %get-tuple-element.40.cum.refs_4_.refs_9_, f32[32,1024]{1,0:T(8,128)} %get-tuple-element.41.cumt), custom_call_target="tpu_custom_call" | custom-call | flops 4000000000 | bytes 16777216 | tf_op jit(solution)/shard_map/within/pallas_call | solution.py:561
  146.3 26.1 %gate_norm.1 = (f32[1024,768]{1,0:T(8,128)}, bf16[1024,1536]{1,0:T(8,128)(2,1)}, f32[1024,1536]{1,0:T(8,128)}, bf16[1024,1536]{1,0:T(8,128)(2,1)}, bf16[1024,153...) custom-call(s32[1]{0:T(128)} %bitcast.refs_0_, ...), custom_call_target="tpu_custom_call" | custom-call | flops 8000000000 | bytes 50331648 | tf_op jit(solution)/shard_map/gate_norm/pallas_call | solution.py:583
  173.4 1.9 convert_element_type.268
  175.3 5.1 %convolution_convert_fusion.3 = bf16[768,1536]{1,0:T(8,128)(2,1)S(1)} fusion(bf16[1024,1536]{1,0:T(8,128)(2,1)} %get-tuple-element.46, f32[1024]{0:T(1024)S(1)} %fusion.51, f32[768]{0:T(1024)S(1)} %slice.84, bf16[1,1024,768]{2,1,0:T(8,128)(2,1)S(1)} %copy-done.1), kind=kOutput, calls=%fused_computation.10 | convolution fusion | flops 2420244480 | bytes 7085056 | tf_op jit(solution)/shard_map/dot_general | solution.py:633
  181.9 2.9 convolution_convert_fusion.2
  186.5 4.3 %fusion.61 = f32[1024,768]{1,0:T(8,128)} fusion(bf16[1024,1536]{1,0:T(8,128)(2,1)S(1)} %copy-done.29, bf16[768,1536]{1,0:T(8,128)(2,1)S(1)} %bitcast.242), kind=kOutput, calls=%fused_computation.196 | convolution fusion | flops 2415919104 | bytes 8650752 | tf_op jit(solution)/shard_map/dot_general | solution.py:696
  192.3 10.5 %within_back.1 = (f32[1024,1536]{1,0:T(8,128)}, f32[1024,256]{1,0:T(8,128)}) custom-call(bf16[1024,1536]{1,0:T(8,128)(2,1)} %get-tuple-element.38.u.refs_4_, bf16[1024,1536]{1,0:T(8,128)(2,1)} %get-tuple-element.47.dy.refs_2_, bf16[1024,256]{1,0:T(8,128)(2,1)} %get-tuple-element.39.bc.refs_3_.refs_6_, f32[1024,128]{1,0:T(8,128)} %get-tuple-element.40.cum.refs_4_.refs_9_, ...), custom_call_target="tpu_custom_call" | custom-call | flops 8000000000 | bytes 16777216 | tf_op jit(solution)/shard_map/within_back/pallas_call | solution.py:618
  202.7 1.6 fusion.11
  204.4 1.9 collective-permute-start.32
  206.2 2.2 collective-permute-done.18
  208.5 1.2 fusion.21
  209.7 1.6 collective-permute-start.19
  211.3 9.3 %collective-permute-done.32 = bf16[2,2,2,48,768]{4,3,2,1,0:T(8,128)(2,1)S(1)} collective-permute-done((bf16[2,2,2,48,768]{4,3,2,1,0:T(8,128)(2,1)S(1)}, bf16[2,2,2,48,768]{4,3,2,1,0:T(8,128)(2,1)S(1)}, u32[]{:S(2)}, u32[]{:S(2)}) %collective-permute-start.32) | collective-permute-done | bytes 589856 | tf_op jit(solution)/shard_map/ppermute | solution.py:368
  220.8 1.6 collective-permute-start.33
  222.5 1.7 collective-permute-start.20
  224.2 5.3 %collective-permute-done.33 = bf16[2,2,48,768]{3,2,1,0:T(8,128)(2,1)S(1)} collective-permute-done((bf16[2,2,48,768]{3,2,1,0:T(8,128)(2,1)S(1)}, bf16[2,2,48,768]{3,2,1,0:T(8,128)(2,1)S(1)}, u32[]{:S(2)}, u32[]{:S(2)}) %collective-permute-start.33) | collective-permute-done | bytes 294944 | tf_op jit(solution)/shard_map/ppermute | solution.py:368
  229.6 1.7 collective-permute-start.34
  231.9 3.7 collective-permute-done.34
  237.8 2.0 collective-permute-start.22
  239.8 51.4 %mixer_back.1 = (bf16[1024,1920]{1,0:T(8,128)(2,1)}, f32[8,1792]{1,0:T(8,128)}, f32[8,1792]{1,0:T(8,128)}, f32[40,1792]{1,0:T(8,128)}, f32[16,128]{1,0:T(8,128)}, /*index=5*/f32[8,1536]{1,0:T(8,128)}) custom-call(s32[1]{0:T(128)} %bitcast.refs_0_, f32[1024,1536]{1,0:T(8,128)} %get-tuple-element.48.refs_1_, bf16[1024,1536]{1,0:T(8,128)(2,1)} %get-tuple-element.47.dy.refs_2_, ...), custom_call_target="tpu_custom_call" | custom-call | flops 4000000000 | bytes 50331648 | tf_op jit(solution)/shard_map/mixer_back/pallas_call | solution.py:649
  291.2 1.3 collective-permute-start.16
  294.6 1.5 fusion.42
  296.1 6.0 %convolution_convert_fusion.4 = bf16[768,1920]{1,0:T(8,128)(2,1)S(1)} fusion(bf16[1024,1920]{1,0:T(8,128)(2,1)} %fusion.42, f32[1024]{0:T(1024)S(1)} %fusion.51, f32[768]{0:T(1024)S(1)} %slice.84, bf16[1,1024,768]{2,1,0:T(8,128)(2,1)S(1)} %copy-done.1), kind=kOutput, calls=%fused_computation.11 | convolution fusion | flops 3024519168 | bytes 8461312 | tf_op jit(solution)/shard_map/dot_general | solution.py:633
  302.1 1.3 dynamic-slice_bitcast_fusion
  309.7 1.3 copy.57
  310.9 1.7 reshape.203
  313.2 2.3 fusion.8
  317.7 8.6 %fusion.3 = (f32[768]{0:T(1024)S(1)}, f32[1024]{0:T(1024)S(1)}, f32[1024,768]{1,0:T(8,128)}) fusion(f32[1024]{0:T(1024)S(1)} %copy-done.27, bf16[1,1024,768]{2,1,0:T(8,128)(2,1)S(1)} %copy-done.1, f32[768]{0:T(1024)S(1)} %slice.84, f32[1024,768]{1,0:T(8,128)} %fusion.61, bf16[1024,1920]{1,0:T(8,128)(2,1)} %fusion.42, bf16[768,1920]{1,0:T(8,128)(2,1)S(1)} %bitcast.236), kind=kOutput, calls=%fused_computation.13 | convolution fusion | flops 3026188544 | bytes 14759936 | tf_op jit(solution)/shard_map/dot_general | solution.py:697
  327.0 1.9 collective-permute-start.38
  328.9 4.5 %fusion.5 = f32[1,1024,768]{2,1,0:T(8,128)} fusion(f32[1024,768]{1,0:T(8,128)} %get-tuple-element.126, f32[1024]{0:T(1024)S(1)} %multiply_multiply_fusion.3, f32[1024]{0:T(1024)S(1)} %copy-done.27, f32[768]{0:T(1024)S(1)} %slice.84, bf16[1,1024,768]{2,1,0:T(8,128)(2,1)S(1)} %copy-done.4, bf16[1,1024,768]{2,1,0:T(8,128)(2,1)S(1)} %copy-done.1), kind=kLoop, calls=%fused_computation.15 | loop fusion | flops 6291456 | bytes 9448448 | tf_op jit(solution)/shard_map/broadcast_in_dim | solution.py:700
  334.6 1.7 collective-permute-done.25
  336.4 1.3 fusion.17
  337.7 1.6 collective-permute-start.26
  340.2 7.3 %collective-permute-done.26 = bf16[2,2,24,1920]{3,2,1,0:T(8,128)(2,1)S(1)} collective-permute-done((bf16[2,2,24,1920]{3,2,1,0:T(8,128)(2,1)S(1)}, bf16[2,2,24,1920]{3,2,1,0:T(8,128)(2,1)S(1)}, u32[]{:S(2)}, u32[]{:S(2)}) %collective-permute-start.26) | collective-permute-done | bytes 368672 | tf_op jit(solution)/shard_map/ppermute | solution.py:368
  349.1 1.6 collective-permute-start.40
  350.7 2.6 collective-permute-done.27
  353.3 2.7 collective-permute-start.28
  356.0 1.5 multiply_subtract_fusion.1
  357.9 1.6 collective-permute-done.28
  361.8 2.3 collective-permute-done.29
  366.0 2.6 multiply_subtract_fusion
  (239 shorter events, 45.9 us)
Async XLA Ops:
  7.2 13.5 %copy-start.20 = (f32[11336]{0:T(1024)S(1)}, f32[11336]{0:T(1024)}, u32[]{:S(2)}) copy-start(f32[11336]{0:T(1024)} %param.19) | copy-start | bytes 136036
  7.2 139.1 %all-gather.5.cloned.1.call-start = ((), (), s32[]{:S(2)}) async-start(), calls=%async_computation | async-start | bytes 2211840 | tf_op jit(solution)/shard_map/all_gather | solution.py:559
  8.0 17.8 %collective-permute-start.5 = (bf16[16,768]{1,0:T(8,128)(2,1)S(1)}, bf16[16,768]{1,0:T(8,128)(2,1)S(1)}, u32[]{:S(2)}, u32[]{:S(2)}) collective-permute-start(bf16[16,768]{1,0:T(8,128)(2,1)S(1)} %slice_bitcast_fusion.1), channel_id=1, source_target_pairs={{0,1},{1,2},{2,3},{4,5},{5,6},{6,7},{8,9},{9,10},{10,11},{12,13},{... | collective-permute-start | bytes 73736 | tf_op jit(solution)/shard_map/ppermute | solution.py:508
  11.3 14.6 %collective-permute-start.11 = (bf16[48,768]{1,0:T(8,128)(2,1)S(1)}, bf16[48,768]{1,0:T(8,128)(2,1)S(1)}, u32[]{:S(2)}, u32[]{:S(2)}) collective-permute-start(bf16[48,768]{1,0:T(8,128)(2,1)S(1)} %dynamic-slice_convert_fusion.1), channel_id=1, source_target_pairs={{0,16},{4,20},{8,24},{12,28},{16,0},{20,4},{24,8},{28,12},{1,17},{... | collective-permute-start | bytes 221192 | tf_op jit(solution)/shard_map/ppermute | solution.py:368
  15.8 12.7 %collective-permute-start.6 = (bf16[24,1536]{1,0:T(8,128)(2,1)S(1)}, bf16[24,1536]{1,0:T(8,128)(2,1)S(1)}, u32[]{:S(2)}, u32[]{:S(2)}) collective-permute-start(bf16[24,1536]{1,0:T(8,128)(2,1)S(1)} %slice.109), channel_id=1, source_target_pairs={{0,16},{4,20},{8,24},{12,28},{16,0},{20,4},{24,8},{28,12},{1,17},{... | collective-permute-start | bytes 221192 | tf_op jit(solution)/shard_map/ppermute | solution.py:368
  15.9 13.2 %collective-permute-start = (bf16[24,1920]{1,0:T(8,128)(2,1)S(1)}, bf16[24,1920]{1,0:T(8,128)(2,1)S(1)}, u32[]{:S(2)}, u32[]{:S(2)}) collective-permute-start(bf16[24,1920]{1,0:T(8,128)(2,1)S(1)} %pad.11), channel_id=1, source_target_pairs={{0,16},{4,20},{8,24},{12,28},{16,0},{20,4},{24,8},{28,12},{1,17},{... | collective-permute-start | bytes 276488 | tf_op jit(solution)/shard_map/ppermute | solution.py:368
  21.3 274.8 %copy-start.26 = (f32[1024]{0:T(1024)}, f32[1024]{0:T(1024)S(1)}, u32[]{:S(2)}) copy-start(f32[1024]{0:T(1024)S(1)} %fusion.51) | copy-start | bytes 12292
  23.7 10.0 %copy-start.18 = (f32[1792,4]{0,1:T(4,128)}, f32[1792,4]{0,1:T(4,128)S(1)}, u32[]{:S(2)}) copy-start(f32[1792,4]{0,1:T(4,128)S(1)} %copy.51) | copy-start | bytes 86020
  25.8 15.1 %copy-start.22 = (bf16[16,768]{1,0:T(8,128)(2,1)}, bf16[16,768]{1,0:T(8,128)(2,1)S(1)}, u32[]{:S(2)}) copy-start(bf16[16,768]{1,0:T(8,128)(2,1)S(1)} %collective-permute-done.5) | copy-start | bytes 73732
  26.9 6.8 %collective-permute-start.12 = (bf16[2,48,768]{2,1,0:T(8,128)(2,1)S(1)}, bf16[2,48,768]{2,1,0:T(8,128)(2,1)S(1)}, u32[]{:S(2)}, u32[]{:S(2)}) collective-permute-start(bf16[2,48,768]{2,1,0:T(8,128)(2,1)S(1)} %pad_maximum_fusion.18), channel_id=1, source_target_pairs={{0,8},{4,12},{8,0},{12,4},{16,24},{20,28},{24,16},{28,20},{1,9},{5... | collective-permute-start | bytes 442376 | tf_op jit(solution)/shard_map/ppermute | solution.py:368
  28.5 13.9 %collective-permute-start.7 = (bf16[2,24,1536]{2,1,0:T(8,128)(2,1)S(1)}, bf16[2,24,1536]{2,1,0:T(8,128)(2,1)S(1)}, u32[]{:S(2)}, u32[]{:S(2)}) collective-permute-start(bf16[2,24,1536]{2,1,0:T(8,128)(2,1)S(1)} %pad_maximum_fusion.17), channel_id=1, source_target_pairs={{0,8},{4,12},{8,0},{12,4},{16,24},{20,28},{24,16},{28,20},{1,9},{5... | collective-permute-start | bytes 442376 | tf_op jit(solution)/shard_map/ppermute | solution.py:368
  29.1 11.6 %collective-permute-start.1 = (bf16[2,24,1920]{2,1,0:T(8,128)(2,1)S(1)}, bf16[2,24,1920]{2,1,0:T(8,128)(2,1)S(1)}, u32[]{:S(2)}, u32[]{:S(2)}) collective-permute-start(bf16[2,24,1920]{2,1,0:T(8,128)(2,1)S(1)} %pad_maximum_fusion.15), channel_id=1, source_target_pairs={{0,8},{4,12},{8,0},{12,4},{16,24},{20,28},{24,16},{28,20},{1,9},{5... | collective-permute-start | bytes 552968 | tf_op jit(solution)/shard_map/ppermute | solution.py:368
  33.7 18.9 %collective-permute-start.13 = (bf16[2,2,48,768]{3,2,0,1:T(8,128)(2,1)S(1)}, bf16[2,2,48,768]{3,2,0,1:T(8,128)(2,1)S(1)}, u32[]{:S(2)}, u32[]{:S(2)}) collective-permute-start(bf16[2,2,48,768]{3,2,0,1:T(8,128)(2,1)S(1)} %pad_maximum_fusion.13), channel_id=1, source_target_pairs={{0,4},{4,0},{8,12},{12,8},{16,20},{20,16},{24,28},{28,24},{1,5},{5... | collective-permute-start | bytes 884744 | tf_op jit(solution)/shard_map/ppermute | solution.py:368
  40.9 11.5 %collective-permute-start.2 = (bf16[2,2,24,1920]{3,2,1,0:T(8,128)(2,1)S(1)}, bf16[2,2,24,1920]{3,2,1,0:T(8,128)(2,1)S(1)}, u32[]{:S(2)}, u32[]{:S(2)}) collective-permute-start(bf16[2,2,24,1920]{3,2,1,0:T(8,128)(2,1)S(1)} %pad_maximum_fusion.10), channel_id=1, source_target_pairs={{0,4},{4,0},{8,12},{12,8},{16,20},{20,16},{24,28},{28,24},{1,5},{5... | collective-permute-start | bytes 1105928 | tf_op jit(solution)/shard_map/ppermute | solution.py:368
  42.5 15.4 %collective-permute-start.8 = (bf16[2,2,24,1536]{3,2,0,1:T(8,128)(2,1)S(1)}, bf16[2,2,24,1536]{3,2,0,1:T(8,128)(2,1)S(1)}, u32[]{:S(2)}, u32[]{:S(2)}) collective-permute-start(bf16[2,2,24,1536]{3,2,0,1:T(8,128)(2,1)S(1)} %pad_maximum_fusion.12), channel_id=1, source_target_pairs={{0,4},{4,0},{8,12},{12,8},{16,20},{20,16},{24,28},{28,24},{1,5},{5... | collective-permute-start | bytes 884744 | tf_op jit(solution)/shard_map/ppermute | solution.py:368
  52.5 19.5 %collective-permute-start.3 = (bf16[2,2,2,24,1920]{4,3,2,1,0:T(8,128)(2,1)S(1)}, bf16[2,2,2,24,1920]{4,3,2,1,0:T(8,128)(2,1)S(1)}, u32[]{:S(2)}, u32[]{:S(2)}) collective-permute-start(bf16[2,2,2,24,1920]{4,3,2,1,0:T(8,128)(2,1)S(1)} %pad_maximum_fusion.6), channel_id=1, source_target_pairs={{0,2},{1,3},{2,0},{3,1},{4,6},{5,7},{6,4},{7,5},{8,10},{9,11},{10,... | collective-permute-start | bytes 2211848 | tf_op jit(solution)/shard_map/ppermute | solution.py:368
  52.8 31.9 %collective-permute-start.14 = (bf16[2,2,2,48,768]{4,3,0,1,2:T(8,128)(2,1)S(1)}, bf16[2,2,2,48,768]{4,3,0,1,2:T(8,128)(2,1)S(1)}, u32[]{:S(2)}, u32[]{:S(2)}) collective-permute-start(bf16[2,2,2,48,768]{4,3,0,1,2:T(8,128)(2,1)S(1)} %pad_maximum_fusion.9), channel_id=1, source_target_pairs={{0,2},{1,3},{2,0},{3,1},{4,6},{5,7},{6,4},{7,5},{8,10},{9,11},{10,... | collective-permute-start | bytes 1769480 | tf_op jit(solution)/shard_map/ppermute | solution.py:368
  72.4 23.7 %collective-permute-start.4 = (bf16[2,2,2,2,24,1920]{5,4,3,2,1,0:T(8,128)(2,1)S(1)}, bf16[2,2,2,2,24,1920]{5,4,3,2,1,0:T(8,128)(2,1)S(1)}, u32[]{:S(2)}, u32[]{:S(2)}) collective-permute-start(bf16[2,2,2,2,24,1920]{5,4,3,2,1,0:T(8,128)(2,1)S(1)} %pad_maximum_fusion.3), channel_id=1, source_target_pairs={{0,1},{1,0},{2,3},{3,2},{4,5},{5,4},{6,7},{7,6},{8,9},{9,8},{10,11... | collective-permute-start | bytes 4423688 | tf_op jit(solution)/shard_map/ppermute | solution.py:368
  72.5 22.2 %collective-permute-start.9 = (bf16[2,2,2,24,1536]{4,3,0,1,2:T(8,128)(2,1)S(1)}, bf16[2,2,2,24,1536]{4,3,0,1,2:T(8,128)(2,1)S(1)}, u32[]{:S(2)}, u32[]{:S(2)}) collective-permute-start(bf16[2,2,2,24,1536]{4,3,0,1,2:T(8,128)(2,1)S(1)} %pad_maximum_fusion.8), channel_id=1, source_target_pairs={{0,2},{1,3},{2,0},{3,1},{4,6},{5,7},{6,4},{7,5},{8,10},{9,11},{10,... | collective-permute-start | bytes 1769480 | tf_op jit(solution)/shard_map/ppermute | solution.py:368
  85.9 40.7 %collective-permute-start.15 = (bf16[2,2,2,2,48,768]{5,4,0,1,2,3:T(8,128)(2,1)}, bf16[2,2,2,2,48,768]{5,4,0,1,2,3:T(8,128)(2,1)}, u32[]{:S(2)}, u32[]{:S(2)}) collective-permute-start(bf16[2,2,2,2,48,768]{5,4,0,1,2,3:T(8,128)(2,1)} %pad_maximum_fusion.5), channel_id=1, source_target_pairs={{0,1},{1,0},{2,3},{3,2},{4,5},{5,4},{6,7},{7,6},{8,9},{9,8},{10,11... | collective-permute-start | bytes 3538952 | tf_op jit(solution)/shard_map/ppermute | solution.py:368
  96.0 34.0 %collective-permute-start.10 = (bf16[2,2,2,2,24,1536]{5,4,0,1,2,3:T(8,128)(2,1)}, bf16[2,2,2,2,24,1536]{5,4,0,1,2,3:T(8,128)(2,1)}, u32[]{:S(2)}, u32[]{:S(2)}) collective-permute-start(bf16[2,2,2,2,24,1536]{5,4,0,1,2,3:T(8,128)(2,1)} %pad_maximum_fusion.4), channel_id=1, source_target_pairs={{0,1},{1,0},{2,3},{3,2},{4,5},{5,4},{6,7},{7,6},{8,9},{9,8},{10,11... | collective-permute-start | bytes 3538952 | tf_op jit(solution)/shard_map/ppermute | solution.py:368
  96.6 6.7 %copy-start.2 = (bf16[2,2,2,2,2,24,1920]{6,5,4,3,2,1,0:T(8,128)(2,1)}, bf16[2,2,2,2,2,24,1920]{6,5,4,3,2,1,0:T(8,128)(2,1)S(1)}, u32[]{:S(2)}) copy-start(bf16[2,2,2,2,2,24,1920]{6,5,4,3,2,1,0:T(8,128)(2,1)S(1)} %pad_maximum_fusion) | copy-start | bytes 8847364
  98.1 5.2 %copy-start.23 = (bf16[16,768]{1,0:T(8,128)(2,1)S(1)}, bf16[16,768]{1,0:T(8,128)(2,1)}, u32[]{:S(2)}) copy-start(bf16[16,768]{1,0:T(8,128)(2,1)} %copy-done.22) | copy-start | bytes 73732
  125.5 114.3 %all-gather.7.cloned.1.call-start = ((), (), s32[]{:S(2)}) async-start(), calls=%async_computation.1 | async-start | bytes 1966080 | tf_op jit(solution)/shard_map/all_gather | solution.py:616
  132.0 4.5 %copy-start.10 = (bf16[2,2,2,2,2,24,1536]{6,5,4,3,2,1,0:T(8,128)(2,1)}, bf16[2,2,2,2,2,24,1536]{6,5,4,3,2,1,0:T(8,128)(2,1)S(1)}, u32[]{:S(2)}) copy-start(bf16[2,2,2,2,2,24,1536]{6,5,4,3,2,1,0:T(8,128)(2,1)S(1)} %copy.52) | copy-start | bytes 7077892
  175.3 5.8 %copy-start.30 = (bf16[1024,1536]{1,0:T(8,128)(2,1)S(1)}, bf16[1024,1536]{1,0:T(8,128)(2,1)}, u32[]{:S(2)}) copy-start(bf16[1024,1536]{1,0:T(8,128)(2,1)} %get-tuple-element.60) | copy-start | bytes 9437188
  180.5 10.3 %collective-permute-start.17 = (bf16[2,2,2,2,24,1536]{5,4,3,2,1,0:T(8,128)(2,1)S(1)}, bf16[2,2,2,2,24,1536]{5,4,3,2,1,0:T(8,128)(2,1)S(1)}, u32[]{:S(2)}, u32[]{:S(2)}) collective-permute-start(bf16[2,2,2,2,24,1536]{5,4,3,2,1,0:T(8,128)(2,1)S(1)} %dynamic-slice_bitcast_fusion.2), channel_id=1, source_target_pairs={{0,1},{1,0},{2,3},{3,2},{4,5},{5,4},{6,7},{7,6},{8,9},{9,8},{10,11... | collective-permute-start | bytes 3538952 | tf_op jit(solution)/shard_map/ppermute | solution.py:368
  184.9 17.8 %collective-permute-start.31 = (bf16[2,2,2,2,48,768]{5,4,3,2,1,0:T(8,128)(2,1)S(1)}, bf16[2,2,2,2,48,768]{5,4,3,2,1,0:T(8,128)(2,1)}, u32[]{:S(2)}, u32[]{:S(2)}) collective-permute-start(bf16[2,2,2,2,48,768]{5,4,3,2,1,0:T(8,128)(2,1)S(1)} %dynamic-slice_bitcast_fusion.1), channel_id=1, source_target_pairs={{0,1},{1,0},{2,3},{3,2},{4,5},{5,4},{6,7},{7,6},{8,9},{9,8},{10,11... | collective-permute-start | bytes 3538952 | tf_op jit(solution)/shard_map/ppermute | solution.py:368
  192.0 16.4 %collective-permute-start.18 = (bf16[2,2,2,24,1536]{4,3,2,1,0:T(8,128)(2,1)}, bf16[2,2,2,24,1536]{4,3,2,1,0:T(8,128)(2,1)}, u32[]{:S(2)}, u32[]{:S(2)}) collective-permute-start(bf16[2,2,2,24,1536]{4,3,2,1,0:T(8,128)(2,1)} %dynamic-slice_bitcast_fusion.5), channel_id=1, source_target_pairs={{0,2},{1,3},{2,0},{3,1},{4,6},{5,7},{6,4},{7,5},{8,10},{9,11},{10,... | collective-permute-start | bytes 1769480 | tf_op jit(solution)/shard_map/ppermute | solution.py:368
  204.4 16.3 %collective-permute-start.32 = (bf16[2,2,2,48,768]{4,3,2,1,0:T(8,128)(2,1)S(1)}, bf16[2,2,2,48,768]{4,3,2,1,0:T(8,128)(2,1)S(1)}, u32[]{:S(2)}, u32[]{:S(2)}) collective-permute-start(bf16[2,2,2,48,768]{4,3,2,1,0:T(8,128)(2,1)S(1)} %dynamic-slice_bitcast_fusion.4), channel_id=1, source_target_pairs={{0,2},{1,3},{2,0},{3,1},{4,6},{5,7},{6,4},{7,5},{8,10},{9,11},{10,... | collective-permute-start | bytes 1769480 | tf_op jit(solution)/shard_map/ppermute | solution.py:368
  209.7 12.7 %collective-permute-start.19 = (bf16[2,2,24,1536]{3,2,1,0:T(8,128)(2,1)S(1)}, bf16[2,2,24,1536]{3,2,1,0:T(8,128)(2,1)S(1)}, u32[]{:S(2)}, u32[]{:S(2)}) collective-permute-start(bf16[2,2,24,1536]{3,2,1,0:T(8,128)(2,1)S(1)} %dynamic-slice_bitcast_fusion.8), channel_id=1, source_target_pairs={{0,4},{4,0},{8,12},{12,8},{16,20},{20,16},{24,28},{28,24},{1,5},{5... | collective-permute-start | bytes 884744 | tf_op jit(solution)/shard_map/ppermute | solution.py:368
  220.8 8.7 %collective-permute-start.33 = (bf16[2,2,48,768]{3,2,1,0:T(8,128)(2,1)S(1)}, bf16[2,2,48,768]{3,2,1,0:T(8,128)(2,1)S(1)}, u32[]{:S(2)}, u32[]{:S(2)}) collective-permute-start(bf16[2,2,48,768]{3,2,1,0:T(8,128)(2,1)S(1)} %dynamic-slice_bitcast_fusion.7), channel_id=1, source_target_pairs={{0,4},{4,0},{8,12},{12,8},{16,20},{20,16},{24,28},{28,24},{1,5},{5... | collective-permute-start | bytes 884744 | tf_op jit(solution)/shard_map/ppermute | solution.py:368
  222.5 8.9 %collective-permute-start.20 = (bf16[2,24,1536]{2,1,0:T(8,128)(2,1)S(1)}, bf16[2,24,1536]{2,1,0:T(8,128)(2,1)S(1)}, u32[]{:S(2)}, u32[]{:S(2)}) collective-permute-start(bf16[2,24,1536]{2,1,0:T(8,128)(2,1)S(1)} %dynamic-slice_bitcast_fusion.11), channel_id=1, source_target_pairs={{0,8},{4,12},{8,0},{12,4},{16,24},{20,28},{24,16},{28,20},{1,9},{5... | collective-permute-start | bytes 442376 | tf_op jit(solution)/shard_map/ppermute | solution.py:368
  229.6 6.0 %collective-permute-start.34 = (bf16[2,48,768]{2,1,0:T(8,128)(2,1)S(1)}, bf16[2,48,768]{2,1,0:T(8,128)(2,1)S(1)}, u32[]{:S(2)}, u32[]{:S(2)}) collective-permute-start(bf16[2,48,768]{2,1,0:T(8,128)(2,1)S(1)} %dynamic-slice_bitcast_fusion.10), channel_id=1, source_target_pairs={{0,8},{4,12},{8,0},{12,4},{16,24},{20,28},{24,16},{28,20},{1,9},{5... | collective-permute-start | bytes 442376 | tf_op jit(solution)/shard_map/ppermute | solution.py:368
  231.4 6.3 %collective-permute-start.21 = (bf16[24,1536]{1,0:T(8,128)(2,1)S(1)}, bf16[24,1536]{1,0:T(8,128)(2,1)S(1)}, u32[]{:S(2)}, u32[]{:S(2)}) collective-permute-start(bf16[24,1536]{1,0:T(8,128)(2,1)S(1)} %dynamic-slice_bitcast_fusion.14), channel_id=1, source_target_pairs={{0,16},{4,20},{8,24},{12,28},{16,0},{20,4},{24,8},{28,12},{1,17},{... | collective-permute-start | bytes 221192 | tf_op jit(solution)/shard_map/ppermute | solution.py:368
  236.3 56.2 %collective-permute-start.35 = (bf16[48,768]{1,0:T(8,128)(2,1)}, bf16[48,768]{1,0:T(8,128)(2,1)S(1)}, u32[]{:S(2)}, u32[]{:S(2)}) collective-permute-start(bf16[48,768]{1,0:T(8,128)(2,1)} %dynamic-slice_bitcast_fusion.13), channel_id=1, source_target_pairs={{0,16},{4,20},{8,24},{12,28},{16,0},{20,4},{24,8},{28,12},{1,17},{... | collective-permute-start | bytes 221192 | tf_op jit(solution)/shard_map/ppermute | solution.py:368
  237.8 66.5 %collective-permute-start.22 = (bf16[24,1536]{1,0:T(8,128)(2,1)S(1)}, bf16[24,1536]{1,0:T(8,128)(2,1)}, u32[]{:S(2)}, u32[]{:S(2)}) collective-permute-start(bf16[24,1536]{1,0:T(8,128)(2,1)S(1)} %fusion.36), channel_id=1, source_target_pairs={{0,2},{1,3},{2,0},{3,1},{4,6},{5,7},{6,4},{7,5},{8,10},{9,11},{10,... | collective-permute-start | bytes 221192 | tf_op jit(solution)/shard_map/ppermute | solution.py:368
  239.8 54.8 %copy-start.19 = (f32[1792,4]{0,1:T(4,128)S(1)}, f32[1792,4]{0,1:T(4,128)}, u32[]{:S(2)}) copy-start(f32[1792,4]{0,1:T(4,128)} %copy-done.18) | copy-start | bytes 86020
  291.2 3.3 collective-permute-start.16
  292.5 13.4 %collective-permute-start.36 = (bf16[48,768]{1,0:T(8,128)(2,1)S(1)}, bf16[48,768]{1,0:T(8,128)(2,1)S(1)}, u32[]{:S(2)}, u32[]{:S(2)}) collective-permute-start(bf16[48,768]{1,0:T(8,128)(2,1)S(1)} %fusion.35), channel_id=1, source_target_pairs={{0,2},{1,3},{2,0},{3,1},{4,6},{5,7},{6,4},{7,5},{8,10},{9,11},{10,... | collective-permute-start | bytes 221192 | tf_op jit(solution)/shard_map/ppermute | solution.py:368
  303.4 9.8 %collective-permute-start.24 = (bf16[2,2,2,2,24,1920]{5,4,3,2,1,0:T(8,128)(2,1)}, bf16[2,2,2,2,24,1920]{5,4,3,2,1,0:T(8,128)(2,1)}, u32[]{:S(2)}, u32[]{:S(2)}) collective-permute-start(bf16[2,2,2,2,24,1920]{5,4,3,2,1,0:T(8,128)(2,1)} %dynamic-slice_bitcast_fusion), channel_id=1, source_target_pairs={{0,1},{1,0},{2,3},{3,2},{4,5},{5,4},{6,7},{7,6},{8,9},{9,8},{10,11... | collective-permute-start | bytes 4423688 | tf_op jit(solution)/shard_map/ppermute | solution.py:368
  305.2 7.4 %copy-start.28 = (f32[16,128]{1,0:T(8,128)S(1)}, f32[16,128]{1,0:T(8,128)}, u32[]{:S(2)}) copy-start(f32[16,128]{1,0:T(8,128)} %get-tuple-element.63) | copy-start | bytes 24580
  305.9 33.4 %collective-permute-start.23 = (bf16[2,24,1536]{2,1,0:T(8,128)(2,1)}, bf16[2,24,1536]{2,1,0:T(8,128)(2,1)}, u32[]{:S(2)}, u32[]{:S(2)}) collective-permute-start(bf16[2,24,1536]{2,1,0:T(8,128)(2,1)} %pad_maximum_fusion.19), channel_id=1, source_target_pairs={{0,1},{1,0},{2,3},{3,2},{4,5},{5,4},{6,7},{7,6},{8,9},{9,8},{10,11... | collective-permute-start | bytes 442376 | tf_op jit(solution)/shard_map/ppermute | solution.py:368
  306.7 41.3 %collective-permute-start.37 = (bf16[2,48,768]{2,1,0:T(8,128)(2,1)}, bf16[2,48,768]{2,1,0:T(8,128)(2,1)}, u32[]{:S(2)}, u32[]{:S(2)}) collective-permute-start(bf16[2,48,768]{2,1,0:T(8,128)(2,1)} %pad_maximum_fusion.20), channel_id=1, source_target_pairs={{0,1},{1,0},{2,3},{3,2},{4,5},{5,4},{6,7},{7,6},{8,9},{9,8},{10,11... | collective-permute-start | bytes 442376 | tf_op jit(solution)/shard_map/ppermute | solution.py:368
  313.2 4.5 %copy-start.3 = (bf16[2,2,2,2,2,24,1920]{6,5,4,3,2,1,0:T(8,128)(2,1)S(1)}, bf16[2,2,2,2,2,24,1920]{6,5,4,3,2,1,0:T(8,128)(2,1)}, u32[]{:S(2)}) copy-start(bf16[2,2,2,2,2,24,1920]{6,5,4,3,2,1,0:T(8,128)(2,1)} %copy-done.2) | copy-start | bytes 8847364
  317.6 18.8 %collective-permute-start.25 = (bf16[2,2,2,24,1920]{4,3,2,1,0:T(8,128)(2,1)}, bf16[2,2,2,24,1920]{4,3,2,1,0:T(8,128)(2,1)}, u32[]{:S(2)}, u32[]{:S(2)}) collective-permute-start(bf16[2,2,2,24,1920]{4,3,2,1,0:T(8,128)(2,1)} %dynamic-slice_bitcast_fusion.3), channel_id=1, source_target_pairs={{0,2},{1,3},{2,0},{3,1},{4,6},{5,7},{6,4},{7,5},{8,10},{9,11},{10,... | collective-permute-start | bytes 2211848 | tf_op jit(solution)/shard_map/ppermute | solution.py:368
  327.0 6.4 %collective-permute-start.38 = (f32[11336]{0:T(1024)S(1)}, f32[11336]{0:T(1024)S(1)}, u32[]{:S(2)}, u32[]{:S(2)}) collective-permute-start(f32[11336]{0:T(1024)S(1)} %concatenate.41), channel_id=1, source_target_pairs={{0,16},{4,20},{8,24},{12,28},{16,0},{20,4},{24,8},{28,12},{1,17},{... | collective-permute-start | bytes 136040 | tf_op jit(solution)/shard_map/ppermute | solution.py:368
  328.9 7.5 %copy-start.6 = (bf16[2,2,2,2,24,1920]{5,4,3,2,1,0:T(8,128)(2,1)S(1)}, bf16[2,2,2,2,24,1920]{5,4,3,2,1,0:T(8,128)(2,1)}, u32[]{:S(2)}) copy-start(bf16[2,2,2,2,24,1920]{5,4,3,2,1,0:T(8,128)(2,1)} %copy-done.5) | copy-start | bytes 4423684
  333.5 15.6 %collective-permute-start.39 = (f32[11336]{0:T(1024)S(1)}, f32[11336]{0:T(1024)S(1)}, u32[]{:S(2)}, u32[]{:S(2)}) collective-permute-start(f32[11336]{0:T(1024)S(1)} %add.278), channel_id=1, source_target_pairs={{0,8},{4,12},{8,0},{12,4},{16,24},{20,28},{24,16},{28,20},{1,9},{5... | collective-permute-start | bytes 136040 | tf_op jit(solution)/shard_map/ppermute | solution.py:368
  337.7 9.8 %collective-permute-start.26 = (bf16[2,2,24,1920]{3,2,1,0:T(8,128)(2,1)S(1)}, bf16[2,2,24,1920]{3,2,1,0:T(8,128)(2,1)S(1)}, u32[]{:S(2)}, u32[]{:S(2)}) collective-permute-start(bf16[2,2,24,1920]{3,2,1,0:T(8,128)(2,1)S(1)} %dynamic-slice_bitcast_fusion.6), channel_id=1, source_target_pairs={{0,4},{4,0},{8,12},{12,8},{16,20},{20,16},{24,28},{28,24},{1,5},{5... | collective-permute-start | bytes 1105928 | tf_op jit(solution)/shard_map/ppermute | solution.py:368
  347.6 5.6 %collective-permute-start.27 = (bf16[2,24,1920]{2,1,0:T(8,128)(2,1)S(1)}, bf16[2,24,1920]{2,1,0:T(8,128)(2,1)S(1)}, u32[]{:S(2)}, u32[]{:S(2)}) collective-permute-start(bf16[2,24,1920]{2,1,0:T(8,128)(2,1)S(1)} %dynamic-slice_bitcast_fusion.9), channel_id=1, source_target_pairs={{0,8},{4,12},{8,0},{12,4},{16,24},{20,28},{24,16},{28,20},{1,9},{5... | collective-permute-start | bytes 552968 | tf_op jit(solution)/shard_map/ppermute | solution.py:368
  348.9 7.1 %copy-start.15 = (f32[192,768]{1,0:T(8,128)S(1)}, f32[192,768]{1,0:T(8,128)}, u32[]{:S(2)}) copy-start(f32[192,768]{1,0:T(8,128)} %param.16) | copy-start | bytes 1769476
  348.9 7.1 %copy-start.16 = (f32[192,768]{1,0:T(8,128)S(1)}, f32[192,768]{1,0:T(8,128)}, u32[]{:S(2)}) copy-start(f32[192,768]{1,0:T(8,128)} %param.17) | copy-start | bytes 1769476
  348.9 7.1 %copy-start.17 = (f32[192,768]{1,0:T(8,128)S(1)}, f32[192,768]{1,0:T(8,128)}, u32[]{:S(2)}) copy-start(f32[192,768]{1,0:T(8,128)} %param.18) | copy-start | bytes 1769476
  349.1 8.5 %collective-permute-start.40 = (f32[11336]{0:T(1024)S(1)}, f32[11336]{0:T(1024)S(1)}, u32[]{:S(2)}, u32[]{:S(2)}) collective-permute-start(f32[11336]{0:T(1024)S(1)} %add.279), channel_id=1, source_target_pairs={{0,4},{4,0},{8,12},{12,8},{16,20},{20,16},{24,28},{28,24},{1,5},{5... | collective-permute-start | bytes 136040 | tf_op jit(solution)/shard_map/ppermute | solution.py:368
  353.3 6.2 %collective-permute-start.28 = (bf16[24,1920]{1,0:T(8,128)(2,1)S(1)}, bf16[24,1920]{1,0:T(8,128)(2,1)S(1)}, u32[]{:S(2)}, u32[]{:S(2)}) collective-permute-start(bf16[24,1920]{1,0:T(8,128)(2,1)S(1)} %dynamic-slice_bitcast_fusion.12), channel_id=1, source_target_pairs={{0,16},{4,20},{8,24},{12,28},{16,0},{20,4},{24,8},{28,12},{1,17},{... | collective-permute-start | bytes 276488 | tf_op jit(solution)/shard_map/ppermute | solution.py:368
  357.5 6.8 %copy-start.21 = (f32[11336]{0:T(1024)S(1)}, f32[11336]{0:T(1024)}, u32[]{:S(2)}) copy-start(f32[11336]{0:T(1024)} %param.19) | copy-start | bytes 136036
  357.5 6.8 %copy-start.24 = (f32[11336]{0:T(1024)S(1)}, f32[11336]{0:T(1024)}, u32[]{:S(2)}) copy-start(f32[11336]{0:T(1024)} %param.20) | copy-start | bytes 136036
  357.5 6.8 %copy-start.25 = (f32[11336]{0:T(1024)S(1)}, f32[11336]{0:T(1024)}, u32[]{:S(2)}) copy-start(f32[11336]{0:T(1024)} %param.21) | copy-start | bytes 136036
  357.6 4.2 %collective-permute-start.41 = (f32[11336]{0:T(1024)S(1)}, f32[11336]{0:T(1024)S(1)}, u32[]{:S(2)}, u32[]{:S(2)}) collective-permute-start(f32[11336]{0:T(1024)S(1)} %add.280), channel_id=1, source_target_pairs={{0,2},{1,3},{2,0},{3,1},{4,6},{5,7},{6,4},{7,5},{8,10},{9,11},{10,... | collective-permute-start | bytes 136040 | tf_op jit(solution)/shard_map/ppermute | solution.py:368
  359.5 4.6 %collective-permute-start.29 = (bf16[24,1920]{1,0:T(8,128)(2,1)S(1)}, bf16[24,1920]{1,0:T(8,128)(2,1)S(1)}, u32[]{:S(2)}, u32[]{:S(2)}) collective-permute-start(bf16[24,1920]{1,0:T(8,128)(2,1)S(1)} %fusion.34), channel_id=1, source_target_pairs={{0,2},{1,3},{2,0},{3,1},{4,6},{5,7},{6,4},{7,5},{8,10},{9,11},{10,... | collective-permute-start | bytes 276488 | tf_op jit(solution)/shard_map/ppermute | solution.py:368
  360.6 5.3 %copy-start.14 = (f32[96,3352]{1,0:T(8,128)S(1)}, f32[96,3352]{1,0:T(8,128)}, u32[]{:S(2)}) copy-start(f32[96,3352]{1,0:T(8,128)} %param.15) | copy-start | bytes 3861508
  361.7 2.6 collective-permute-start.42
  364.2 1.5 collective-permute-start.30
  (12 other events, 26.5 us)
Sparse Core Ops, SparseCore 0:
  125.6 19.2 all-gather.4
  175.4 18.2 all-gather.6

commit v3 on v2

--- a/solution.py
+++ b/solution.py
@@ -380,25 +380,53 @@
     return (lax.axis_index(axis) >> bit) & 1
 
 
-def gather_pairs(v, bits):
-    dims = v.shape
+def merge_pair(v, other, place, axis, bit):
+    second = mine(axis, bit) == 1
+    return jnp.stack([jnp.where(second, other, v), jnp.where(second, v, other)], axis=place)
+
+
+def gather_step(v, place, axis, bit):
+    return merge_pair(v, swap(v, axis, bit), place, axis, bit)
+
+
+def gather_pairs(v, bits, lead=0):
     for place, (axis, bit) in enumerate(bits):
-        other = swap(v, axis, bit)
-        second = mine(axis, bit) == 1
-        v = jnp.stack([jnp.where(second, other, v), jnp.where(second, v, other)], axis=place)
-    return v.reshape((dims[0] << len(bits),) + dims[1:])
-
-
-def scatter_pairs(v, bits):
-    width = v.shape[1]
-    v = v.reshape((2,) * len(bits) + (v.shape[0] >> len(bits), width))
-    for place in reversed(range(len(bits))):
-        axis, bit = bits[place]
-        own = mine(axis, bit)
-        keep = lax.dynamic_index_in_dim(v, own, place, keepdims=False)
-        give = lax.dynamic_index_in_dim(v, 1 - own, place, keepdims=False)
-        v = (keep.astype(f32) + swap(give, axis, bit).astype(f32)).astype(v.dtype)
+        v = gather_step(v, lead + place, axis, bit)
     return v
+
+
+def flat(v):
+    return v.reshape(-1, v.shape[-1])
+
+
+def gather_crossed(v, bits):
+    cross = len(bits) - 3
+    v = gather_pairs(v, bits[:cross])
+    half = v.shape[-1] // 256 * 128
+    left, right = v[..., :half], v[..., half:]
+    left = gather_step(left, cross, *bits[cross])
+    right = gather_step(right, cross, *bits[cross + 1])
+    left = gather_step(left, cross + 1, *bits[cross + 1])
+    right = gather_step(right, cross, *bits[cross])
+    left = gather_step(left, cross + 2, *bits[cross + 2])
+    right = gather_step(right, cross + 2, *bits[cross + 2])
+    return jnp.concatenate([flat(left), flat(right)], axis=1)
+
+
+def split_pair(v, place, axis, bit):
+    own = mine(axis, bit)
+    keep = lax.dynamic_index_in_dim(v, own, place, keepdims=False)
+    give = lax.dynamic_index_in_dim(v, 1 - own, place, keepdims=False)
+    return keep, give
+
+
+def add_low(keep, got):
+    return (keep.astype(f32) + got.astype(f32)).astype(keep.dtype)
+
+
+def scatter_step(v, place, axis, bit):
+    keep, give = split_pair(v, place, axis, bit)
+    return add_low(keep, swap(give, axis, bit))
 
 
 def sum_pairs(v, bits):
@@ -499,9 +527,13 @@
 
     in_part = quarter(in_weight)
     side_part = jnp.pad(in_part[:, INNER:], ((0, 0), (0, SIDE + INNER - PROJ)))
-    full_side = gather_pairs(side_part, bits)
-    full_gate = gather_pairs(in_part[:, :INNER], bits)
-    full_out = gather_pairs(quarter(out_weight), bits)
+    full_side = gather_crossed(side_part, bits)
+
+    beside = [
+        lax.all_gather(part, "dp", axis=0, tiled=False)
+        for part in (in_part[:, :INNER], quarter(out_weight))
+    ]
+    (y_axis, y_bit), (core_axis, core_bit) = seq_bits
 
     forward = [(s, s + 1) for s in range(groups - 1)]
     backward = [(s + 1, s) for s in range(groups - 1)]
@@ -526,6 +558,8 @@
 
     proj = dot(normed_low, full_side).astype(bf16)
     halo = dot(halo_norm, full_side[:, :XBC]).astype(bf16)
+    proj, halo, beside = lax.optimization_barrier((proj, halo, beside))
+    others = [swap(part, y_axis, y_bit) for part in beside]
 
     x, bc, u, cum, cumt, dt, hst, pfx, send = pl.pallas_call(
         conv_state_kernel,
@@ -552,11 +586,16 @@
             pltpu.VMEM((CHUNK, INNER), bf16), pltpu.VMEM((8, LANES), f32),
         ],
         compiler_params=params(),
-        cost_estimate=cost(10**9, 24 * 2**20),
+        cost_estimate=cost(24 * 10**9, 24 * 2**20),
         name="conv_state",
     )(proj, halo, convp, headp, spread)
 
     states = lax.all_gather(send, "seq", axis=0, tiled=False)
+    (x, bc, u, cum, cumt, dt, hst, pfx), others = lax.optimization_barrier(
+        ((x, bc, u, cum, cumt, dt, hst, pfx), others)
+    )
+    beside = [merge_pair(part, other, 1, y_axis, y_bit) for part, other in zip(beside, others)]
+    others = [swap(part, core_axis, core_bit) for part in beside]
 
     y_within = pl.pallas_call(
         within_kernel,
@@ -568,9 +607,13 @@
         out_specs=by_chunk(INNER),
         out_shape=shape((count, INNER), f32),
         compiler_params=params(),
-        cost_estimate=cost(4 * 10**9, 16 * 2**20),
+        cost_estimate=cost(11 * 10**9, 16 * 2**20),
         name="within",
     )(u, bc, cum, cumt)
+    y_within, others = lax.optimization_barrier((y_within, others))
+    full_gate, full_out = [
+        flat(merge_pair(part, other, 2, core_axis, core_bit)) for part, other in zip(beside, others)
+    ]
     gate = dot(normed_low, full_gate).astype(bf16)
 
     gathered_spec = full((groups, STATE, INNER))
@@ -606,7 +649,7 @@
             pltpu.VMEM((CHUNK, INNER), bf16),
         ],
         compiler_params=params(),
-        cost_estimate=cost(8 * 10**9, 48 * 2**20),
+        cost_estimate=cost(30 * 10**9, 48 * 2**20),
         name="gate_norm",
     )(
         rank, y_within, x, bc, cum, hst, states, states, gate, tok_low, cot_low, full_out, spread,
@@ -615,26 +658,51 @@
 
     grads = lax.all_gather(glocal.astype(bf16), "seq", axis=0, tiled=False)
 
+    def product(left, right):
+        return lax.dot_general(left, right, TN, preferred_element_type=f32).astype(bf16)
+
+    def blocks(v, cut):
+        return v.reshape((2,) * len(cut) + (v.shape[0] >> len(cut), v.shape[1]))
+
+    dp_size = lax.axis_size("dp")
+
+    def by_owner(v):
+        return v.reshape(dp_size, 2, 2, v.shape[0] // (4 * dp_size), v.shape[1])
+
+    keeps, gives = zip(
+        *[
+            split_pair(by_owner(product(left, right)), 2, core_axis, core_bit)
+            for left, right in ((hidden, cot_low), (normed_low, dgate))
+        ]
+    )
+    first_got = [swap(give, core_axis, core_bit) for give in gives]
+    anywhere = pl.BlockSpec(memory_space=pl.ANY)
+
+    def within_back_call(u, dy, bc, cum, cumt, sent_a, sent_b, dxs_out, dbc_out):
+        within_back_kernel(u, dy, bc, cum, cumt, dxs_out, dbc_out)
+
     dxs, dbc = pl.pallas_call(
-        within_back_kernel,
+        within_back_call,
         grid=(chunks,),
         in_specs=[
             by_chunk(INNER), by_chunk(INNER), by_chunk(2 * STATE), by_chunk(LANES),
-            pl.BlockSpec((32, CHUNK), lambda c: (0, c)),
+            pl.BlockSpec((32, CHUNK), lambda c: (0, c)), anywhere, anywhere,
         ],
         out_specs=[by_chunk(INNER), by_chunk(2 * STATE)],
         out_shape=[shape((count, INNER), f32), shape((count, 2 * STATE), f32)],
         compiler_params=params(),
-        cost_estimate=cost(8 * 10**9, 16 * 2**20),
+        cost_estimate=cost(12 * 10**9, 16 * 2**20),
         name="within_back",
-    )(u, dy, bc, cum, cumt)
-
-    def summed(left, right):
-        product = lax.dot_general(left, right, TN, preferred_element_type=f32).astype(bf16)
-        return scatter_pairs(product, bits)
-
-    out_scattered = summed(hidden, cot_low)
-    gate_scattered = summed(normed_low, dgate)
+    )(u, dy, bc, cum, cumt, *gives)
+
+    halves_got, dxs, dbc = lax.optimization_barrier((first_got, dxs, dbc))
+    keeps, gives = zip(
+        *[
+            split_pair(add_low(keep, got), 1, y_axis, y_bit)
+            for keep, got in zip(keeps, halves_got)
+        ]
+    )
+    second_got = [swap(give, y_axis, y_bit) for give in gives]
 
     def back(width, height=CHUNK):
         return pl.BlockSpec((height, width), lambda c: (chunks - 1 - c, 0))
@@ -642,7 +710,7 @@
     def back_three(height):
         return pl.BlockSpec((1, height, INNER), lambda c: (chunks - 1 - c, 0, 0))
 
-    def back_call(*refs):
+    def back_call(sent_a, sent_b, *refs):
         back_kernel(groups, *refs)
 
     per = CHUNK // 16
@@ -650,7 +718,7 @@
         back_call,
         grid=(chunks,),
         in_specs=[
-            smem, back(INNER), back(INNER), back(INNER), back(INNER), back(INNER), back(2 * STATE),
+            anywhere, anywhere, smem, back(INNER), back(INNER), back(INNER), back(INNER), back(INNER), back(2 * STATE),
             back(2 * STATE), back(LANES), back(LANES), back(LANES), back_three(STATE),
             pl.BlockSpec((1, 8, LANES), lambda c: (chunks - 1 - c, 0, 0)),
             full((STATE, INNER)), gathered_spec, logs_spec, back_three(STATE), back(SIDE),
@@ -674,13 +742,16 @@
             pltpu.VMEM((CHUNK, 2 * INNER), bf16), pltpu.VMEM((CHUNK, 2 * INNER), bf16),
         ],
         compiler_params=params(),
-        cost_estimate=cost(4 * 10**9, 48 * 2**20),
+        cost_estimate=cost(47 * 10**9, 48 * 2**20),
         name="mixer_back",
     )(
-        rank, dxs, dy, x, u, y, bc, dbc, dcc, cum, dt, hst, pfx, h0, grads, states, ust, proj, proj,
+        *gives, rank, dxs, dy, x, u, y, bc, dbc, dcc, cum, dt, hst, pfx, h0, grads, states, ust, proj, proj,
         halo, convp, headp, spread, collect, rows,
     )
 
+    second_got, pg, first, tail, wg, hgr, skip = lax.optimization_barrier(
+        (second_got, pg, first, tail, wg, hgr, skip)
+    )
     after = lax.ppermute(first, "seq", backward)
     fixes = [jnp.zeros((5, XBC), f32)]
     for m in range(CONV - 1):
@@ -691,13 +762,40 @@
     tail_low = (tail + jnp.concatenate(fixes, axis=0)).astype(bf16)
     pg = lax.dynamic_update_slice(pg, tail_low, (count - 8, 0))
 
-    side_scattered = summed(normed_low, pg)
-
+    out_scattered, gate_scattered = [
+        lax.psum_scatter(flat(add_low(keep, got)), "dp", scatter_dimension=0, tiled=True)
+        for keep, got in zip(keeps, second_got)
+    ]
+
+    cross = len(bits) - 3
+    half = SIDE // 256 * 128
+    left = blocks(product(normed_low, pg[:, :half]), bits)
+    right = blocks(product(normed_low, pg[:, half:]), bits)
+    barrier = lax.optimization_barrier
+    keep_l, give_l = split_pair(left, cross + 2, core_axis, core_bit)
+    keep_r, give_r = split_pair(right, cross + 2, core_axis, core_bit)
+    got_l, got_r = swap(give_l, core_axis, core_bit), swap(give_r, core_axis, core_bit)
+    pg, dgate, _, _ = barrier((pg, dgate, give_l, give_r))
     normed_grad = lax.dot_general(dgate, full_gate, NT, preferred_element_type=f32)
     normed_grad = normed_grad + lax.dot_general(pg, full_side, NT, preferred_element_type=f32)
+    got_l, got_r, normed_grad = barrier((got_l, got_r, normed_grad))
+    x_axis, x_bit = bits[cross]
+    keep_l, give_l = split_pair(add_low(keep_l, got_l), cross + 1, y_axis, y_bit)
+    keep_r, give_r = split_pair(add_low(keep_r, got_r), cross, x_axis, x_bit)
+    got_l, got_r = swap(give_l, y_axis, y_bit), swap(give_r, x_axis, x_bit)
+    normed_grad, _, _ = barrier((normed_grad, give_l, give_r))
     _, norm_pull = jax.vjp(pre_norm, tok_vals, pre_gain)
     tok_norm_grad, pre_gain_grad = norm_pull(normed_grad)
     token_grad = (cot_low.astype(f32) + tok_norm_grad)[None]
+    got_l, got_r, token_grad, pre_gain_grad = barrier((got_l, got_r, token_grad, pre_gain_grad))
+    left = scatter_step(add_low(keep_l, got_l), cross, x_axis, x_bit)
+    right = scatter_step(add_low(keep_r, got_r), cross, y_axis, y_bit)
+    side_scattered = jnp.concatenate([left, right], axis=-1)
+    side_scattered, out_scattered, gate_scattered = barrier(
+        (side_scattered, out_scattered, gate_scattered)
+    )
+    for place in reversed(range(cross)):
+        side_scattered = scatter_step(side_scattered, place, *bits[place])
 
     wg_sum = jnp.sum(wg.reshape(5, 8, XBC), axis=1)
     chan_grad = jnp.concatenate(
@@ -714,7 +812,7 @@
     chan_grad = sum_pairs(chan_grad, bits)
 
     def owned(part):
-        return gather_pairs(part, seq_bits).astype(f32)
+        return flat(gather_pairs(part, seq_bits)).astype(f32)
 
     out_grad = owned(out_scattered)
     in_grad = jnp.concatenate(

time: 380 us -> 452 us (1.19)
  blocking collectives: 0 us -> 67.2 us
  waiting for transfers between devices: 95.7 us -> 119 us
  Pallas kernels: 119 us -> 108 us
  matrix products: 37.7 us -> 29.7 us
    reduce_scatter x0 -> x2, waiting for transfers between devices: none -> 74.6 us  [local(): lax.psum_scatter(flat(add_low(keep, got)), 'dp', scatter_dimension=0, til...]
    all_gather x0 -> x2, blocking collectives: none -> 67.2 us  [local(): lax.all_gather(part, 'dp', axis=0, tiled=False)]
    ppermute x41 -> x35, waiting for transfers between devices: 94.5 us -> 39.9 us  [swap(): return lax.ppermute(v, axis, [(i, i ^ 1 << bit) for i in range(size)])]
    pallas_call x2, Pallas kernels: 61.9 us -> 51 us  [the longest x1 40.5 us: local(): pl.pallas_call(back_call, grid=(chunks,), in_specs=[anywhere, anywhere, s...]
    dot_general x1, matrix products: 8.57 us -> 3.46 us  [local(): lax.dot_general(pg, full_side, NT, preferred_element_type=f32)]
    ppermute x41 -> x35, starting transfers between devices: 42.3 us -> 38.2 us  [swap(): return lax.ppermute(v, axis, [(i, i ^ 1 << bit) for i in range(size)])]
    another operation x41 -> x35, other arithmetic: 12.7 us -> 15 us  [merge_pair(): jnp.stack([jnp.where(second, other, v), jnp.where(second, v, other)], axi...]
    dot_general x3 -> x4, matrix products: 14 us -> 13.1 us  [product(): lax.dot_general(left, right, TN, preferred_element_type=f32).astype(bf16)]
  transfers between devices with their start and end apart: 45 -> 41, of which waited for: 20 -> 19; matrix products, arithmetic and copies ran while one was open for 24% -> 14% of each run, Pallas kernels for 25% -> 18%
where the time goes in v3:
time: 452 us; the launch traced here: 444 us
  waiting for transfers between devices  119 us (26%)
  Pallas kernels  108 us (24%)
  blocking collectives  67.2 us (15%)
  starting transfers between devices  42.6 us (9%)
  other arithmetic  39.2 us (9%)
  matrix products  29.7 us (7%)
  local copies, waits for them, and re-layouts  22.7 us (5%)
  between operations  15.4 us (3%)
    reduce_scatter x2, waiting for transfers between devices, local(): lax.psum_scatter(flat(add_low(keep, got)), 'dp', scatter_dimension=0, til...  74.6 us
    all_gather x2, blocking collectives, local(): lax.all_gather(part, 'dp', axis=0, tiled=False)  67.2 us
    pallas_call x1, Pallas kernels, local(): pl.pallas_call(back_call, grid=(chunks,), in_specs=[anywhere, anywhere, s...  40.5 us
    ppermute x35, waiting for transfers between devices, swap(): return lax.ppermute(v, axis, [(i, i ^ 1 << bit) for i in range(size)])  39.9 us
    ppermute x35, starting transfers between devices, swap(): return lax.ppermute(v, axis, [(i, i ^ 1 << bit) for i in range(size)])  38.2 us
    pallas_call x1, Pallas kernels, local(): pl.pallas_call(gate_call, grid=(chunks,), in_specs=[smem, by_chunk(INNER)...  26.2 us
    pallas_call x1, Pallas kernels, local(): pl.pallas_call(conv_state_kernel, grid=(chunks,), in_specs=[by_chunk(SIDE...  21 us
    another operation x35, other arithmetic, merge_pair(): jnp.stack([jnp.where(second, other, v), jnp.where(second, v, other)], axi...  15 us
  transfers between devices with their start and end apart: 41, of which 19 were waited for; matrix products, arithmetic and copies ran while one was open for 14% of the time, Pallas kernels for 18%

profile of v3, /device:TPU:0, one launch (start us, length us, event | category | flops | bytes accessed | tf_op | source)
XLA Modules:
  0.0 443.5 jit_solution(3485901597409616068)
XLA Ops:
  8.0 2.3 collective-permute-start.8
  11.4 3.5 collective-permute-start
  17.4 33.6 %all-gather = bf16[192,1536]{1,0:T(8,128)(2,1)} all-gather(bf16[24,1536]{1,0:T(8,128)(2,1)S(1)} %slice.124), channel_id=2, replica_groups=mesh['dp'=8,'seq'=4] {'dp'}, dimensions={0}, use_global_device_ids=true | all-gather | bytes 663552 | tf_op jit(solution)/shard_map/all_gather | solution.py:533
  51.9 33.6 %all-gather.1 = bf16[384,768]{1,0:T(8,128)(2,1)} all-gather(bf16[48,768]{1,0:T(8,128)(2,1)S(1)} %dynamic-slice_convert_fusion.1), channel_id=3, replica_groups=mesh['dp'=8,'seq'=4] {'dp'}, dimensions={0}, use_global_device_ids=true | all-gather | bytes 663552 | tf_op jit(solution)/shard_map/all_gather | solution.py:533
  89.5 5.1 %collective-permute-done.1 = bf16[2,24,1920]{2,1,0:T(8,128)(2,1)S(1)} collective-permute-done((bf16[2,24,1920]{2,1,0:T(8,128)(2,1)S(1)}, bf16[2,24,1920]{2,1,0:T(8,128)(2,1)S(1)}, u32[]{:S(2)}, u32[]{:S(2)}) %collective-permute-start.1) | collective-permute-done | bytes 184352 | tf_op jit(solution)/shard_map/ppermute | solution.py:368
  95.7 2.2 collective-permute-start.5
  97.8 2.3 collective-permute-done.2
  100.3 2.2 collective-permute-start.3
  103.8 3.9 collective-permute-done.3
  108.7 1.7 collective-permute-done.6
  113.8 1.3 select_bitcast_fusion.7
  115.2 1.7 select_bitcast_fusion.5
  117.3 5.1 %convolution_convert_fusion.1.proj.refs_17_.refs_18_ = bf16[1024,1920]{1,0:T(8,128)(2,1)} fusion(bf16[768,1024]{1,0:T(8,128)(2,1)S(1)} %bitcast.233, bf16[768,896]{1,0:T(8,128)(2,1)S(1)} %bitcast.239, f32[768]{0:T(1024)S(1)} %slice.96, f32[1024]{0:T(1024)S(1)} %fusion.60, bf16[1,1024,768]{2,1,0:T(8,128)(2,1)S(1)} %copy-done), kind=kOutput, calls=%fused_computation.6 | convolution fusion | flops 3030908928 | bytes 8461312 | tf_op jit(solution)/shard_map/dot_general | solution.py:43
  125.6 21.0 %conv_state.1 = (bf16[1024,1536]{1,0:T(8,128)(2,1)}, bf16[1024,256]{1,0:T(8,128)(2,1)}, bf16[1024,1536]{1,0:T(8,128)(2,1)}, f32[1024,128]{1,0:T(8,128)}, f32[32,...) custom-call(bf16[1024,1920]{1,0:T(8,128)(2,1)} %convolution_convert_, ...), custom_call_target="tpu_custom_call" | custom-call | flops 24000000000 | bytes 25165824 | tf_op jit(solution)/shard_map/conv_state/pallas_call | solution.py:564
  146.6 5.4 %collective-permute-done.10 = bf16[8,48,768]{2,1,0:T(8,128)(2,1)S(1)} collective-permute-done((bf16[8,48,768]{2,1,0:T(8,128)(2,1)S(1)}, bf16[8,48,768]{2,1,0:T(8,128)(2,1)S(1)}, u32[]{:S(2)}, u32[]{:S(2)}) %collective-permute-start.10) | collective-permute-done | bytes 589856 | tf_op jit(solution)/shard_map/ppermute | solution.py:368
  152.2 1.2 pad_maximum_fusion.7
  155.9 9.8 %within.1.refs_1_ = f32[1024,1536]{1,0:T(8,128)} custom-call(bf16[1024,1536]{1,0:T(8,128)(2,1)} %get-tuple-element.92.u.refs_4_, bf16[1024,256]{1,0:T(8,128)(2,1)} %get-tuple-element.93.bc.refs_3_.refs_6_, f32[1024,128]{1,0:T(8,128)} %get-tuple-element.94.cum.refs_4_.refs_9_, f32[32,1024]{1,0:T(8,128)} %get-tuple-element.95.cumt), custom_call_target="tpu_custom_call" | custom-call | flops 11000000512 | bytes 16777216 | tf_op jit(solution)/shard_map/within/pallas_call | solution.py:600
  165.8 1.4 select_bitcast_fusion.1
  167.2 1.7 pad_maximum_fusion.2
  168.9 1.4 select_bitcast_fusion.3
  170.6 1.4 copy-done.11
  172.0 4.2 convolution_convert_fusion.refs_8_
  176.2 26.2 %gate_norm.1 = (f32[1024,768]{1,0:T(8,128)}, bf16[1024,1536]{1,0:T(8,128)(2,1)}, f32[1024,1536]{1,0:T(8,128)}, bf16[1024,1536]{1,0:T(8,128)(2,1)}, bf16[1024,153...) custom-call(s32[1]{0:T(128)} %bitcast.refs_0_, ...), custom_call_target="tpu_custom_call" | custom-call | flops 30000001024 | bytes 50331648 | tf_op jit(solution)/shard_map/gate_norm/pallas_call | solution.py:626
  202.4 4.6 %convolution_convert_fusion.3 = bf16[1536,768]{1,0:T(8,128)(2,1)S(1)} fusion(bf16[1024,1536]{1,0:T(8,128)(2,1)} %get-tuple-element.105, bf16[1,1024,768]{2,1,0:T(8,128)(2,1)S(1)} %copy-done.14), kind=kOutput, calls=%fused_computation.10 | convolution fusion | flops 2417098752 | bytes 7077888 | tf_op jit(solution)/shard_map/dot_general | solution.py:662
  210.2 3.0 convolution_convert_fusion.2
  218.7 10.6 %within_back.1 = (f32[1024,1536]{1,0:T(8,128)}, f32[1024,256]{1,0:T(8,128)}) custom-call(bf16[1024,1536]{1,0:T(8,128)(2,1)} %get-tuple-element.92.u.refs_4_, bf16[1024,1536]{1,0:T(8,128)(2,1)} %get-tuple-element.107.dy.refs_2_, bf16[1024,256]{1,0:T(8,128)(2,1)} %get-tuple-element.93.bc.refs_3_.refs_6_, f32[1024,128]{1,0:T(8,128)} %get-tuple-element.94.cum.refs_4_.refs_9_, ...), custom_call_target="tpu_custom_call" | custom-call | flops 12000000000 | bytes 16777216 | tf_op jit(solution)/shard_map/within_back/pallas_call | solution.py:684
  229.3 1.7 fusion.13
  231.0 1.2 collective-permute-start.15
  232.2 1.6 fusion.12
  235.6 4.2 all-gather.9.cloned.1.call-done
  239.8 40.5 %mixer_back.1 = (bf16[1024,1920]{1,0:T(8,128)(2,1)}, f32[8,1792]{1,0:T(8,128)}, f32[8,1792]{1,0:T(8,128)}, f32[40,1792]{1,0:T(8,128)}, f32[16,128]{1,0:T(8,128)}, /*index=5*/f32[8,1536]{1,0:T(8,128)}) custom-call(bf16[8,48,768]{2,1,0:T(8,128)(2,1)} %copy-done.25, bf16[8,24,1536]{2,1,0:T(8,128)(2,1)} %dynamic-slice_bitcast_fusion.2.sent_b, s32[1]{0:T(128)} %bitcast.refs_0_, ...), custom_call_target="tpu_custom_call" | custom-call | flops 46999998464 | bytes 50331648 | tf_op jit(solution)/shard_map/mixer_back/pallas_call | solution.py:717
  280.4 2.1 fusion.37
  282.8 1.5 collective-permute-start.17
  284.5 1.3 copy.87
  285.7 1.7 reshape.199
  287.5 2.0 fusion.36
  290.3 3.6 fusion.25
  293.9 1.9 fusion.22
  295.9 1.2 collective-permute-start.18
  297.7 3.5 fusion.19
  301.2 2.6 convolution_add_fusion
  304.4 2.5 collective-permute-start.20
  307.0 1.7 collective-permute-start.21
  308.6 1.2 fusion.3
  309.9 2.6 fusion.5
  312.4 3.1 collective-permute-done.20
  315.5 2.4 collective-permute-done.21
  318.1 3.2 collective-permute-start.32
  321.3 1.4 collective-permute-start.22
  323.3 2.2 collective-permute-start.33
  325.7 1.9 collective-permute-done.33
  327.6 1.4 collective-permute-start.34
  329.0 2.1 collective-permute-start.23
  331.7 2.0 collective-permute-start.35
  333.7 2.1 collective-permute-done.35
  336.4 9.4 %reduce-scatter.3.cloned.1.call-done = bf16[48,768]{1,0:T(8,128)(2,1)} async-done(((bf16[384,768]{1,0:T(8,128)(2,1)}), bf16[48,768]{1,0:T(8,128)(2,1)}) %reduce-scatter.3.cloned.1.call-update) | async-done | bytes 73744 | tf_op jit(solution)/shard_map/reduce_scatter | solution.py:766
  345.8 65.2 %reduce-scatter.5.cloned.1.call-done = bf16[24,1536]{1,0:T(8,128)(2,1)} async-done(((bf16[192,1536]{1,0:T(8,128)(2,1)}), bf16[24,1536]{1,0:T(8,128)(2,1)}) %reduce-scatter.5.cloned.1.call-update) | async-done | bytes 73744 | tf_op jit(solution)/shard_map/reduce_scatter | solution.py:766
  411.0 1.5 collective-permute-start.24
  413.0 1.4 collective-permute-start.26
  418.7 1.5 collective-permute-start.27
  420.4 5.7 %collective-permute-done.27 = bf16[24,1920]{1,0:T(8,128)(2,1)S(1)} collective-permute-done((bf16[24,1920]{1,0:T(8,128)(2,1)S(1)}, bf16[24,1920]{1,0:T(8,128)(2,1)S(1)}, u32[]{:S(2)}, u32[]{:S(2)}) %collective-permute-start.27) | collective-permute-done | bytes 92192 | tf_op jit(solution)/shard_map/ppermute | solution.py:368
  427.3 3.4 collective-permute-done.28
  430.9 1.5 multiply_subtract_fusion.1
  433.9 2.6 multiply_subtract_fusion
  (254 shorter events, 45.2 us)
Async XLA Ops:
  7.2 169.0 %all-gather.7.cloned.1.call-start = ((), (), s32[]{:S(2)}) async-start(), calls=%async_computation.4 | async-start | bytes 2211840 | tf_op jit(solution)/shard_map/all_gather | solution.py:593
  8.0 105.7 %collective-permute-start.8 = (bf16[16,768]{1,0:T(8,128)(2,1)S(1)}, bf16[16,768]{1,0:T(8,128)(2,1)S(1)}, u32[]{:S(2)}, u32[]{:S(2)}) collective-permute-start(bf16[16,768]{1,0:T(8,128)(2,1)S(1)} %slice_bitcast_fusion.1), channel_id=1, source_target_pairs={{0,1},{1,2},{2,3},{4,5},{5,6},{6,7},{8,9},{9,10},{10,11},{12,13},{... | collective-permute-start | bytes 73736 | tf_op jit(solution)/shard_map/ppermute | solution.py:540
  11.4 77.6 %collective-permute-start = (bf16[24,1920]{1,0:T(8,128)(2,1)S(1)}, bf16[24,1920]{1,0:T(8,128)(2,1)S(1)}, u32[]{:S(2)}, u32[]{:S(2)}) collective-permute-start(bf16[24,1920]{1,0:T(8,128)(2,1)S(1)} %pad.11), channel_id=1, source_target_pairs={{0,16},{4,20},{8,24},{12,28},{16,0},{20,4},{24,8},{28,12},{1,17},{... | collective-permute-start | bytes 276488 | tf_op jit(solution)/shard_map/ppermute | solution.py:368
  85.5 3.0 copy-start
  87.7 6.9 %copy-start.29 = (f32[1792,4]{0,1:T(4,128)}, f32[1792,4]{0,1:T(4,128)S(1)}, u32[]{:S(2)}) copy-start(f32[1792,4]{0,1:T(4,128)S(1)} %copy.73) | copy-start | bytes 86020
  89.0 5.6 %collective-permute-start.1 = (bf16[2,24,1920]{2,1,0:T(8,128)(2,1)S(1)}, bf16[2,24,1920]{2,1,0:T(8,128)(2,1)S(1)}, u32[]{:S(2)}, u32[]{:S(2)}) collective-permute-start(bf16[2,24,1920]{2,1,0:T(8,128)(2,1)S(1)} %pad_maximum_fusion.18), channel_id=1, source_target_pairs={{0,8},{4,12},{8,0},{12,4},{16,24},{20,28},{24,16},{28,20},{1,9},{5... | collective-permute-start | bytes 552968 | tf_op jit(solution)/shard_map/ppermute | solution.py:368
  94.7 5.5 %collective-permute-start.2 = (bf16[2,2,24,896]{3,2,1,0:T(8,128)(2,1)S(1)}, bf16[2,2,24,896]{3,2,1,0:T(8,128)(2,1)S(1)}, u32[]{:S(2)}, u32[]{:S(2)}) collective-permute-start(bf16[2,2,24,896]{3,2,1,0:T(8,128)(2,1)S(1)} %pad_maximum_fusion.20), channel_id=1, source_target_pairs={{0,4},{4,0},{8,12},{12,8},{16,20},{20,16},{24,28},{28,24},{1,5},{5... | collective-permute-start | bytes 516104 | tf_op jit(solution)/shard_map/ppermute | solution.py:368
  95.7 6.8 %collective-permute-start.5 = (bf16[2,2,24,1024]{3,2,1,0:T(8,128)(2,1)S(1)}, bf16[2,2,24,1024]{3,2,1,0:T(8,128)(2,1)S(1)}, u32[]{:S(2)}, u32[]{:S(2)}) collective-permute-start(bf16[2,2,24,1024]{3,2,1,0:T(8,128)(2,1)S(1)} %pad_maximum_fusion.17), channel_id=1, source_target_pairs={{0,2},{1,3},{2,0},{3,1},{4,6},{5,7},{6,4},{7,5},{8,10},{9,11},{10,... | collective-permute-start | bytes 589832 | tf_op jit(solution)/shard_map/ppermute | solution.py:368
  100.3 7.4 %collective-permute-start.3 = (bf16[2,2,2,24,896]{4,3,2,1,0:T(8,128)(2,1)S(1)}, bf16[2,2,2,24,896]{4,3,2,1,0:T(8,128)(2,1)S(1)}, u32[]{:S(2)}, u32[]{:S(2)}) collective-permute-start(bf16[2,2,2,24,896]{4,3,2,1,0:T(8,128)(2,1)S(1)} %pad_maximum_fusion.15), channel_id=1, source_target_pairs={{0,2},{1,3},{2,0},{3,1},{4,6},{5,7},{6,4},{7,5},{8,10},{9,11},{10,... | collective-permute-start | bytes 1032200 | tf_op jit(solution)/shard_map/ppermute | solution.py:368
  102.6 7.8 %collective-permute-start.6 = (bf16[2,2,2,24,1024]{4,3,1,0,2:T(8,128)(2,1)S(1)}, bf16[2,2,2,24,1024]{4,3,1,0,2:T(8,128)(2,1)S(1)}, u32[]{:S(2)}, u32[]{:S(2)}) collective-permute-start(bf16[2,2,2,24,1024]{4,3,1,0,2:T(8,128)(2,1)S(1)} %pad_maximum_fusion.12), channel_id=1, source_target_pairs={{0,4},{4,0},{8,12},{12,8},{16,20},{20,16},{24,28},{28,24},{1,5},{5... | collective-permute-start | bytes 1179656 | tf_op jit(solution)/shard_map/ppermute | solution.py:368
  108.7 5.1 %collective-permute-start.4 = (bf16[2,2,2,2,24,896]{5,4,3,2,1,0:T(8,128)(2,1)}, bf16[2,2,2,2,24,896]{5,4,3,2,1,0:T(8,128)(2,1)}, u32[]{:S(2)}, u32[]{:S(2)}) collective-permute-start(bf16[2,2,2,2,24,896]{5,4,3,2,1,0:T(8,128)(2,1)} %pad_maximum_fusion.10), channel_id=1, source_target_pairs={{0,1},{1,0},{2,3},{3,2},{4,5},{5,4},{6,7},{7,6},{8,9},{9,8},{10,11... | collective-permute-start | bytes 2064392 | tf_op jit(solution)/shard_map/ppermute | solution.py:368
  111.4 3.8 collective-permute-start.7
  115.2 7.2 %copy-start.18 = (bf16[2,2,2,2,2,24,896]{6,5,4,3,2,1,0:T(8,128)(2,1)}, bf16[2,2,2,2,2,24,896]{6,5,4,3,2,1,0:T(8,128)(2,1)S(1)}, u32[]{:S(2)}) copy-start(bf16[2,2,2,2,2,24,896]{6,5,4,3,2,1,0:T(8,128)(2,1)S(1)} %pad_maximum_fusion.6) | copy-start | bytes 4128772
  117.3 5.2 %copy-start.16 = (bf16[2,2,2,2,2,24,1024]{6,5,4,3,2,1,0:T(8,128)(2,1)}, bf16[2,2,2,2,2,24,1024]{6,5,4,3,2,1,0:T(8,128)(2,1)S(1)}, u32[]{:S(2)}) copy-start(bf16[2,2,2,2,2,24,1024]{6,5,4,3,2,1,0:T(8,128)(2,1)S(1)} %copy.72) | copy-start | bytes 4718596
  123.6 23.0 %collective-permute-start.9 = (bf16[8,24,1536]{2,1,0:T(8,128)(2,1)S(1)}, bf16[8,24,1536]{2,1,0:T(8,128)(2,1)S(1)}, u32[]{:S(2)}, u32[]{:S(2)}) collective-permute-start(bf16[8,24,1536]{2,1,0:T(8,128)(2,1)S(1)} %bitcast.223), channel_id=1, source_target_pairs={{0,2},{1,3},{2,0},{3,1},{4,6},{5,7},{6,4},{7,5},{8,10},{9,11},{10,... | collective-permute-start | bytes 1769480 | tf_op jit(solution)/shard_map/ppermute | solution.py:368
  124.7 27.3 %collective-permute-start.10 = (bf16[8,48,768]{2,1,0:T(8,128)(2,1)S(1)}, bf16[8,48,768]{2,1,0:T(8,128)(2,1)S(1)}, u32[]{:S(2)}, u32[]{:S(2)}) collective-permute-start(bf16[8,48,768]{2,1,0:T(8,128)(2,1)S(1)} %bitcast.225), channel_id=1, source_target_pairs={{0,2},{1,3},{2,0},{3,1},{4,6},{5,7},{6,4},{7,5},{8,10},{9,11},{10,... | collective-permute-start | bytes 1769480 | tf_op jit(solution)/shard_map/ppermute | solution.py:368
  153.4 12.4 %collective-permute-start.11 = (bf16[8,2,24,1536]{3,2,1,0:T(8,128)(2,1)}, bf16[8,2,24,1536]{3,2,1,0:T(8,128)(2,1)}, u32[]{:S(2)}, u32[]{:S(2)}) collective-permute-start(bf16[8,2,24,1536]{3,2,1,0:T(8,128)(2,1)} %pad_maximum_fusion.7), channel_id=1, source_target_pairs={{0,1},{1,0},{2,3},{3,2},{4,5},{5,4},{6,7},{7,6},{8,9},{9,8},{10,11... | collective-permute-start | bytes 3538952 | tf_op jit(solution)/shard_map/ppermute | solution.py:368
  154.5 11.3 %collective-permute-start.12 = (bf16[8,2,48,768]{3,2,1,0:T(8,128)(2,1)}, bf16[8,2,48,768]{3,2,1,0:T(8,128)(2,1)}, u32[]{:S(2)}, u32[]{:S(2)}) collective-permute-start(bf16[8,2,48,768]{3,2,1,0:T(8,128)(2,1)} %pad_maximum_fusion.8), channel_id=1, source_target_pairs={{0,1},{1,0},{2,3},{3,2},{4,5},{5,4},{6,7},{7,6},{8,9},{9,8},{10,11... | collective-permute-start | bytes 3538952 | tf_op jit(solution)/shard_map/ppermute | solution.py:368
  155.7 84.1 %all-gather.9.cloned.1.call-start = ((), (), s32[]{:S(2)}) async-start(), calls=%async_computation.5 | async-start | bytes 1966080 | tf_op jit(solution)/shard_map/all_gather | solution.py:659
  155.9 9.8 %copy-start.3 = (bf16[8,1,48,768]{3,2,1,0:T(8,128)(2,1)S(1)}, bf16[8,1,48,768]{3,2,1,0:T(8,128)(2,1)}, u32[]{:S(2)}) copy-start(bf16[8,1,48,768]{3,2,1,0:T(8,128)(2,1)} %copy-done.2) | copy-start | bytes 1769476
  176.2 26.2 %copy-start.14 = (bf16[1,1024,768]{2,1,0:T(8,128)(2,1)S(1)}, bf16[1,1024,768]{2,1,0:T(8,128)(2,1)}, u32[]{:S(2)}) copy-start(bf16[1,1024,768]{2,1,0:T(8,128)(2,1)} %param.12) | copy-start | bytes 4718596
  207.2 3.0 copy-start.1
  209.3 20.0 %collective-permute-start.13 = (bf16[8,2,48,768]{3,2,0,1:T(8,128)(2,1)}, bf16[8,2,48,768]{3,2,0,1:T(8,128)(2,1)}, u32[]{:S(2)}, u32[]{:S(2)}) collective-permute-start(bf16[8,2,48,768]{3,2,0,1:T(8,128)(2,1)} %bitcast.216), channel_id=1, source_target_pairs={{0,1},{1,0},{2,3},{3,2},{4,5},{5,4},{6,7},{7,6},{8,9},{9,8},{10,11... | collective-permute-start | bytes 3538952 | tf_op jit(solution)/shard_map/ppermute | solution.py:368
  216.5 12.7 %collective-permute-start.14 = (bf16[8,2,24,1536]{3,2,0,1:T(8,128)(2,1)}, bf16[8,2,24,1536]{3,2,0,1:T(8,128)(2,1)}, u32[]{:S(2)}, u32[]{:S(2)}) collective-permute-start(bf16[8,2,24,1536]{3,2,0,1:T(8,128)(2,1)} %bitcast.215), channel_id=1, source_target_pairs={{0,1},{1,0},{2,3},{3,2},{4,5},{5,4},{6,7},{7,6},{8,9},{9,8},{10,11... | collective-permute-start | bytes 3538952 | tf_op jit(solution)/shard_map/ppermute | solution.py:368
  218.4 127.4 %reduce-scatter.3.cloned.1.call-start = ((), (), s32[]{:S(2)}) async-start(), calls=%async_computation.2 | async-start | bytes 663552 | tf_op jit(solution)/shard_map/reduce_scatter | solution.py:766
  229.3 3.0 copy-start.4
  231.0 49.3 %collective-permute-start.15 = (bf16[8,48,768]{2,1,0:T(8,128)(2,1)S(1)}, bf16[8,48,768]{2,1,0:T(8,128)(2,1)}, u32[]{:S(2)}, u32[]{:S(2)}) collective-permute-start(bf16[8,48,768]{2,1,0:T(8,128)(2,1)S(1)} %dynamic-slice_bitcast_fusion.3.sent_a), channel_id=1, source_target_pairs={{0,2},{1,3},{2,0},{3,1},{4,6},{5,7},{6,4},{7,5},{8,10},{9,11},{10,... | collective-permute-start | bytes 1769480 | tf_op jit(solution)/shard_map/ppermute | solution.py:368
  234.7 45.7 %collective-permute-start.16 = (bf16[8,24,1536]{2,1,0:T(8,128)(2,1)}, bf16[8,24,1536]{2,1,0:T(8,128)(2,1)}, u32[]{:S(2)}, u32[]{:S(2)}) collective-permute-start(bf16[8,24,1536]{2,1,0:T(8,128)(2,1)} %dynamic-slice_bitcast_fusion.2.sent_b), channel_id=1, source_target_pairs={{0,2},{1,3},{2,0},{3,1},{4,6},{5,7},{6,4},{7,5},{8,10},{9,11},{10,... | collective-permute-start | bytes 1769480 | tf_op jit(solution)/shard_map/ppermute | solution.py:368
  239.8 40.5 %copy-start.6 = (bf16[8,2,48,768]{3,2,0,1:T(8,128)(2,1)S(1)}, bf16[8,2,48,768]{3,2,0,1:T(8,128)(2,1)}, u32[]{:S(2)}) copy-start(bf16[8,2,48,768]{3,2,0,1:T(8,128)(2,1)} %copy-done.5) | copy-start | bytes 3538948
  280.3 4.0 copy-start.28
  282.5 128.5 %reduce-scatter.5.cloned.1.call-start = ((), (), s32[]{:S(2)}) async-start(), calls=%async_computation.3 | async-start | bytes 663552 | tf_op jit(solution)/shard_map/reduce_scatter | solution.py:766
  282.8 6.8 %collective-permute-start.17 = (f32[8,1792]{1,0:T(8,128)S(1)}, f32[8,1792]{1,0:T(8,128)S(1)}, u32[]{:S(2)}, u32[]{:S(2)}) collective-permute-start(f32[8,1792]{1,0:T(8,128)S(1)} %copy-done.41), channel_id=1, source_target_pairs={{1,0},{2,1},{3,2},{5,4},{6,5},{7,6},{9,8},{10,9},{11,10},{13,12},{... | collective-permute-start | bytes 172040 | tf_op jit(solution)/shard_map/ppermute | solution.py:755
  285.7 3.8 copy-start.39
  285.7 3.8 copy-start.30
  285.7 3.9 copy-start.32
  290.3 3.6 copy-start.40
  295.9 7.9 %collective-permute-start.18 = (bf16[2,2,2,2,24,896]{5,4,3,2,1,0:T(8,128)(2,1)S(1)}, bf16[2,2,2,2,24,896]{5,4,3,2,1,0:T(8,128)(2,1)S(1)}, u32[]{:S(2)}, u32[]{:S(2)}) collective-permute-start(bf16[2,2,2,2,24,896]{5,4,3,2,1,0:T(8,128)(2,1)S(1)} %dynamic-slice_bitcast_fusion.1), channel_id=1, source_target_pairs={{0,1},{1,0},{2,3},{3,2},{4,5},{5,4},{6,7},{7,6},{8,9},{9,8},{10,11... | collective-permute-start | bytes 2064392 | tf_op jit(solution)/shard_map/ppermute | solution.py:368
  297.2 4.0 copy-start.12
  297.2 4.0 copy-start.43
  297.2 6.6 %collective-permute-start.19 = (bf16[2,2,2,2,24,1024]{5,4,3,2,1,0:T(8,128)(2,1)S(1)}, bf16[2,2,2,2,24,1024]{5,4,3,2,1,0:T(8,128)(2,1)S(1)}, u32[]{:S(2)}, u32[]{:S(2)}) collective-permute-start(bf16[2,2,2,2,24,1024]{5,4,3,2,1,0:T(8,128)(2,1)S(1)} %dynamic-slice_bitcast_fusion), channel_id=1, source_target_pairs={{0,1},{1,0},{2,3},{3,2},{4,5},{5,4},{6,7},{7,6},{8,9},{9,8},{10,11... | collective-permute-start | bytes 2359304 | tf_op jit(solution)/shard_map/ppermute | solution.py:368
  304.4 11.1 %collective-permute-start.20 = (bf16[2,2,2,24,896]{4,3,2,1,0:T(8,128)(2,1)S(1)}, bf16[2,2,2,24,896]{4,3,2,1,0:T(8,128)(2,1)S(1)}, u32[]{:S(2)}, u32[]{:S(2)}) collective-permute-start(bf16[2,2,2,24,896]{4,3,2,1,0:T(8,128)(2,1)S(1)} %dynamic-slice_bitcast_fusion.5), channel_id=1, source_target_pairs={{0,2},{1,3},{2,0},{3,1},{4,6},{5,7},{6,4},{7,5},{8,10},{9,11},{10,... | collective-permute-start | bytes 1032200 | tf_op jit(solution)/shard_map/ppermute | solution.py:368
  306.9 2.9 copy-start.15
  307.0 10.9 %collective-permute-start.21 = (bf16[2,2,2,24,1024]{4,3,2,1,0:T(8,128)(2,1)S(1)}, bf16[2,2,2,24,1024]{4,3,2,1,0:T(8,128)(2,1)S(1)}, u32[]{:S(2)}, u32[]{:S(2)}) collective-permute-start(bf16[2,2,2,24,1024]{4,3,2,1,0:T(8,128)(2,1)S(1)} %dynamic-slice_bitcast_fusion.4), channel_id=1, source_target_pairs={{0,4},{4,0},{8,12},{12,8},{16,20},{20,16},{24,28},{28,24},{1,5},{5... | collective-permute-start | bytes 1179656 | tf_op jit(solution)/shard_map/ppermute | solution.py:368
  318.1 5.3 %collective-permute-start.32 = (f32[11336]{0:T(1024)S(1)}, f32[11336]{0:T(1024)S(1)}, u32[]{:S(2)}, u32[]{:S(2)}) collective-permute-start(f32[11336]{0:T(1024)S(1)} %concatenate.49), channel_id=1, source_target_pairs={{0,16},{4,20},{8,24},{12,28},{16,0},{20,4},{24,8},{28,12},{1,17},{... | collective-permute-start | bytes 136040 | tf_op jit(solution)/shard_map/ppermute | solution.py:368
  321.3 12.4 %collective-permute-start.22 = (bf16[2,2,24,896]{3,2,1,0:T(8,128)(2,1)S(1)}, bf16[2,2,24,896]{3,2,1,0:T(8,128)(2,1)S(1)}, u32[]{:S(2)}, u32[]{:S(2)}) collective-permute-start(bf16[2,2,24,896]{3,2,1,0:T(8,128)(2,1)S(1)} %dynamic-slice_bitcast_fusion.8), channel_id=1, source_target_pairs={{0,4},{4,0},{8,12},{12,8},{16,20},{20,16},{24,28},{28,24},{1,5},{5... | collective-permute-start | bytes 516104 | tf_op jit(solution)/shard_map/ppermute | solution.py:368
  323.3 4.2 collective-permute-start.33
  325.6 88.8 %copy-start.31 = (f32[11336]{0:T(1024)S(1)}, f32[11336]{0:T(1024)}, u32[]{:S(2)}) copy-start(f32[11336]{0:T(1024)} %param.19) | copy-start | bytes 136036
  325.7 88.8 %copy-start.33 = (f32[11336]{0:T(1024)S(1)}, f32[11336]{0:T(1024)}, u32[]{:S(2)}) copy-start(f32[11336]{0:T(1024)} %param.20) | copy-start | bytes 136036
  325.7 88.8 %copy-start.34 = (f32[11336]{0:T(1024)S(1)}, f32[11336]{0:T(1024)}, u32[]{:S(2)}) copy-start(f32[11336]{0:T(1024)} %param.21) | copy-start | bytes 136036
  327.6 4.2 collective-permute-start.34
  329.0 7.2 %collective-permute-start.23 = (bf16[2,2,24,1024]{3,2,1,0:T(8,128)(2,1)S(1)}, bf16[2,2,24,1024]{3,2,1,0:T(8,128)(2,1)S(1)}, u32[]{:S(2)}, u32[]{:S(2)}) collective-permute-start(bf16[2,2,24,1024]{3,2,1,0:T(8,128)(2,1)S(1)} %dynamic-slice_bitcast_fusion.6), channel_id=1, source_target_pairs={{0,2},{1,3},{2,0},{3,1},{4,6},{5,7},{6,4},{7,5},{8,10},{9,11},{10,... | collective-permute-start | bytes 589832 | tf_op jit(solution)/shard_map/ppermute | solution.py:368
  331.7 4.2 collective-permute-start.35
  335.9 78.5 %collective-permute-start.36 = (f32[11336]{0:T(1024)S(1)}, f32[11336]{0:T(1024)S(1)}, u32[]{:S(2)}, u32[]{:S(2)}) collective-permute-start(f32[11336]{0:T(1024)S(1)} %add.264), channel_id=1, source_target_pairs={{0,1},{1,0},{2,3},{3,2},{4,5},{5,4},{6,7},{7,6},{8,9},{9,8},{10,11... | collective-permute-start | bytes 136040 | tf_op jit(solution)/shard_map/ppermute | solution.py:368
  411.0 4.6 %collective-permute-start.24 = (bf16[24,1536]{1,0:T(8,128)(2,1)}, bf16[24,1536]{1,0:T(8,128)(2,1)S(1)}, u32[]{:S(2)}, u32[]{:S(2)}) collective-permute-start(bf16[24,1536]{1,0:T(8,128)(2,1)} %reduce-scatter.5.cloned.1.call-done), channel_id=1, source_target_pairs={{0,2},{1,3},{2,0},{3,1},{4,6},{5,7},{6,4},{7,5},{8,10},{9,11},{10,... | collective-permute-start | bytes 221192 | tf_op jit(solution)/shard_map/ppermute | solution.py:368
  412.5 4.6 %collective-permute-start.30 = (bf16[48,768]{1,0:T(8,128)(2,1)}, bf16[48,768]{1,0:T(8,128)(2,1)S(1)}, u32[]{:S(2)}, u32[]{:S(2)}) collective-permute-start(bf16[48,768]{1,0:T(8,128)(2,1)} %reduce-scatter.3.cloned.1.call-done), channel_id=1, source_target_pairs={{0,2},{1,3},{2,0},{3,1},{4,6},{5,7},{6,4},{7,5},{8,10},{9,11},{10,... | collective-permute-start | bytes 221192 | tf_op jit(solution)/shard_map/ppermute | solution.py:368
  413.0 5.6 %collective-permute-start.26 = (bf16[2,24,1920]{2,1,0:T(8,128)(2,1)S(1)}, bf16[2,24,1920]{2,1,0:T(8,128)(2,1)S(1)}, u32[]{:S(2)}, u32[]{:S(2)}) collective-permute-start(bf16[2,24,1920]{2,1,0:T(8,128)(2,1)S(1)} %dynamic-slice_bitcast_fusion.7), channel_id=1, source_target_pairs={{0,8},{4,12},{8,0},{12,4},{16,24},{20,28},{24,16},{28,20},{1,9},{5... | collective-permute-start | bytes 552968 | tf_op jit(solution)/shard_map/ppermute | solution.py:368
  416.5 3.7 collective-permute-start.25
  417.9 2.3 collective-permute-start.31
  418.7 7.4 %collective-permute-start.27 = (bf16[24,1920]{1,0:T(8,128)(2,1)S(1)}, bf16[24,1920]{1,0:T(8,128)(2,1)S(1)}, u32[]{:S(2)}, u32[]{:S(2)}) collective-permute-start(bf16[24,1920]{1,0:T(8,128)(2,1)S(1)} %dynamic-slice_bitcast_fusion.9), channel_id=1, source_target_pairs={{0,16},{4,20},{8,24},{12,28},{16,0},{20,4},{24,8},{28,12},{1,17},{... | collective-permute-start | bytes 276488 | tf_op jit(solution)/shard_map/ppermute | solution.py:368
  420.4 10.5 %copy-start.24 = (f32[192,768]{1,0:T(8,128)S(1)}, f32[192,768]{1,0:T(8,128)}, u32[]{:S(2)}) copy-start(f32[192,768]{1,0:T(8,128)} %param.16) | copy-start | bytes 1769476
  420.4 10.5 %copy-start.26 = (f32[192,768]{1,0:T(8,128)S(1)}, f32[192,768]{1,0:T(8,128)}, u32[]{:S(2)}) copy-start(f32[192,768]{1,0:T(8,128)} %param.17) | copy-start | bytes 1769476
  420.4 10.5 %copy-start.27 = (f32[192,768]{1,0:T(8,128)S(1)}, f32[192,768]{1,0:T(8,128)}, u32[]{:S(2)}) copy-start(f32[192,768]{1,0:T(8,128)} %param.18) | copy-start | bytes 1769476
  426.1 4.6 %collective-permute-start.28 = (bf16[24,1920]{1,0:T(8,128)(2,1)S(1)}, bf16[24,1920]{1,0:T(8,128)(2,1)S(1)}, u32[]{:S(2)}, u32[]{:S(2)}) collective-permute-start(bf16[24,1920]{1,0:T(8,128)(2,1)S(1)} %fusion.45), channel_id=1, source_target_pairs={{0,2},{1,3},{2,0},{3,1},{4,6},{5,7},{6,4},{7,5},{8,10},{9,11},{10,... | collective-permute-start | bytes 276488 | tf_op jit(solution)/shard_map/ppermute | solution.py:368
  430.8 1.6 collective-permute-start.29
  (21 other events, 40.9 us)
Sparse Core Ops, SparseCore 0:
  155.8 19.5 all-gather.6
  218.5 21.2 all-gather.8
  282.6 63.1 reduce-scatter.2
  349.9 61.0 reduce-scatter.4

commit v4 on v3

--- a/solution.py
+++ b/solution.py
@@ -51,10 +51,6 @@
     return lax.dot_general(a, b, TN, preferred_element_type=f32)
 
 
-def dot_full(a, b):
-    return jnp.dot(a, b, preferred_element_type=f32, precision=lax.Precision.HIGHEST)
-
-
 def sigmoid(v):
     return 0.5 * jnp.tanh(0.5 * v) + 0.5
 
@@ -62,6 +58,13 @@
 def halves(v):
     high = v.astype(bf16)
     return high, (v - high.astype(f32)).astype(bf16)
+
+
+def running(mask, v):
+    high, rest = halves(v)
+    left = (v - high.astype(f32) - rest.astype(f32)).astype(bf16)
+    parts = dot(jnp.where(mask, 1.0, 0.0).astype(bf16), jnp.concatenate([high, rest, left], axis=1))
+    return parts[:, :LANES] + parts[:, LANES : 2 * LANES] + parts[:, 2 * LANES :]
 
 
 def expand(v, spread):
@@ -121,13 +124,15 @@
     raw = proj[:, XBC:].astype(f32) + headp[0:1, :]
     steps = jnp.maximum(raw, 0.0) + jnp.log1p(jnp.exp(-jnp.abs(raw)))
     log_decay = steps * (headp[1:2, :] * (-LOG2E))
-    cum = dot_full(jnp.where(tri(True), 1.0, 0.0), log_decay)
+    cum = running(tri(True), log_decay)
     cum_out[...] = cum
     cumt_out[...] = jnp.transpose(cum)[0:32, :]
     dt_out[...] = steps
     last = cum[CHUNK - 1 : CHUNK, :]
-    steps_wide = expand(steps, spread[...])
-    tail_wide = expand(jnp.exp2(last - cum), spread[...])
+    decayed = jnp.broadcast_to(jnp.exp2(last), (8, LANES))
+    wide = expand(jnp.concatenate([steps, jnp.exp2(last - cum), decayed], axis=0), spread[...])
+    steps_wide, tail_wide = wide[:CHUNK], wide[CHUNK : 2 * CHUNK]
+    decay = wide[2 * CHUNK : 2 * CHUNK + 1]
     for tile in range(TILES):
         pre, _ = conv_pre(ext, convp, tile)
         value = (pre * sigmoid(pre)).astype(bf16)
@@ -138,7 +143,6 @@
             scaled[:, lane(tile)] = (u.astype(f32) * tail_wide[:, lane(tile)]).astype(bf16)
         else:
             bc_out[:, lane(tile - PAIRS)] = value
-    decay = expand(jnp.broadcast_to(jnp.exp2(last), (8, LANES)), spread[...])[0:1, :]
     new_state = state[...] * decay + dot_tn(bc_out[:, :STATE], scaled[...])
     state[...] = new_state
     hst_out[0] = new_state
@@ -204,10 +208,10 @@
         glocal_out[...] = jnp.zeros_like(glocal_out)
         ng_out[...] = jnp.zeros_like(ng_out)
 
-    start = expand(jnp.exp2(prefix[...]), spread[...])[0:1, :]
+    wide = expand(jnp.exp2(jnp.concatenate([cum[...], prefix[...]], axis=0)), spread[...])
+    grown, start = wide[:CHUNK], wide[CHUNK : CHUNK + 1]
     state = h0[...] * start + jnp.where(step > 0, hst[0], 0.0)
     state_low = state.astype(bf16)
-    grown = expand(jnp.exp2(cum[...]), spread[...])
     carried = dot(bc[:, STATE:], state_low)
     hg_all[...] = dot_nt(cot[...], wout[...])
     squares = jnp.zeros((CHUNK, LANES), f32)
@@ -273,7 +277,7 @@
     groups, rank, dxs, dy, x, u, y, bc, dbc, dcc, cum, dt, hst, pfx, h0, gathered, logs, ust, proj,
     before, halo, convp, headp, spread, collect, rows,
     pg_out, first_out, tail_out, wg_out, hg_out, skip_out,
-    gstate, ext, dext, scaled, prod_q, prod_p,
+    gstate, ext, dext, scaled, prod,
 ):
     step = pl.program_id(0)
     chunk = pl.num_programs(0) - 1 - step
@@ -302,8 +306,14 @@
     grad_state = gstate[...]
     grad_low = grad_state.astype(bf16)
     last = cum[CHUNK - 1 : CHUNK, :]
-    tail_wide = expand(jnp.exp2(last - cum[...]), spread[...])
-    steps_wide = expand(dt[...], spread[...])
+    decayed = jnp.broadcast_to(jnp.exp2(last), (8, LANES))
+    wide = expand(
+        jnp.concatenate([jnp.exp2(last - cum[...]), dt[...], decayed, jnp.exp2(pfx[0])], axis=0),
+        spread[...],
+    )
+    tail_wide, steps_wide = wide[:CHUNK], wide[CHUNK : 2 * CHUNK]
+    decay = wide[2 * CHUNK : 2 * CHUNK + 1]
+    end = wide[2 * CHUNK + 8 : 2 * CHUNK + 9]
     reach = dot(bc[:, :STATE], grad_low)
 
     def conv_back(tile, grad):
@@ -332,26 +342,26 @@
         scaled[:, cols] = (uf * tail_wide[:, cols]).astype(bf16)
         q = uf * dxs_full
         high, rest = halves(q)
-        prod_q[:, cols] = high
-        prod_q[:, INNER + tile * LANES : INNER + (tile + 1) * LANES] = rest
+        prod[:CHUNK, cols] = high
+        prod[:CHUNK, INNER + tile * LANES : INNER + (tile + 1) * LANES] = rest
         high, rest = halves(dyf * y[:, cols] - q)
-        prod_p[:, cols] = high
-        prod_p[:, INNER + tile * LANES : INNER + (tile + 1) * LANES] = rest
+        prod[CHUNK : 2 * CHUNK, cols] = high
+        prod[CHUNK : 2 * CHUNK, INNER + tile * LANES : INNER + (tile + 1) * LANES] = rest
         skip_out[:, cols] += fold(dyf * x[:, cols].astype(f32))
         conv_back(tile, rows[1:2, cols] * dyf + steps_wide[:, cols] * dxs_full)
     conv_back(PAIRS, dbc[:, :STATE] + dot_nt(scaled[...], grad_low))
     conv_back(PAIRS + 1, dbc[:, STATE:] + dcc[...])
     first_out[...] = dext[0:8, :]
 
-    q_heads = dot(prod_q[...], collect[...])
-    gap_heads = dot(prod_p[...], collect[...])
-    end = expand(jnp.exp2(pfx[0]), spread[...])[0:1, :]
     meet = fold(grad_state * (hst[0] + h0[...] * end))
-    meet_high, meet_rest = halves(meet)
-    meet_heads = jnp.sum(
-        dot(jnp.concatenate([meet_high, meet_rest], axis=1), collect[...]), axis=0, keepdims=True
-    )
-    dlog = dot_full(jnp.where(tri(False), 1.0, 0.0), gap_heads) + meet_heads
+    meet = jnp.concatenate([meet, jnp.zeros_like(meet)], axis=0)
+    high, rest = halves(meet)
+    prod[2 * CHUNK :, :INNER] = high
+    prod[2 * CHUNK :, INNER:] = rest
+    heads = dot(prod[...], collect[...])
+    q_heads, gap_heads = heads[:CHUNK], heads[CHUNK : 2 * CHUNK]
+    meet_heads = jnp.sum(heads[2 * CHUNK :], axis=0, keepdims=True)
+    dlog = running(tri(False), gap_heads) + meet_heads
     sig = sigmoid(proj[:, XBC:].astype(f32) + headp[0:1, :])
     steps = dt[...]
     ratio = jnp.where(steps > 1e-30, sig / jnp.maximum(steps, 1e-30), 1.0)
@@ -359,7 +369,6 @@
     pg_out[:, XBC:] = raw_grad.astype(bf16)
     hg_out[0:8, :] += fold(raw_grad)
     hg_out[8:16, :] += fold(dlog * steps * headp[1:2, :]) * (-1.0)
-    decay = expand(jnp.broadcast_to(jnp.exp2(last), (8, LANES)), spread[...])[0:1, :]
     gstate[...] = grad_state * decay + ust[0]
 
 
@@ -399,18 +408,8 @@
     return v.reshape(-1, v.shape[-1])
 
 
-def gather_crossed(v, bits):
-    cross = len(bits) - 3
-    v = gather_pairs(v, bits[:cross])
-    half = v.shape[-1] // 256 * 128
-    left, right = v[..., :half], v[..., half:]
-    left = gather_step(left, cross, *bits[cross])
-    right = gather_step(right, cross, *bits[cross + 1])
-    left = gather_step(left, cross + 1, *bits[cross + 1])
-    right = gather_step(right, cross, *bits[cross])
-    left = gather_step(left, cross + 2, *bits[cross + 2])
-    right = gather_step(right, cross + 2, *bits[cross + 2])
-    return jnp.concatenate([flat(left), flat(right)], axis=1)
+def blocks(v, bits):
+    return v.reshape((2,) * len(bits) + (v.shape[0] >> len(bits), v.shape[1]))
 
 
 def split_pair(v, place, axis, bit):
@@ -427,6 +426,12 @@
 def scatter_step(v, place, axis, bit):
     keep, give = split_pair(v, place, axis, bit)
     return add_low(keep, swap(give, axis, bit))
+
+
+def scatter_pairs(v, bits, lead=0):
+    for place in reversed(range(len(bits))):
+        v = scatter_step(v, lead + place, *bits[place])
+    return v
 
 
 def sum_pairs(v, bits):
@@ -527,13 +532,34 @@
 
     in_part = quarter(in_weight)
     side_part = jnp.pad(in_part[:, INNER:], ((0, 0), (0, SIDE + INNER - PROJ)))
-    full_side = gather_crossed(side_part, bits)
-
-    beside = [
-        lax.all_gather(part, "dp", axis=0, tiled=False)
-        for part in (in_part[:, :INNER], quarter(out_weight))
-    ]
-    (y_axis, y_bit), (core_axis, core_bit) = seq_bits
+    out_rows = out_weight.shape[0] // groups
+    in_rows = in_weight.shape[0] // groups
+    beside = jnp.concatenate(
+        [quarter(out_weight), in_part[:, :D], in_part[:, D:INNER]], axis=0
+    )
+    barrier = lax.optimization_barrier
+    cross = len(bits) - 3
+    (x_axis, x_bit), (y_axis, y_bit), (core_axis, core_bit) = bits[cross:]
+    side = gather_pairs(side_part, bits[:cross])
+    side, beside = barrier((side, beside))
+    half = SIDE // 256 * 128
+    left, right = side[..., :half], side[..., half:]
+    got_l, got_r = swap(left, x_axis, x_bit), swap(right, y_axis, y_bit)
+    early = cross // 2
+    beside = gather_pairs(beside, bits[:early])
+    got_l, got_r, beside = barrier((got_l, got_r, beside))
+    left = merge_pair(left, got_l, cross, x_axis, x_bit)
+    right = merge_pair(right, got_r, cross, y_axis, y_bit)
+    got_l, got_r = swap(left, y_axis, y_bit), swap(right, x_axis, x_bit)
+    beside = gather_pairs(beside, bits[early:cross], early)
+    got_l, got_r, beside = barrier((got_l, got_r, beside))
+    left = merge_pair(left, got_l, cross + 1, y_axis, y_bit)
+    right = merge_pair(right, got_r, cross, x_axis, x_bit)
+    got_l, got_r = swap(left, core_axis, core_bit), swap(right, core_axis, core_bit)
+    got_b = swap(beside, x_axis, x_bit)
+    left = merge_pair(left, got_l, cross + 2, core_axis, core_bit)
+    right = merge_pair(right, got_r, cross + 2, core_axis, core_bit)
+    full_side = jnp.concatenate([flat(left), flat(right)], axis=1)
 
     forward = [(s, s + 1) for s in range(groups - 1)]
     backward = [(s + 1, s) for s in range(groups - 1)]
@@ -558,8 +584,9 @@
 
     proj = dot(normed_low, full_side).astype(bf16)
     halo = dot(halo_norm, full_side[:, :XBC]).astype(bf16)
-    proj, halo, beside = lax.optimization_barrier((proj, halo, beside))
-    others = [swap(part, y_axis, y_bit) for part in beside]
+    proj, halo, got_b = barrier((proj, halo, got_b))
+    beside = merge_pair(beside, got_b, cross, x_axis, x_bit)
+    got_b = swap(beside, y_axis, y_bit)
 
     x, bc, u, cum, cumt, dt, hst, pfx, send = pl.pallas_call(
         conv_state_kernel,
@@ -591,11 +618,11 @@
     )(proj, halo, convp, headp, spread)
 
     states = lax.all_gather(send, "seq", axis=0, tiled=False)
-    (x, bc, u, cum, cumt, dt, hst, pfx), others = lax.optimization_barrier(
-        ((x, bc, u, cum, cumt, dt, hst, pfx), others)
-    )
-    beside = [merge_pair(part, other, 1, y_axis, y_bit) for part, other in zip(beside, others)]
-    others = [swap(part, core_axis, core_bit) for part in beside]
+    x, bc, u, cum, cumt, dt, hst, pfx, got_b = barrier(
+        (x, bc, u, cum, cumt, dt, hst, pfx, got_b)
+    )
+    beside = merge_pair(beside, got_b, cross + 1, y_axis, y_bit)
+    got_b = swap(beside, core_axis, core_bit)
 
     y_within = pl.pallas_call(
         within_kernel,
@@ -610,10 +637,16 @@
         cost_estimate=cost(11 * 10**9, 16 * 2**20),
         name="within",
     )(u, bc, cum, cumt)
-    y_within, others = lax.optimization_barrier((y_within, others))
-    full_gate, full_out = [
-        flat(merge_pair(part, other, 2, core_axis, core_bit)) for part, other in zip(beside, others)
-    ]
+    y_within, got_b = barrier((y_within, got_b))
+    beside = merge_pair(beside, got_b, cross + 2, core_axis, core_bit)
+    full_out = flat(beside[..., :out_rows, :])
+    full_gate = jnp.concatenate(
+        [
+            flat(beside[..., out_rows : out_rows + in_rows, :]),
+            flat(beside[..., out_rows + in_rows :, :]),
+        ],
+        axis=1,
+    )
     gate = dot(normed_low, full_gate).astype(bf16)
 
     gathered_spec = full((groups, STATE, INNER))
@@ -661,24 +694,19 @@
     def product(left, right):
         return lax.dot_general(left, right, TN, preferred_element_type=f32).astype(bf16)
 
-    def blocks(v, cut):
-        return v.reshape((2,) * len(cut) + (v.shape[0] >> len(cut), v.shape[1]))
-
-    dp_size = lax.axis_size("dp")
-
-    def by_owner(v):
-        return v.reshape(dp_size, 2, 2, v.shape[0] // (4 * dp_size), v.shape[1])
-
-    keeps, gives = zip(
-        *[
-            split_pair(by_owner(product(left, right)), 2, core_axis, core_bit)
-            for left, right in ((hidden, cot_low), (normed_low, dgate))
-        ]
-    )
-    first_got = [swap(give, core_axis, core_bit) for give in gives]
+    beside = jnp.concatenate(
+        [
+            blocks(product(hidden, cot_low), bits),
+            blocks(product(normed_low, dgate[:, :D]), bits),
+            blocks(product(normed_low, dgate[:, D:]), bits),
+        ],
+        axis=-2,
+    )
+    keep_b, give_b = split_pair(beside, cross + 2, core_axis, core_bit)
+    got_b = swap(give_b, core_axis, core_bit)
     anywhere = pl.BlockSpec(memory_space=pl.ANY)
 
-    def within_back_call(u, dy, bc, cum, cumt, sent_a, sent_b, dxs_out, dbc_out):
+    def within_back_call(u, dy, bc, cum, cumt, sent, dxs_out, dbc_out):
         within_back_kernel(u, dy, bc, cum, cumt, dxs_out, dbc_out)
 
     dxs, dbc = pl.pallas_call(
@@ -686,23 +714,18 @@
         grid=(chunks,),
         in_specs=[
             by_chunk(INNER), by_chunk(INNER), by_chunk(2 * STATE), by_chunk(LANES),
-            pl.BlockSpec((32, CHUNK), lambda c: (0, c)), anywhere, anywhere,
+            pl.BlockSpec((32, CHUNK), lambda c: (0, c)), anywhere,
         ],
         out_specs=[by_chunk(INNER), by_chunk(2 * STATE)],
         out_shape=[shape((count, INNER), f32), shape((count, 2 * STATE), f32)],
         compiler_params=params(),
         cost_estimate=cost(12 * 10**9, 16 * 2**20),
         name="within_back",
-    )(u, dy, bc, cum, cumt, *gives)
-
-    halves_got, dxs, dbc = lax.optimization_barrier((first_got, dxs, dbc))
-    keeps, gives = zip(
-        *[
-            split_pair(add_low(keep, got), 1, y_axis, y_bit)
-            for keep, got in zip(keeps, halves_got)
-        ]
-    )
-    second_got = [swap(give, y_axis, y_bit) for give in gives]
+    )(u, dy, bc, cum, cumt, give_b)
+
+    got_b, dxs, dbc = barrier((got_b, dxs, dbc))
+    keep_b, give_b = split_pair(add_low(keep_b, got_b), cross + 1, y_axis, y_bit)
+    got_b = swap(give_b, y_axis, y_bit)
 
     def back(width, height=CHUNK):
         return pl.BlockSpec((height, width), lambda c: (chunks - 1 - c, 0))
@@ -710,7 +733,7 @@
     def back_three(height):
         return pl.BlockSpec((1, height, INNER), lambda c: (chunks - 1 - c, 0, 0))
 
-    def back_call(sent_a, sent_b, *refs):
+    def back_call(sent, *refs):
         back_kernel(groups, *refs)
 
     per = CHUNK // 16
@@ -718,7 +741,7 @@
         back_call,
         grid=(chunks,),
         in_specs=[
-            anywhere, anywhere, smem, back(INNER), back(INNER), back(INNER), back(INNER), back(INNER), back(2 * STATE),
+            anywhere, smem, back(INNER), back(INNER), back(INNER), back(INNER), back(INNER), back(2 * STATE),
             back(2 * STATE), back(LANES), back(LANES), back(LANES), back_three(STATE),
             pl.BlockSpec((1, 8, LANES), lambda c: (chunks - 1 - c, 0, 0)),
             full((STATE, INNER)), gathered_spec, logs_spec, back_three(STATE), back(SIDE),
@@ -739,19 +762,19 @@
         scratch_shapes=[
             pltpu.VMEM((STATE, INNER), f32), pltpu.VMEM((CHUNK + 8, XBC), f32),
             pltpu.VMEM((CHUNK + 8, XBC), f32), pltpu.VMEM((CHUNK, INNER), bf16),
-            pltpu.VMEM((CHUNK, 2 * INNER), bf16), pltpu.VMEM((CHUNK, 2 * INNER), bf16),
+            pltpu.VMEM((2 * CHUNK + 16, 2 * INNER), bf16),
         ],
         compiler_params=params(),
         cost_estimate=cost(47 * 10**9, 48 * 2**20),
         name="mixer_back",
     )(
-        *gives, rank, dxs, dy, x, u, y, bc, dbc, dcc, cum, dt, hst, pfx, h0, grads, states, ust, proj, proj,
+        give_b, rank, dxs, dy, x, u, y, bc, dbc, dcc, cum, dt, hst, pfx, h0, grads, states, ust, proj, proj,
         halo, convp, headp, spread, collect, rows,
     )
 
-    second_got, pg, first, tail, wg, hgr, skip = lax.optimization_barrier(
-        (second_got, pg, first, tail, wg, hgr, skip)
-    )
+    got_b, pg, first, tail, wg, hgr, skip = barrier((got_b, pg, first, tail, wg, hgr, skip))
+    keep_b, give_b = split_pair(add_low(keep_b, got_b), cross, x_axis, x_bit)
+    got_b = swap(give_b, x_axis, x_bit)
     after = lax.ppermute(first, "seq", backward)
     fixes = [jnp.zeros((5, XBC), f32)]
     for m in range(CONV - 1):
@@ -762,41 +785,26 @@
     tail_low = (tail + jnp.concatenate(fixes, axis=0)).astype(bf16)
     pg = lax.dynamic_update_slice(pg, tail_low, (count - 8, 0))
 
-    out_scattered, gate_scattered = [
-        lax.psum_scatter(flat(add_low(keep, got)), "dp", scatter_dimension=0, tiled=True)
-        for keep, got in zip(keeps, second_got)
-    ]
-
-    cross = len(bits) - 3
-    half = SIDE // 256 * 128
     left = blocks(product(normed_low, pg[:, :half]), bits)
     right = blocks(product(normed_low, pg[:, half:]), bits)
-    barrier = lax.optimization_barrier
     keep_l, give_l = split_pair(left, cross + 2, core_axis, core_bit)
     keep_r, give_r = split_pair(right, cross + 2, core_axis, core_bit)
     got_l, got_r = swap(give_l, core_axis, core_bit), swap(give_r, core_axis, core_bit)
     pg, dgate, _, _ = barrier((pg, dgate, give_l, give_r))
     normed_grad = lax.dot_general(dgate, full_gate, NT, preferred_element_type=f32)
     normed_grad = normed_grad + lax.dot_general(pg, full_side, NT, preferred_element_type=f32)
-    got_l, got_r, normed_grad = barrier((got_l, got_r, normed_grad))
-    x_axis, x_bit = bits[cross]
+    got_l, got_r, got_b, normed_grad = barrier((got_l, got_r, got_b, normed_grad))
     keep_l, give_l = split_pair(add_low(keep_l, got_l), cross + 1, y_axis, y_bit)
     keep_r, give_r = split_pair(add_low(keep_r, got_r), cross, x_axis, x_bit)
     got_l, got_r = swap(give_l, y_axis, y_bit), swap(give_r, x_axis, x_bit)
+    beside = scatter_pairs(add_low(keep_b, got_b), bits[early:cross], early)
     normed_grad, _, _ = barrier((normed_grad, give_l, give_r))
     _, norm_pull = jax.vjp(pre_norm, tok_vals, pre_gain)
     tok_norm_grad, pre_gain_grad = norm_pull(normed_grad)
     token_grad = (cot_low.astype(f32) + tok_norm_grad)[None]
-    got_l, got_r, token_grad, pre_gain_grad = barrier((got_l, got_r, token_grad, pre_gain_grad))
-    left = scatter_step(add_low(keep_l, got_l), cross, x_axis, x_bit)
-    right = scatter_step(add_low(keep_r, got_r), cross, y_axis, y_bit)
-    side_scattered = jnp.concatenate([left, right], axis=-1)
-    side_scattered, out_scattered, gate_scattered = barrier(
-        (side_scattered, out_scattered, gate_scattered)
-    )
-    for place in reversed(range(cross)):
-        side_scattered = scatter_step(side_scattered, place, *bits[place])
-
+    got_l, got_r, beside, token_grad, pre_gain_grad = barrier(
+        (got_l, got_r, beside, token_grad, pre_gain_grad)
+    )
     wg_sum = jnp.sum(wg.reshape(5, 8, XBC), axis=1)
     chan_grad = jnp.concatenate(
         [
@@ -809,14 +817,43 @@
             jnp.sum(skip.reshape(8, HEADS, HEADDIM), axis=(0, 2)),
         ]
     )
-    chan_grad = sum_pairs(chan_grad, bits)
-
-    def owned(part):
-        return flat(gather_pairs(part, seq_bits)).astype(f32)
-
-    out_grad = owned(out_scattered)
+
+    def together(side_got, beside, chan):
+        return barrier((side_got, beside, chan))
+
+    keep_l, give_l = split_pair(add_low(keep_l, got_l), cross, x_axis, x_bit)
+    keep_r, give_r = split_pair(add_low(keep_r, got_r), cross, y_axis, y_bit)
+    got_l, got_r = swap(give_l, x_axis, x_bit), swap(give_r, y_axis, y_bit)
+    beside = scatter_pairs(beside, bits[:early])
+    chan_grad = sum_pairs(chan_grad, bits[cross + 2 :])
+    (got_l, got_r), beside, chan_grad = together((got_l, got_r), beside, chan_grad)
+    side = jnp.concatenate([add_low(keep_l, got_l), add_low(keep_r, got_r)], axis=-1)
+    sums = [bits[:early], bits[early:cross], bits[cross : cross + 1], bits[cross + 1 : cross + 2]]
+    side = scatter_pairs(side, bits[early:cross], early)
+    beside = gather_step(beside, 0, y_axis, y_bit)
+    chan_grad = sum_pairs(chan_grad, sums[0])
+    side, beside, chan_grad = together(side, beside, chan_grad)
+    side = scatter_pairs(side, bits[:early])
+    beside = gather_step(beside, 1, core_axis, core_bit)
+    chan_grad = sum_pairs(chan_grad, sums[1])
+    side, beside, chan_grad = together(side, beside, chan_grad)
+    got = swap(side, y_axis, y_bit)
+    chan_grad = sum_pairs(chan_grad, sums[2])
+    got, chan_grad = barrier((got, chan_grad))
+    side = merge_pair(side, got, 0, y_axis, y_bit)
+    got = swap(side, core_axis, core_bit)
+    chan_grad = sum_pairs(chan_grad, sums[3])
+    side = flat(merge_pair(side, got, 1, core_axis, core_bit))
+
+    beside = beside.astype(f32)
+    out_grad = flat(beside[..., :out_rows, :])
     in_grad = jnp.concatenate(
-        [owned(gate_scattered), owned(side_scattered)[:, : PROJ - INNER]], axis=1
+        [
+            flat(beside[..., out_rows : out_rows + in_rows, :]),
+            flat(beside[..., out_rows + in_rows :, :]),
+            side[:, : PROJ - INNER].astype(f32),
+        ],
+        axis=1,
     )
     in_new, in_mom, in_sec = adamw_step(
         in_weight, in_moment, in_second, in_grad, rate_matrix, decay_matrix

time: 452 us -> 321 us (0.71); the launches traced: 444 us -> 318 us
  blocking collectives: 67.2 us -> 0 us
  waiting for transfers between devices: 119 us -> 56.7 us
  Pallas kernels: 108 us -> 123 us
  starting transfers between devices: 42.6 us -> 35.8 us
    reduce_scatter x2 -> x0, waiting for transfers between devices: 74.6 us -> none  [local(): lax.psum_scatter(flat(add_low(keep, got)), 'dp', scatter_dimension=0, til...]
    all_gather x2 -> x0, blocking collectives: 67.2 us -> none  [local(): lax.all_gather(part, 'dp', axis=0, tiled=False)]
    ppermute x35, waiting for transfers between devices: 39.9 us -> 56.6 us  [swap(): return lax.ppermute(v, axis, [(i, i ^ 1 << bit) for i in range(size)])]
    pallas_call x1, Pallas kernels: 10.6 us -> 22.9 us  [local(): pl.pallas_call(within_back_call, grid=(chunks,), in_specs=[by_chunk(INNER...]
    ppermute x35, starting transfers between devices: 38.2 us -> 31.8 us  [swap(): return lax.ppermute(v, axis, [(i, i ^ 1 << bit) for i in range(size)])]
    another operation x35 -> x34, other arithmetic: 15 us -> 10.9 us  [merge_pair(): jnp.stack([jnp.where(second, other, v), jnp.where(second, v, other)], axi...]
    dot_general x4 -> x5, matrix products: 13.1 us -> 13.3 us  [product(): lax.dot_general(left, right, TN, preferred_element_type=f32).astype(bf16)]
  transfers between devices with their start and end apart: 41 -> 39, of which waited for: 19 -> 18; matrix products, arithmetic and copies ran while one was open for 14% -> 18% of each run, Pallas kernels for 18% -> 31%
where the time goes in v4:
time: 321 us; the launch traced here: 318 us
  Pallas kernels  123 us (38%)
  waiting for transfers between devices  56.7 us (18%)
  other arithmetic  38.1 us (12%)
  starting transfers between devices  35.8 us (11%)
  matrix products  30 us (9%)
  local copies, waits for them, and re-layouts  19.2 us (6%)
  between operations  15.5 us (5%)
    ppermute x35, waiting for transfers between devices, swap(): return lax.ppermute(v, axis, [(i, i ^ 1 << bit) for i in range(size)])  56.6 us
    pallas_call x1, Pallas kernels, local(): pl.pallas_call(back_call, grid=(chunks,), in_specs=[anywhere, smem, back(...  42.1 us
    ppermute x35, starting transfers between devices, swap(): return lax.ppermute(v, axis, [(i, i ^ 1 << bit) for i in range(size)])  31.8 us
    pallas_call x1, Pallas kernels, local(): pl.pallas_call(gate_call, grid=(chunks,), in_specs=[smem, by_chunk(INNER)...  25.8 us
    pallas_call x1, Pallas kernels, local(): pl.pallas_call(within_back_call, grid=(chunks,), in_specs=[by_chunk(INNER...  22.9 us
    pallas_call x1, Pallas kernels, local(): pl.pallas_call(conv_state_kernel, grid=(chunks,), in_specs=[by_chunk(SIDE...  22.2 us
    dot_general x5, matrix products, product(): lax.dot_general(left, right, TN, preferred_element_type=f32).astype(bf16)  13.3 us
    another operation x34, other arithmetic, merge_pair(): jnp.stack([jnp.where(second, other, v), jnp.where(second, v, other)], axi...  10.9 us
  transfers between devices with their start and end apart: 39, of which 18 were waited for; matrix products, arithmetic and copies ran while one was open for 18% of the time, Pallas kernels for 31%

profile of v4, /device:TPU:0, one launch (start us, length us, event | category | flops | bytes accessed | tf_op | source)
XLA Modules:
  0.0 318.2 jit_solution(16077170427401647635)
XLA Ops:
  8.0 2.3 collective-permute-start.10
  11.4 3.5 %collective-permute-start = (bf16[24,1920]{1,0:T(8,128)(2,1)S(1)}, bf16[24,1920]{1,0:T(8,128)(2,1)S(1)}, u32[]{:S(2)}, u32[]{:S(2)}) collective-permute-start(bf16[24,1920]{1,0:T(8,128)(2,1)S(1)} %pad.11), channel_id=1, source_target_pairs={{0,16},{4,20},{8,24},{12,28},{16,0},{20,4},{24,8},{28,12},{1,17},{... | collective-permute-start | bytes 276488 | tf_op jit(solution)/shard_map/ppermute | solution.py:377
  14.9 1.8 fusion.7
  21.6 1.6 collective-permute-start.1
  23.2 5.4 %collective-permute-done.1 = bf16[2,24,1920]{2,1,0:T(8,128)(2,1)S(1)} collective-permute-done((bf16[2,24,1920]{2,1,0:T(8,128)(2,1)S(1)}, bf16[2,24,1920]{2,1,0:T(8,128)(2,1)S(1)}, u32[]{:S(2)}, u32[]{:S(2)}) %collective-permute-start.1) | collective-permute-done | bytes 184352 | tf_op jit(solution)/shard_map/ppermute | solution.py:377
  28.8 1.4 collective-permute-start.4
  30.4 1.6 collective-permute-start.2
  32.0 7.0 %collective-permute-done.4 = bf16[96,768]{1,0:T(8,128)(2,1)S(1)} collective-permute-done((bf16[96,768]{1,0:T(8,128)(2,1)S(1)}, bf16[96,768]{1,0:T(8,128)(2,1)S(1)}, u32[]{:S(2)}, u32[]{:S(2)}) %collective-permute-start.4) | collective-permute-done | bytes 147488 | tf_op jit(solution)/shard_map/ppermute | solution.py:377
  39.4 1.4 collective-permute-start.6
  40.9 6.6 %collective-permute-done.7 = bf16[2,96,768]{2,1,0:T(8,128)(2,1)S(1)} collective-permute-done((bf16[2,96,768]{2,1,0:T(8,128)(2,1)S(1)}, bf16[2,96,768]{2,1,0:T(8,128)(2,1)S(1)}, u32[]{:S(2)}, u32[]{:S(2)}) %collective-permute-start.7) | collective-permute-done | bytes 294944 | tf_op jit(solution)/shard_map/ppermute | solution.py:377
  47.6 2.5 collective-permute-done.5
  52.7 1.2 collective-permute-start.11
  53.9 1.3 select_bitcast_fusion.7
  55.3 1.7 select_bitcast_fusion.5
  57.4 1.1 fusion.14.halo.refs_19_
  59.4 5.1 %convolution_convert_fusion.1.proj.refs_17_.refs_18_ = bf16[1024,1920]{1,0:T(8,128)(2,1)} fusion(bf16[768,1024]{1,0:T(8,128)(2,1)S(1)} %bitcast.217, bf16[768,896]{1,0:T(8,128)(2,1)S(1)} %bitcast.223, f32[768]{0:T(1024)S(1)} %slice.122, f32[1024]{0:T(1024)S(1)} %fusion.70, bf16[1,1024,768]{2,1,0:T(8,128)(2,1)S(1)} %copy-done), kind=kOutput, calls=%fused_computation.9 | convolution fusion | flops 3030908928 | bytes 8461312 | tf_op jit(solution)/shard_map/dot_general | solution.py:43
  64.5 3.4 %collective-permute-done.11 = bf16[2,2,96,768]{3,2,1,0:T(8,128)(2,1)S(1)} collective-permute-done((bf16[2,2,96,768]{3,2,1,0:T(8,128)(2,1)S(1)}, bf16[2,2,96,768]{3,2,1,0:T(8,128)(2,1)S(1)}, u32[]{:S(2)}, u32[]{:S(2)}) %collective-permute-start.11) | collective-permute-done | bytes 589856 | tf_op jit(solution)/shard_map/ppermute | solution.py:377
  68.5 22.2 %conv_state.1 = (bf16[1024,1536]{1,0:T(8,128)(2,1)}, bf16[1024,256]{1,0:T(8,128)(2,1)}, bf16[1024,1536]{1,0:T(8,128)(2,1)}, f32[1024,128]{1,0:T(8,128)}, f32[32,...) custom-call(bf16[1024,1920]{1,0:T(8,128)(2,1)} %convolution_convert_, ...), custom_call_target="tpu_custom_call" | custom-call | flops 24000000000 | bytes 25165824 | tf_op jit(solution)/shard_map/conv_state/pallas_call | solution.py:591
  90.7 4.6 %collective-permute-done.12 = bf16[2,2,2,96,768]{4,3,2,1,0:T(8,128)(2,1)S(1)} collective-permute-done((bf16[2,2,2,96,768]{4,3,2,1,0:T(8,128)(2,1)S(1)}, bf16[2,2,2,96,768]{4,3,2,1,0:T(8,128)(2,1)S(1)}, u32[]{:S(2)}, u32[]{:S(2)}) %collective-permute-start.12) | collective-permute-done | bytes 1179680 | tf_op jit(solution)/shard_map/ppermute | solution.py:377
  95.5 1.8 pad_maximum_fusion.3
  98.4 9.9 %within.1.refs_1_ = f32[1024,1536]{1,0:T(8,128)} custom-call(bf16[1024,1536]{1,0:T(8,128)(2,1)} %get-tuple-element.113.u.refs_4_, bf16[1024,256]{1,0:T(8,128)(2,1)} %get-tuple-element.114.bc.refs_3_.refs_6_, f32[1024,128]{1,0:T(8,128)} %get-tuple-element.115.cum.refs_4_.refs_9_, f32[32,1024]{1,0:T(8,128)} %get-tuple-element.116.cumt), custom_call_target="tpu_custom_call" | custom-call | flops 11000000512 | bytes 16777216 | tf_op jit(solution)/shard_map/within/pallas_call | solution.py:627
  108.4 2.0 select_bitcast_fusion.1
  110.4 1.5 pad_maximum_fusion.2
  113.6 4.4 %convolution_convert_fusion.refs_8_ = bf16[1024,1536]{1,0:T(8,128)(2,1)} fusion(bf16[768,768]{1,0:T(8,128)(2,1)S(1)} %bitcast.233, bf16[768,768]{1,0:T(8,128)(2,1)S(1)} %bitcast.231, f32[768]{0:T(1024)S(1)} %slice.122, f32[1024]{0:T(1024)S(1)} %fusion.70, bf16[1,1024,768]{2,1,0:T(8,128)(2,1)S(1)} %copy-done), kind=kOutput, calls=%fused_computation.8 | convolution fusion | flops 2425356288 | bytes 7085056 | tf_op jit(solution)/shard_map/dot_general | solution.py:43
  118.0 25.8 %gate_norm.1 = (f32[1024,768]{1,0:T(8,128)}, bf16[1024,1536]{1,0:T(8,128)(2,1)}, f32[1024,1536]{1,0:T(8,128)}, bf16[1024,1536]{1,0:T(8,128)(2,1)}, bf16[1024,153...) custom-call(s32[1]{0:T(128)} %bitcast.refs_0_, ...), custom_call_target="tpu_custom_call" | custom-call | flops 30000001024 | bytes 50331648 | tf_op jit(solution)/shard_map/gate_norm/pallas_call | solution.py:659
  143.9 3.2 %fusion.36 = bf16[768,768]{1,0:T(8,128)(2,1)S(1)} fusion(bf16[1024,1536]{1,0:T(8,128)(2,1)} %get-tuple-element.149, f32[768]{0:T(1024)S(1)} %slice.122, f32[1024]{0:T(1024)S(1)} %fusion.70, bf16[1,1024,768]{2,1,0:T(8,128)(2,1)S(1)} %copy-done.1), kind=kOutput, calls=%fused_computation.53 | convolution fusion | flops 1211695104 | bytes 4332544 | tf_op jit(solution)/shard_map/dot_general | solution.py:695
  147.1 1.6 fusion.33
  149.4 2.9 convolution_convert_fusion.2
  153.0 1.7 constant_dynamic-slice_fusion.1
  154.7 1.6 copy.89
  159.0 1.0 add_convert_fusion.1.refs_23_
  160.0 22.9 %within_back.1 = (f32[1024,1536]{1,0:T(8,128)}, f32[1024,256]{1,0:T(8,128)}) custom-call(bf16[1024,1536]{1,0:T(8,128)(2,1)} %get-tuple-element.113.u.refs_4_, bf16[1024,1536]{1,0:T(8,128)(2,1)} %get-tuple-element.126.dy.refs_2_, bf16[1024,256]{1,0:T(8,128)(2,1)} %get-tuple-element.114.bc.refs_3_.refs_6_, f32[1024,128]{1,0:T(8,128)} %get-tuple-element.115.cum.refs_4_.refs_9_, ...), custom_call_target="tpu_custom_call" | custom-call | flops 12000000000 | bytes 16777216 | tf_op jit(solution)/shard_map/within_back/pallas_call | solution.py:712
  182.9 2.4 fusion
  185.3 1.4 copy-done.6
  187.8 42.1 %mixer_back.1 = (bf16[1024,1920]{1,0:T(8,128)(2,1)}, f32[8,1792]{1,0:T(8,128)}, f32[8,1792]{1,0:T(8,128)}, f32[40,1792]{1,0:T(8,128)}, f32[16,128]{1,0:T(8,128)}, /*index=5*/f32[8,1536]{1,0:T(8,128)}) custom-call(bf16[2,2,2,96,768]{4,3,2,1,0:T(8,128)(2,1)} %copy-done.20, s32[1]{0:T(128)} %bitcast.refs_0_, f32[1024,1536]{1,0:T(8,128)} %get-tuple-element.130.refs_1_, ...), custom_call_target="tpu_custom_call" | custom-call | flops 46999998464 | bytes 50331648 | tf_op jit(solution)/shard_map/mixer_back/pallas_call | solution.py:740
  232.5 1.3 collective-permute-start.16
  233.8 1.9 fusion.13
  235.8 1.3 collective-permute-start.19
  237.1 1.3 copy.76
  238.4 1.7 reshape.191
  240.2 1.3 fusion.61
  241.5 3.6 %fusion.25 = bf16[768,896]{1,0:T(8,128)(2,1)S(1)} fusion(bf16[1024,1920]{1,0:T(8,128)(2,1)} %fusion.61, f32[768]{0:T(1024)S(1)} %slice.122, f32[1024]{0:T(1024)S(1)} %fusion.70, bf16[1,1024,768]{2,1,0:T(8,128)(2,1)S(1)} %copy-done.1), kind=kOutput, calls=%fused_computation.42 | convolution fusion | flops 1413120000 | bytes 4791296 | tf_op jit(solution)/shard_map/dot_general | solution.py:695
  245.1 2.0 fusion.22
  248.8 3.5 %fusion.19 = f32[1024,768]{1,0:T(8,128)S(1)} fusion(bf16[1024,1920]{1,0:T(8,128)(2,1)S(1)} %copy-done.37, bf16[768,1024]{1,0:T(8,128)(2,1)S(1)} %bitcast.218, bf16[768,896]{1,0:T(8,128)(2,1)S(1)} %bitcast.224), kind=kOutput, calls=%fused_computation.37 | convolution fusion | flops 3025797120 | bytes 10027008 | tf_op jit(solution)/shard_map/dot_general | solution.py:795
  252.3 2.6 convolution_add_fusion
  255.5 1.2 fusion.41
  256.8 1.8 collective-permute-start.22
  258.6 2.3 collective-permute-start.20
  261.9 1.2 fusion.4
  263.1 2.6 fusion.6
  266.7 2.5 collective-permute-done.20
  269.2 2.0 collective-permute-done.21
  271.7 1.1 collective-permute-start.25
  274.5 7.3 %collective-permute-done.25 = bf16[96,768]{1,0:T(8,128)(2,1)S(1)} collective-permute-done((bf16[96,768]{1,0:T(8,128)(2,1)S(1)}, bf16[96,768]{1,0:T(8,128)(2,1)S(1)}, u32[]{:S(2)}, u32[]{:S(2)}) %collective-permute-start.25) | collective-permute-done | bytes 147488 | tf_op jit(solution)/shard_map/ppermute | solution.py:377
  283.6 2.0 collective-permute-start.27
  285.6 1.7 collective-permute-done.29
  288.1 2.6 collective-permute-done.27
  290.7 1.5 collective-permute-start.30
  293.1 3.3 %collective-permute-done.32 = f32[11336]{0:T(1024)S(1)} collective-permute-done((f32[11336]{0:T(1024)S(1)}, f32[11336]{0:T(1024)S(1)}, u32[]{:S(2)}, u32[]{:S(2)}) %collective-permute-start.32) | collective-permute-done | bytes 45376 | tf_op jit(solution)/shard_map/ppermute | solution.py:377
  299.5 1.5 multiply_subtract_fusion.1
  301.6 1.9 collective-permute-done.33
  303.5 1.1 collective-permute-start.36
  304.6 3.0 collective-permute-done.36
  308.5 2.6 multiply_subtract_fusion
  (247 shorter events, 37.2 us)
Async XLA Ops:
  7.2 10.2 %copy-start.27 = (f32[11336]{0:T(1024)S(1)}, f32[11336]{0:T(1024)}, u32[]{:S(2)}) copy-start(f32[11336]{0:T(1024)} %param.19) | copy-start | bytes 136036
  7.2 110.8 %all-gather.5.cloned.1.call-start = ((), (), s32[]{:S(2)}) async-start(), calls=%async_computation | async-start | bytes 2211840 | tf_op jit(solution)/shard_map/all_gather | solution.py:620
  8.0 44.5 %collective-permute-start.10 = (bf16[16,768]{1,0:T(8,128)(2,1)S(1)}, bf16[16,768]{1,0:T(8,128)(2,1)S(1)}, u32[]{:S(2)}, u32[]{:S(2)}) collective-permute-start(bf16[16,768]{1,0:T(8,128)(2,1)S(1)} %slice_bitcast_fusion.1), channel_id=1, source_target_pairs={{0,1},{1,2},{2,3},{4,5},{5,6},{6,7},{8,9},{9,10},{10,11},{12,13},{... | collective-permute-start | bytes 73736 | tf_op jit(solution)/shard_map/ppermute | solution.py:566
  11.4 10.1 %collective-permute-start = (bf16[24,1920]{1,0:T(8,128)(2,1)S(1)}, bf16[24,1920]{1,0:T(8,128)(2,1)S(1)}, u32[]{:S(2)}, u32[]{:S(2)}) collective-permute-start(bf16[24,1920]{1,0:T(8,128)(2,1)S(1)} %pad.11), channel_id=1, source_target_pairs={{0,16},{4,20},{8,24},{12,28},{16,0},{20,4},{24,8},{28,12},{1,17},{... | collective-permute-start | bytes 276488 | tf_op jit(solution)/shard_map/ppermute | solution.py:377
  16.6 12.1 %copy-start.33 = (f32[1024]{0:T(1024)}, f32[1024]{0:T(1024)S(1)}, u32[]{:S(2)}) copy-start(f32[1024]{0:T(1024)S(1)} %fusion.7) | copy-start | bytes 12292
  19.7 19.3 %copy-start.25 = (f32[1792,4]{0,1:T(4,128)}, f32[1792,4]{0,1:T(4,128)S(1)}, u32[]{:S(2)}) copy-start(f32[1792,4]{0,1:T(4,128)S(1)} %copy.68) | copy-start | bytes 86020
  21.6 7.1 %collective-permute-start.1 = (bf16[2,24,1920]{2,1,0:T(8,128)(2,1)S(1)}, bf16[2,24,1920]{2,1,0:T(8,128)(2,1)S(1)}, u32[]{:S(2)}, u32[]{:S(2)}) collective-permute-start(bf16[2,24,1920]{2,1,0:T(8,128)(2,1)S(1)} %pad_maximum_fusion.25), channel_id=1, source_target_pairs={{0,8},{4,12},{8,0},{12,4},{16,24},{20,28},{24,16},{28,20},{1,9},{5... | collective-permute-start | bytes 552968 | tf_op jit(solution)/shard_map/ppermute | solution.py:377
  28.8 10.2 %collective-permute-start.4 = (bf16[96,768]{1,0:T(8,128)(2,1)S(1)}, bf16[96,768]{1,0:T(8,128)(2,1)S(1)}, u32[]{:S(2)}, u32[]{:S(2)}) collective-permute-start(bf16[96,768]{1,0:T(8,128)(2,1)S(1)} %pad_maximum_fusion.27), channel_id=1, source_target_pairs={{0,16},{4,20},{8,24},{12,28},{16,0},{20,4},{24,8},{28,12},{1,17},{... | collective-permute-start | bytes 442376 | tf_op jit(solution)/shard_map/ppermute | solution.py:377
  30.4 8.6 %collective-permute-start.2 = (bf16[2,2,24,896]{3,2,1,0:T(8,128)(2,1)S(1)}, bf16[2,2,24,896]{3,2,1,0:T(8,128)(2,1)S(1)}, u32[]{:S(2)}, u32[]{:S(2)}) collective-permute-start(bf16[2,2,24,896]{3,2,1,0:T(8,128)(2,1)S(1)} %slice.126), channel_id=1, source_target_pairs={{0,4},{4,0},{8,12},{12,8},{16,20},{20,16},{24,28},{28,24},{1,5},{5... | collective-permute-start | bytes 516104 | tf_op jit(solution)/shard_map/ppermute | solution.py:377
  32.0 7.1 %collective-permute-start.3 = (bf16[2,2,24,1024]{3,2,1,0:T(8,128)(2,1)S(1)}, bf16[2,2,24,1024]{3,2,1,0:T(8,128)(2,1)S(1)}, u32[]{:S(2)}, u32[]{:S(2)}) collective-permute-start(bf16[2,2,24,1024]{3,2,1,0:T(8,128)(2,1)S(1)} %slice.127), channel_id=1, source_target_pairs={{0,2},{1,3},{2,0},{3,1},{4,6},{5,7},{6,4},{7,5},{8,10},{9,11},{10,... | collective-permute-start | bytes 589832 | tf_op jit(solution)/shard_map/ppermute | solution.py:377
  39.1 8.5 %collective-permute-start.7 = (bf16[2,96,768]{2,1,0:T(8,128)(2,1)S(1)}, bf16[2,96,768]{2,1,0:T(8,128)(2,1)S(1)}, u32[]{:S(2)}, u32[]{:S(2)}) collective-permute-start(bf16[2,96,768]{2,1,0:T(8,128)(2,1)S(1)} %pad_maximum_fusion.23), channel_id=1, source_target_pairs={{0,8},{4,12},{8,0},{12,4},{16,24},{20,28},{24,16},{28,20},{1,9},{5... | collective-permute-start | bytes 884744 | tf_op jit(solution)/shard_map/ppermute | solution.py:377
  39.4 10.8 %collective-permute-start.6 = (bf16[2,2,2,24,1024]{4,3,1,0,2:T(8,128)(2,1)S(1)}, bf16[2,2,2,24,1024]{4,3,1,0,2:T(8,128)(2,1)S(1)}, u32[]{:S(2)}, u32[]{:S(2)}) collective-permute-start(bf16[2,2,2,24,1024]{4,3,1,0,2:T(8,128)(2,1)S(1)} %pad_maximum_fusion.19), channel_id=1, source_target_pairs={{0,4},{4,0},{8,12},{12,8},{16,20},{20,16},{24,28},{28,24},{1,5},{5... | collective-permute-start | bytes 1179656 | tf_op jit(solution)/shard_map/ppermute | solution.py:377
  40.9 9.3 %collective-permute-start.5 = (bf16[2,2,2,24,896]{4,3,2,1,0:T(8,128)(2,1)S(1)}, bf16[2,2,2,24,896]{4,3,2,1,0:T(8,128)(2,1)S(1)}, u32[]{:S(2)}, u32[]{:S(2)}) collective-permute-start(bf16[2,2,2,24,896]{4,3,2,1,0:T(8,128)(2,1)S(1)} %pad_maximum_fusion.22), channel_id=1, source_target_pairs={{0,2},{1,3},{2,0},{3,1},{4,6},{5,7},{6,4},{7,5},{8,10},{9,11},{10,... | collective-permute-start | bytes 1032200 | tf_op jit(solution)/shard_map/ppermute | solution.py:377
  51.2 2.7 collective-permute-start.8
  51.3 4.1 %collective-permute-start.9 = (bf16[2,2,2,2,24,1024]{5,4,1,0,3,2:T(8,128)(2,1)S(1)}, bf16[2,2,2,2,24,1024]{5,4,1,0,3,2:T(8,128)(2,1)}, u32[]{:S(2)}, u32[]{:S(2)}) collective-permute-start(bf16[2,2,2,2,24,1024]{5,4,1,0,3,2:T(8,128)(2,1)S(1)} %pad_maximum_fusion.15), channel_id=1, source_target_pairs={{0,1},{1,0},{2,3},{3,2},{4,5},{5,4},{6,7},{7,6},{8,9},{9,8},{10,11... | collective-permute-start | bytes 2359304 | tf_op jit(solution)/shard_map/ppermute | solution.py:377
  52.7 15.3 %collective-permute-start.11 = (bf16[2,2,96,768]{3,2,1,0:T(8,128)(2,1)S(1)}, bf16[2,2,96,768]{3,2,1,0:T(8,128)(2,1)S(1)}, u32[]{:S(2)}, u32[]{:S(2)}) collective-permute-start(bf16[2,2,96,768]{3,2,1,0:T(8,128)(2,1)S(1)} %pad_maximum_fusion.17), channel_id=1, source_target_pairs={{0,4},{4,0},{8,12},{12,8},{16,20},{20,16},{24,28},{28,24},{1,5},{5... | collective-permute-start | bytes 1769480 | tf_op jit(solution)/shard_map/ppermute | solution.py:377
  55.3 3.2 %copy-start.12 = (bf16[2,2,2,2,2,24,896]{6,5,4,3,2,1,0:T(8,128)(2,1)}, bf16[2,2,2,2,2,24,896]{6,5,4,3,2,1,0:T(8,128)(2,1)S(1)}, u32[]{:S(2)}) copy-start(bf16[2,2,2,2,2,24,896]{6,5,4,3,2,1,0:T(8,128)(2,1)S(1)} %pad_maximum_fusion.10) | copy-start | bytes 4128772
  57.4 7.1 %copy-start.10 = (bf16[2,2,2,2,2,24,1024]{6,5,4,3,2,1,0:T(8,128)(2,1)}, bf16[2,2,2,2,2,24,1024]{6,5,4,3,2,1,0:T(8,128)(2,1)S(1)}, u32[]{:S(2)}) copy-start(bf16[2,2,2,2,2,24,1024]{6,5,4,3,2,1,0:T(8,128)(2,1)S(1)} %copy.67) | copy-start | bytes 4718596
  68.2 27.1 %collective-permute-start.12 = (bf16[2,2,2,96,768]{4,3,2,1,0:T(8,128)(2,1)S(1)}, bf16[2,2,2,96,768]{4,3,2,1,0:T(8,128)(2,1)S(1)}, u32[]{:S(2)}, u32[]{:S(2)}) collective-permute-start(bf16[2,2,2,96,768]{4,3,2,1,0:T(8,128)(2,1)S(1)} %pad_maximum_fusion.14), channel_id=1, source_target_pairs={{0,2},{1,3},{2,0},{3,1},{4,6},{5,7},{6,4},{7,5},{8,10},{9,11},{10,... | collective-permute-start | bytes 3538952 | tf_op jit(solution)/shard_map/ppermute | solution.py:377
  97.2 11.1 %collective-permute-start.13 = (bf16[2,2,2,2,96,768]{5,4,3,2,1,0:T(8,128)(2,1)}, bf16[2,2,2,2,96,768]{5,4,3,2,1,0:T(8,128)(2,1)}, u32[]{:S(2)}, u32[]{:S(2)}) collective-permute-start(bf16[2,2,2,2,96,768]{5,4,3,2,1,0:T(8,128)(2,1)} %pad_maximum_fusion.3), channel_id=1, source_target_pairs={{0,1},{1,0},{2,3},{3,2},{4,5},{5,4},{6,7},{7,6},{8,9},{9,8},{10,11... | collective-permute-start | bytes 7077896 | tf_op jit(solution)/shard_map/ppermute | solution.py:377
  97.4 89.6 %all-gather.7.cloned.1.call-start = ((), (), s32[]{:S(2)}) async-start(), calls=%async_computation.1 | async-start | bytes 1966080 | tf_op jit(solution)/shard_map/all_gather | solution.py:692
  98.4 9.9 %copy-start.3 = (bf16[2,2,2,1,96,768]{5,4,3,2,1,0:T(8,128)(2,1)S(1)}, bf16[2,2,2,1,96,768]{5,4,3,2,1,0:T(8,128)(2,1)}, u32[]{:S(2)}) copy-start(bf16[2,2,2,1,96,768]{5,4,3,2,1,0:T(8,128)(2,1)} %copy-done.2) | copy-start | bytes 3538948
  118.0 25.8 %copy-start.1 = (bf16[1,1024,768]{2,1,0:T(8,128)(2,1)S(1)}, bf16[1,1024,768]{2,1,0:T(8,128)(2,1)}, u32[]{:S(2)}) copy-start(bf16[1,1024,768]{2,1,0:T(8,128)(2,1)} %param.11) | copy-start | bytes 4718596
  143.9 3.2 %copy-start.38 = (bf16[1024,1536]{1,0:T(8,128)(2,1)S(1)}, bf16[1024,1536]{1,0:T(8,128)(2,1)}, u32[]{:S(2)}) copy-start(bf16[1024,1536]{1,0:T(8,128)(2,1)} %get-tuple-element.149) | copy-start | bytes 9437188
  154.7 3.2 %copy-start.21 = (f32[128,1536]{1,0:T(8,128)S(1)}, f32[128,1536]{1,0:T(8,128)}, u32[]{:S(2)}) copy-start(f32[128,1536]{1,0:T(8,128)} %get-tuple-element.137) | copy-start | bytes 2359300
  156.9 3.1 copy-start.32
  156.9 26.0 %collective-permute-start.14 = (bf16[2,2,2,2,96,768]{5,4,2,1,0,3:T(8,128)(2,1)}, bf16[2,2,2,2,96,768]{5,4,2,1,0,3:T(8,128)(2,1)}, u32[]{:S(2)}, u32[]{:S(2)}) collective-permute-start(bf16[2,2,2,2,96,768]{5,4,2,1,0,3:T(8,128)(2,1)} %bitcast.210), channel_id=1, source_target_pairs={{0,1},{1,0},{2,3},{3,2},{4,5},{5,4},{6,7},{7,6},{8,9},{9,8},{10,11... | collective-permute-start | bytes 7077896 | tf_op jit(solution)/shard_map/ppermute | solution.py:377
  160.0 22.9 %copy-start.4 = (bf16[2,2,2,2,1,96,768]{6,5,4,3,2,1,0:T(8,128)(2,1)S(1)}, bf16[2,2,2,2,1,96,768]{6,5,4,3,2,1,0:T(8,128)(2,1)}, u32[]{:S(2)}) copy-start(bf16[2,2,2,2,1,96,768]{6,5,4,3,2,1,0:T(8,128)(2,1)} %get-tuple-element.190) | copy-start | bytes 7077892
  186.8 43.1 %collective-permute-start.15 = (bf16[2,2,2,96,768]{4,3,2,1,0:T(8,128)(2,1)S(1)}, bf16[2,2,2,96,768]{4,3,2,1,0:T(8,128)(2,1)}, u32[]{:S(2)}, u32[]{:S(2)}) collective-permute-start(bf16[2,2,2,96,768]{4,3,2,1,0:T(8,128)(2,1)S(1)} %dynamic-slice_bitcast_fusion.sent), channel_id=1, source_target_pairs={{0,2},{1,3},{2,0},{3,1},{4,6},{5,7},{6,4},{7,5},{8,10},{9,11},{10,... | collective-permute-start | bytes 3538952 | tf_op jit(solution)/shard_map/ppermute | solution.py:377
  232.5 7.5 %collective-permute-start.16 = (f32[8,1792]{1,0:T(8,128)}, f32[8,1792]{1,0:T(8,128)S(1)}, u32[]{:S(2)}, u32[]{:S(2)}) collective-permute-start(f32[8,1792]{1,0:T(8,128)} %get-tuple-element.147), channel_id=1, source_target_pairs={{1,0},{2,1},{3,2},{5,4},{6,5},{7,6},{9,8},{10,9},{11,10},{13,12},{... | collective-permute-start | bytes 172040 | tf_op jit(solution)/shard_map/ppermute | solution.py:778
  235.7 4.3 %copy-start.35 = (f32[16,128]{1,0:T(8,128)S(1)}, f32[16,128]{1,0:T(8,128)}, u32[]{:S(2)}) copy-start(f32[16,128]{1,0:T(8,128)} %get-tuple-element.163) | copy-start | bytes 24580
  235.8 4.3 %copy-start.26 = (f32[1792,4]{0,1:T(4,128)S(1)}, f32[1792,4]{0,1:T(4,128)}, u32[]{:S(2)}) copy-start(f32[1792,4]{0,1:T(4,128)} %copy-done.25) | copy-start | bytes 86020
  235.8 4.4 %copy-start.29 = (f32[8,1792]{1,0:T(8,128)S(1)}, f32[8,1792]{1,0:T(8,128)}, u32[]{:S(2)}) copy-start(f32[8,1792]{1,0:T(8,128)} %get-tuple-element.146) | copy-start | bytes 172036
  235.8 19.1 %collective-permute-start.19 = (bf16[2,2,96,768]{3,2,1,0:T(8,128)(2,1)S(1)}, bf16[2,2,96,768]{3,2,1,0:T(8,128)(2,1)}, u32[]{:S(2)}, u32[]{:S(2)}) collective-permute-start(bf16[2,2,96,768]{3,2,1,0:T(8,128)(2,1)S(1)} %dynamic-slice_bitcast_fusion.3), channel_id=1, source_target_pairs={{0,4},{4,0},{8,12},{12,8},{16,20},{20,16},{24,28},{28,24},{1,5},{5... | collective-permute-start | bytes 1769480 | tf_op jit(solution)/shard_map/ppermute | solution.py:377
  241.5 3.6 %copy-start.37 = (bf16[1024,1920]{1,0:T(8,128)(2,1)S(1)}, bf16[1024,1920]{1,0:T(8,128)(2,1)}, u32[]{:S(2)}) copy-start(bf16[1024,1920]{1,0:T(8,128)(2,1)} %fusion.61) | copy-start | bytes 11796484
  247.1 7.9 %collective-permute-start.17 = (bf16[2,2,2,2,24,896]{5,4,3,2,1,0:T(8,128)(2,1)S(1)}, bf16[2,2,2,2,24,896]{5,4,3,2,1,0:T(8,128)(2,1)S(1)}, u32[]{:S(2)}, u32[]{:S(2)}) collective-permute-start(bf16[2,2,2,2,24,896]{5,4,3,2,1,0:T(8,128)(2,1)S(1)} %dynamic-slice_bitcast_fusion.2), channel_id=1, source_target_pairs={{0,1},{1,0},{2,3},{3,2},{4,5},{5,4},{6,7},{7,6},{8,9},{9,8},{10,11... | collective-permute-start | bytes 2064392 | tf_op jit(solution)/shard_map/ppermute | solution.py:377
  248.1 4.2 %copy-start.17 = (bf16[2,2,2,2,2,24,768]{6,5,4,3,2,1,0:T(8,128)(2,1)S(1)}, bf16[2,2,2,2,2,24,768]{6,5,4,3,2,1,0:T(8,128)(2,1)}, u32[]{:S(2)}) copy-start(bf16[2,2,2,2,2,24,768]{6,5,4,3,2,1,0:T(8,128)(2,1)} %copy-done.16) | copy-start | bytes 3538948
  248.1 4.2 %copy-start.19 = (bf16[2,2,2,2,2,24,768]{6,5,4,3,2,1,0:T(8,128)(2,1)S(1)}, bf16[2,2,2,2,2,24,768]{6,5,4,3,2,1,0:T(8,128)(2,1)}, u32[]{:S(2)}) copy-start(bf16[2,2,2,2,2,24,768]{6,5,4,3,2,1,0:T(8,128)(2,1)} %copy-done.18) | copy-start | bytes 3538948
  248.1 4.2 %copy-start.39 = (bf16[1024,1536]{1,0:T(8,128)(2,1)S(1)}, bf16[1024,1536]{1,0:T(8,128)(2,1)}, u32[]{:S(2)}) copy-start(bf16[1024,1536]{1,0:T(8,128)(2,1)} %get-tuple-element.149) | copy-start | bytes 9437188
  248.1 6.9 %collective-permute-start.18 = (bf16[2,2,2,2,24,1024]{5,4,3,2,1,0:T(8,128)(2,1)S(1)}, bf16[2,2,2,2,24,1024]{5,4,3,2,1,0:T(8,128)(2,1)S(1)}, u32[]{:S(2)}, u32[]{:S(2)}) collective-permute-start(bf16[2,2,2,2,24,1024]{5,4,3,2,1,0:T(8,128)(2,1)S(1)} %dynamic-slice_bitcast_fusion.1), channel_id=1, source_target_pairs={{0,1},{1,0},{2,3},{3,2},{4,5},{5,4},{6,7},{7,6},{8,9},{9,8},{10,11... | collective-permute-start | bytes 2359304 | tf_op jit(solution)/shard_map/ppermute | solution.py:377
  256.8 9.8 %collective-permute-start.22 = (bf16[2,96,768]{2,1,0:T(8,128)(2,1)S(1)}, bf16[2,96,768]{2,1,0:T(8,128)(2,1)S(1)}, u32[]{:S(2)}, u32[]{:S(2)}) collective-permute-start(bf16[2,96,768]{2,1,0:T(8,128)(2,1)S(1)} %dynamic-slice_bitcast_fusion.6), channel_id=1, source_target_pairs={{0,8},{4,12},{8,0},{12,4},{16,24},{20,28},{24,16},{28,20},{1,9},{5... | collective-permute-start | bytes 884744 | tf_op jit(solution)/shard_map/ppermute | solution.py:377
  258.6 10.6 %collective-permute-start.20 = (bf16[2,2,2,24,896]{4,3,2,1,0:T(8,128)(2,1)S(1)}, bf16[2,2,2,24,896]{4,3,2,1,0:T(8,128)(2,1)S(1)}, u32[]{:S(2)}, u32[]{:S(2)}) collective-permute-start(bf16[2,2,2,24,896]{4,3,2,1,0:T(8,128)(2,1)S(1)} %dynamic-slice_bitcast_fusion.5), channel_id=1, source_target_pairs={{0,2},{1,3},{2,0},{3,1},{4,6},{5,7},{6,4},{7,5},{8,10},{9,11},{10,... | collective-permute-start | bytes 1032200 | tf_op jit(solution)/shard_map/ppermute | solution.py:377
  261.0 10.2 %collective-permute-start.21 = (bf16[2,2,2,24,1024]{4,3,2,1,0:T(8,128)(2,1)S(1)}, bf16[2,2,2,24,1024]{4,3,2,1,0:T(8,128)(2,1)S(1)}, u32[]{:S(2)}, u32[]{:S(2)}) collective-permute-start(bf16[2,2,2,24,1024]{4,3,2,1,0:T(8,128)(2,1)S(1)} %dynamic-slice_bitcast_fusion.4), channel_id=1, source_target_pairs={{0,4},{4,0},{8,12},{12,8},{16,20},{20,16},{24,28},{28,24},{1,5},{5... | collective-permute-start | bytes 1179656 | tf_op jit(solution)/shard_map/ppermute | solution.py:377
  265.6 5.9 %copy-start.36 = (f32[24]{0:T(128)S(1)}, f32[24]{0:T(128)}, u32[]{:S(2)}) copy-start(f32[24]{0:T(128)} %reduce_sum.110) | copy-start | bytes 292
  271.7 2.8 collective-permute-start.26
  271.7 10.1 %collective-permute-start.25 = (bf16[96,768]{1,0:T(8,128)(2,1)S(1)}, bf16[96,768]{1,0:T(8,128)(2,1)S(1)}, u32[]{:S(2)}, u32[]{:S(2)}) collective-permute-start(bf16[96,768]{1,0:T(8,128)(2,1)S(1)} %dynamic-slice_bitcast_fusion.9), channel_id=1, source_target_pairs={{0,16},{4,20},{8,24},{12,28},{16,0},{20,4},{24,8},{28,12},{1,17},{... | collective-permute-start | bytes 442376 | tf_op jit(solution)/shard_map/ppermute | solution.py:377
  272.9 9.0 %collective-permute-start.23 = (bf16[2,2,24,896]{3,2,1,0:T(8,128)(2,1)S(1)}, bf16[2,2,24,896]{3,2,1,0:T(8,128)(2,1)S(1)}, u32[]{:S(2)}, u32[]{:S(2)}) collective-permute-start(bf16[2,2,24,896]{3,2,1,0:T(8,128)(2,1)S(1)} %dynamic-slice_bitcast_fusion.8), channel_id=1, source_target_pairs={{0,4},{4,0},{8,12},{12,8},{16,20},{20,16},{24,28},{28,24},{1,5},{5... | collective-permute-start | bytes 516104 | tf_op jit(solution)/shard_map/ppermute | solution.py:377
  273.5 8.4 %collective-permute-start.24 = (bf16[2,2,24,1024]{3,2,1,0:T(8,128)(2,1)S(1)}, bf16[2,2,24,1024]{3,2,1,0:T(8,128)(2,1)S(1)}, u32[]{:S(2)}, u32[]{:S(2)}) collective-permute-start(bf16[2,2,24,1024]{3,2,1,0:T(8,128)(2,1)S(1)} %dynamic-slice_bitcast_fusion.7), channel_id=1, source_target_pairs={{0,2},{1,3},{2,0},{3,1},{4,6},{5,7},{6,4},{7,5},{8,10},{9,11},{10,... | collective-permute-start | bytes 589832 | tf_op jit(solution)/shard_map/ppermute | solution.py:377
  282.0 5.3 %collective-permute-start.29 = (f32[11336]{0:T(1024)S(1)}, f32[11336]{0:T(1024)S(1)}, u32[]{:S(2)}, u32[]{:S(2)}) collective-permute-start(f32[11336]{0:T(1024)S(1)} %add.250), channel_id=1, source_target_pairs={{0,16},{4,20},{8,24},{12,28},{16,0},{20,4},{24,8},{28,12},{1,17},{... | collective-permute-start | bytes 136040 | tf_op jit(solution)/shard_map/ppermute | solution.py:377
  282.7 5.3 %collective-permute-start.28 = (bf16[96,768]{1,0:T(8,128)(2,1)S(1)}, bf16[96,768]{1,0:T(8,128)(2,1)S(1)}, u32[]{:S(2)}, u32[]{:S(2)}) collective-permute-start(bf16[96,768]{1,0:T(8,128)(2,1)S(1)} %fusion.50), channel_id=1, source_target_pairs={{0,2},{1,3},{2,0},{3,1},{4,6},{5,7},{6,4},{7,5},{8,10},{9,11},{10,... | collective-permute-start | bytes 442376 | tf_op jit(solution)/shard_map/ppermute | solution.py:377
  283.6 7.0 %collective-permute-start.27 = (bf16[2,24,1920]{2,1,0:T(8,128)(2,1)S(1)}, bf16[2,24,1920]{2,1,0:T(8,128)(2,1)S(1)}, u32[]{:S(2)}, u32[]{:S(2)}) collective-permute-start(bf16[2,24,1920]{2,1,0:T(8,128)(2,1)S(1)} %fusion.52), channel_id=1, source_target_pairs={{0,8},{4,12},{8,0},{12,4},{16,24},{20,28},{24,16},{28,20},{1,9},{5... | collective-permute-start | bytes 552968 | tf_op jit(solution)/shard_map/ppermute | solution.py:377
  290.7 6.5 %collective-permute-start.30 = (bf16[24,1920]{1,0:T(8,128)(2,1)S(1)}, bf16[24,1920]{1,0:T(8,128)(2,1)S(1)}, u32[]{:S(2)}, u32[]{:S(2)}) collective-permute-start(bf16[24,1920]{1,0:T(8,128)(2,1)S(1)} %dynamic-slice_bitcast_fusion.10), channel_id=1, source_target_pairs={{0,16},{4,20},{8,24},{12,28},{16,0},{20,4},{24,8},{28,12},{1,17},{... | collective-permute-start | bytes 276488 | tf_op jit(solution)/shard_map/ppermute | solution.py:377
  292.3 4.1 %collective-permute-start.32 = (f32[11336]{0:T(1024)S(1)}, f32[11336]{0:T(1024)S(1)}, u32[]{:S(2)}, u32[]{:S(2)}) collective-permute-start(f32[11336]{0:T(1024)S(1)} %add.254), channel_id=1, source_target_pairs={{0,8},{4,12},{8,0},{12,4},{16,24},{20,28},{24,16},{28,20},{1,9},{5... | collective-permute-start | bytes 136040 | tf_op jit(solution)/shard_map/ppermute | solution.py:377
  293.1 4.2 %collective-permute-start.31 = (bf16[2,96,768]{2,1,0:T(8,128)(2,1)S(1)}, bf16[2,96,768]{2,1,0:T(8,128)(2,1)S(1)}, u32[]{:S(2)}, u32[]{:S(2)}) collective-permute-start(bf16[2,96,768]{2,1,0:T(8,128)(2,1)S(1)} %pad_maximum_fusion.24), channel_id=1, source_target_pairs={{0,1},{1,0},{2,3},{3,2},{4,5},{5,4},{6,7},{7,6},{8,9},{9,8},{10,11... | collective-permute-start | bytes 884744 | tf_op jit(solution)/shard_map/ppermute | solution.py:377
  297.4 4.2 %collective-permute-start.34 = (f32[11336]{0:T(1024)S(1)}, f32[11336]{0:T(1024)S(1)}, u32[]{:S(2)}, u32[]{:S(2)}) collective-permute-start(f32[11336]{0:T(1024)S(1)} %add.256), channel_id=1, source_target_pairs={{0,4},{4,0},{8,12},{12,8},{16,20},{20,16},{24,28},{28,24},{1,5},{5... | collective-permute-start | bytes 136040 | tf_op jit(solution)/shard_map/ppermute | solution.py:377
  298.4 5.1 %collective-permute-start.33 = (bf16[24,1920]{1,0:T(8,128)(2,1)S(1)}, bf16[24,1920]{1,0:T(8,128)(2,1)S(1)}, u32[]{:S(2)}, u32[]{:S(2)}) collective-permute-start(bf16[24,1920]{1,0:T(8,128)(2,1)S(1)} %fusion.55), channel_id=1, source_target_pairs={{0,2},{1,3},{2,0},{3,1},{4,6},{5,7},{6,4},{7,5},{8,10},{9,11},{10,... | collective-permute-start | bytes 276488 | tf_op jit(solution)/shard_map/ppermute | solution.py:377
  301.0 6.6 %copy-start.28 = (f32[11336]{0:T(1024)S(1)}, f32[11336]{0:T(1024)}, u32[]{:S(2)}) copy-start(f32[11336]{0:T(1024)} %param.19) | copy-start | bytes 136036
  301.0 6.6 %copy-start.30 = (f32[11336]{0:T(1024)S(1)}, f32[11336]{0:T(1024)}, u32[]{:S(2)}) copy-start(f32[11336]{0:T(1024)} %param.20) | copy-start | bytes 136036
  301.0 6.6 %copy-start.31 = (f32[11336]{0:T(1024)S(1)}, f32[11336]{0:T(1024)}, u32[]{:S(2)}) copy-start(f32[11336]{0:T(1024)} %param.21) | copy-start | bytes 136036
  301.1 7.4 %copy-start.7 = (f32[96,3352]{1,0:T(8,128)S(1)}, f32[96,3352]{1,0:T(8,128)}, u32[]{:S(2)}) copy-start(f32[96,3352]{1,0:T(8,128)} %param.13) | copy-start | bytes 3861508
  301.1 7.4 %copy-start.14 = (f32[96,3352]{1,0:T(8,128)S(1)}, f32[96,3352]{1,0:T(8,128)}, u32[]{:S(2)}) copy-start(f32[96,3352]{1,0:T(8,128)} %param.14) | copy-start | bytes 3861508
  301.1 7.4 %copy-start.15 = (f32[96,3352]{1,0:T(8,128)S(1)}, f32[96,3352]{1,0:T(8,128)}, u32[]{:S(2)}) copy-start(f32[96,3352]{1,0:T(8,128)} %param.15) | copy-start | bytes 3861508
  303.5 4.2 %collective-permute-start.36 = (f32[11336]{0:T(1024)S(1)}, f32[11336]{0:T(1024)S(1)}, u32[]{:S(2)}, u32[]{:S(2)}) collective-permute-start(f32[11336]{0:T(1024)S(1)} %add.257), channel_id=1, source_target_pairs={{0,2},{1,3},{2,0},{3,1},{4,6},{5,7},{6,4},{7,5},{8,10},{9,11},{10,... | collective-permute-start | bytes 136040 | tf_op jit(solution)/shard_map/ppermute | solution.py:377
  304.6 3.8 %collective-permute-start.35 = (bf16[2,24,1920]{2,1,0:T(8,128)(2,1)S(1)}, bf16[2,24,1920]{2,1,0:T(8,128)(2,1)S(1)}, u32[]{:S(2)}, u32[]{:S(2)}) collective-permute-start(bf16[2,24,1920]{2,1,0:T(8,128)(2,1)S(1)} %pad_maximum_fusion.26), channel_id=1, source_target_pairs={{0,1},{1,0},{2,3},{3,2},{4,5},{5,4},{6,7},{7,6},{8,9},{9,8},{10,11... | collective-permute-start | bytes 552968 | tf_op jit(solution)/shard_map/ppermute | solution.py:377
  (16 other events, 28.9 us)
Sparse Core Ops, SparseCore 0:
  97.6 19.2 all-gather.4
  158.8 18.2 all-gather.6
